TPU v7x, 512 devices: a whole 4x8x8 slice. The times are simulated.
512 devices in a mesh: lon: 16 (over x_hi, z), lat: 32 (over x_lo, y, core).
Axes of the slice: x: 4 (x_hi: 2, x_lo: 2; x = x_hi * 2 + x_lo), y: 8, z: 8, core: 2. Of those that a mesh axis runs over, the one named last changes fastest.
Arguments:
- temp: float32 [8, 1024, 4096], P(None, 'lat', 'lon'), may hold values from -6 to 6
- salt: float32 [8, 1024, 4096], P(None, 'lat', 'lon'), may hold values from -6 to 6
- u_courant: float32 [8, 1024, 4096], P(None, 'lat', 'lon'), may hold values from -0.4 to 0.4
- v_courant: float32 [8, 1024, 4096], P(None, 'lat', 'lon'), may hold values from -0.4 to 0.4
- diffusion: float32 [8, 1024, 4096], P(None, 'lat', 'lon'), may hold values from 0.02 to 0.12
- slope_x: float32 [8, 1024, 4096], P(None, 'lat', 'lon'), may hold values from -1 to 1
- slope_y: float32 [8, 1024, 4096], P(None, 'lat', 'lon'), may hold values from -1 to 1
- u_mask: int32 [8, 1024, 4096], P(None, 'lat', 'lon'), may hold values 0 or 1
- v_mask: int32 [8, 1024, 4096], P(None, 'lat', 'lon'), may hold values 0 or 1
Outputs:
- temp_next: float32 [8, 1024, 4096], P(None, 'lat', 'lon')
- salt_next: float32 [8, 1024, 4096], P(None, 'lat', 'lon')
All inputs are finite; a program needn't handle non-finite values. No bound on the sum of `u_mask` or of `v_mask` on one device may be relied on, other than what follows from the above.
Results may differ from a plain program's by a relative error of at most 0.0003.
Values sent between devices are 32-bit elements; how exact they have to be, the bound alone decides.
No kernel may reach another device: no remote copies, remote signals or barrier semaphores. Data moves between devices by JAX's collectives and lax.ppermute only.
A program may use at most 64 MiB of HBM per device.

v0:
```python
import jax
import jax.numpy as jnp
from jax import lax
from jax.sharding import PartitionSpec as P

STEPS = 4


def passed_along(value, axis, steps):
    count = lax.axis_size(axis)
    pairs = [(source, (source + steps) % count) for source in range(count)]
    return lax.ppermute(value, axis, pairs)


def shifted(block, axis, distance):
    devices = range(lax.axis_size(axis))
    route = [(i - distance, i) for i in devices if i - distance in devices]
    return lax.ppermute(block, axis, route)


def padded(cells, sides, width, closed):
    for axis, dim in sides:
        count = lax.axis_size(axis)
        ends = count if closed else count - 1
        head = lax.slice_in_dim(cells, 0, width, axis=dim)
        tail = lax.slice_in_dim(cells, cells.shape[dim] - width, cells.shape[dim], axis=dim)
        cells = jnp.concatenate(
            [
                lax.ppermute(tail, axis, [(i, (i + 1) % count) for i in range(ends)]),
                cells,
                lax.ppermute(head, axis, [((i + 1) % count, i) for i in range(ends)]),
            ],
            axis=dim,
        )
    return cells


def from_partner(value, axis, stride):
    mask = 2**stride
    pairs = [(source, source ^ mask) for source in range(lax.axis_size(axis))]
    return lax.ppermute(value, axis, pairs)


def minmod(first, second):
    return 0.5 * (jnp.sign(first) + jnp.sign(second)) * jnp.minimum(jnp.abs(first), jnp.abs(second))


def vertical_grad(field):
    upper = jnp.concatenate([field[..., 1:, :, :], field[..., -1:, :, :]], axis=-3)
    lower = jnp.concatenate([field[..., :1, :, :], field[..., :-1, :, :]], axis=-3)
    return 0.5 * (upper - lower)


def face_flux(far_back, here_cell, next_cell, far_next, grad_here, grad_next, faces):
    velocity, diffuse, slope, wetness = (faces[0], faces[1], faces[2], faces[3])
    forward = velocity >= 0.0
    jump_diff = next_cell - here_cell
    upwind_value = jnp.where(forward, here_cell, next_cell)
    upwind_diff = jnp.where(forward, here_cell - far_back, far_next - next_cell)
    speed = jnp.abs(velocity)
    advected = velocity * upwind_value + 0.5 * speed * (1.0 - speed) * minmod(
        jump_diff, upwind_diff
    )
    diffused = diffuse * (jump_diff - slope * 0.5 * (grad_here + grad_next))
    return wetness * (advected - diffused)


def advance(tracers, lon_ext, lat_ext, east_faces, north_faces):
    width = tracers.shape[-1]
    height = tracers.shape[-2]
    grad_x = vertical_grad(lon_ext)
    grad_y = vertical_grad(lat_ext)
    flux_x = face_flux(
        lon_ext[..., 0 : width + 1],
        lon_ext[..., 1 : width + 2],
        lon_ext[..., 2 : width + 3],
        lon_ext[..., 3 : width + 4],
        grad_x[..., 1 : width + 2],
        grad_x[..., 2 : width + 3],
        east_faces,
    )
    flux_y = face_flux(
        lat_ext[..., 0 : height + 1, :],
        lat_ext[..., 1 : height + 2, :],
        lat_ext[..., 2 : height + 3, :],
        lat_ext[..., 3 : height + 4, :],
        grad_y[..., 1 : height + 2, :],
        grad_y[..., 2 : height + 3, :],
        north_faces,
    )
    return (
        tracers - (flux_x[..., 1:] - flux_x[..., :-1]) - (flux_y[..., 1:, :] - flux_y[..., :-1, :])
    )


def on_device(temp, salt, u_courant, v_courant, diffusion, slope_x, slope_y, u_mask, v_mask):
    east_stack = jnp.stack([u_courant, diffusion, slope_x, u_mask.astype(jnp.float32)])
    north_stack = jnp.stack([v_courant, diffusion, slope_y, v_mask.astype(jnp.float32)])
    west_column = passed_along(east_stack[..., -1], "lon", 1)
    south_row = shifted(north_stack[..., -1, :], "lat", 1)
    east_faces = jnp.concatenate([west_column[..., None], east_stack], axis=-1)
    north_faces = jnp.concatenate([south_row[..., None, :], north_stack], axis=-2)
    height = temp.shape[-2]
    lon_count = lax.axis_size("lon")
    at_top = lax.axis_index("lat") == lax.axis_size("lat") - 1
    tracers = jnp.stack([temp, salt])
    for substep in range(STEPS):
        lon_ext = padded(tracers, (("lon", 3),), 2, True)
        lat_ext = padded(tracers, (("lat", 2),), 2, False)
        mirror_rows = tracers[:, :, height - 2 :, :]
        for bit_number in range(lon_count.bit_length() - 1):
            mirror_rows = from_partner(mirror_rows, "lon", bit_number)
        folded = mirror_rows[:, :, ::-1, ::-1]
        northern = jnp.where(at_top, folded, lat_ext[:, :, height + 2 :, :])
        lat_ext = jnp.concatenate([lat_ext[:, :, : height + 2, :], northern], axis=2)
        tracers = advance(tracers, lon_ext, lat_ext, east_faces, north_faces)
    return (tracers[0], tracers[1])


def solution(mesh):
    placed = (
        P(None, "lat", "lon"),
        P(None, "lat", "lon"),
        P(None, "lat", "lon"),
        P(None, "lat", "lon"),
        P(None, "lat", "lon"),
        P(None, "lat", "lon"),
        P(None, "lat", "lon"),
        P(None, "lat", "lon"),
        P(None, "lat", "lon"),
    )
    return jax.shard_map(
        on_device,
        mesh=mesh,
        in_specs=placed,
        out_specs=(P(None, "lat", "lon"), P(None, "lat", "lon")),
        check_vma=False,
    )
```

profile of v0, /device:TPU:66, one launch (start us, length us, event | category | flops | bytes accessed | tf_op | source)
XLA Modules:
  0.0 216.4 jit_solution(1884454644229541452)
XLA Ops:
  0.7 1.7 fusion.149
  2.3 1.9 collective-permute-start.5
  4.2 1.9 collective-permute-start.4
  6.2 2.0 fusion.147
  8.1 6.8 %collective-permute-start.1 = (f32[2,8,32,2]{3,2,1,0:T(8,128)}, f32[2,8,32,2]{3,2,1,0:T(8,128)S(1)}, u32[]{:S(2)}, u32[]{:S(2)}) collective-permute-start(f32[2,8,32,2]{3,2,1,0:T(8,128)} %get-tuple-element.45), channel_id=1, source_target_pairs={{0,32},{32,64},{64,96},{96,128},{128,160},{160,192},{192,224},{224... | collective-permute-start | bytes 12296 | tf_op jit(solution)/shard_map/ppermute | solution.py:29
  14.9 2.1 collective-permute-start.2
  17.5 3.9 %collective-permute-start = (f32[4,8,32]{2,1,0:T(8,128)S(1)}, f32[4,8,32]{2,1,0:T(8,128)S(1)}, u32[]{:S(2)}, u32[]{:S(2)}) collective-permute-start(f32[4,8,32]{2,1,0:T(8,128)S(1)} %bitcast.106), channel_id=1, source_target_pairs={{0,32},{32,64},{64,96},{96,128},{128,160},{160,192},{192,224},{224... | collective-permute-start | bytes 12296 | tf_op jit(solution)/shard_map/ppermute | solution.py:12
  21.6 1.6 copy.79
  23.2 4.0 %collective-permute-done = f32[4,8,32]{2,1,0:T(8,128)S(1)} collective-permute-done((f32[4,8,32]{2,1,0:T(8,128)S(1)}, f32[4,8,32]{2,1,0:T(8,128)S(1)}, u32[]{:S(2)}, u32[]{:S(2)}) %collective-permute-start) | collective-permute-done | bytes 4128 | tf_op jit(solution)/shard_map/ppermute | solution.py:12
  27.2 5.2 %collective-permute-start.9 = (f32[2,8,2,256]{3,2,1,0:T(2,128)}, f32[2,8,2,256]{3,2,1,0:T(2,128)}, u32[]{:S(2)}, u32[]{:S(2)}) collective-permute-start(f32[2,8,2,256]{3,2,1,0:T(2,128)} %get-tuple-element.48), channel_id=1, source_target_pairs={{1,0},{2,1},{3,2},{4,3},{5,4},{6,5},{7,6},{8,7},{9,8},{10,9},{11,1... | collective-permute-start | bytes 98312 | tf_op jit(solution)/shard_map/ppermute | solution.py:31
  33.5 1.9 collective-permute-start.3
  36.4 1.9 fusion.64
  38.4 3.4 %collective-permute-start.6 = (f32[2,8,2,256]{3,2,1,0:T(2,128)S(1)}, f32[2,8,2,256]{3,2,1,0:T(2,128)S(1)}, u32[]{:S(2)}, u32[]{:S(2)}) collective-permute-start(f32[2,8,2,256]{3,2,1,0:T(2,128)S(1)} %collective-permute-done.5), channel_id=1, source_target_pairs={{0,64},{32,96},{64,0},{96,32},{128,192},{160,224},{192,128},{224,1... | collective-permute-start | bytes 98312 | tf_op jit(solution)/shard_map/ppermute | solution.py:41
  41.8 3.3 %collective-permute-done.6 = f32[2,8,2,256]{3,2,1,0:T(2,128)S(1)} collective-permute-done((f32[2,8,2,256]{3,2,1,0:T(2,128)S(1)}, f32[2,8,2,256]{3,2,1,0:T(2,128)S(1)}, u32[]{:S(2)}, u32[]{:S(2)}) %collective-permute-start.6) | collective-permute-done | bytes 32800 | tf_op jit(solution)/shard_map/ppermute | solution.py:41
  45.0 5.0 %collective-permute-start.7 = (f32[2,8,2,256]{3,2,1,0:T(2,128)S(1)}, f32[2,8,2,256]{3,2,1,0:T(2,128)S(1)}, u32[]{:S(2)}, u32[]{:S(2)}) collective-permute-start(f32[2,8,2,256]{3,2,1,0:T(2,128)S(1)} %collective-permute-done.6), channel_id=1, source_target_pairs={{0,128},{32,160},{64,192},{96,224},{128,0},{160,32},{192,64},{224,... | collective-permute-start | bytes 98312 | tf_op jit(solution)/shard_map/ppermute | solution.py:41
  50.1 4.7 %collective-permute-done.7 = f32[2,8,2,256]{3,2,1,0:T(2,128)S(1)} collective-permute-done((f32[2,8,2,256]{3,2,1,0:T(2,128)S(1)}, f32[2,8,2,256]{3,2,1,0:T(2,128)S(1)}, u32[]{:S(2)}, u32[]{:S(2)}) %collective-permute-start.7) | collective-permute-done | bytes 32800 | tf_op jit(solution)/shard_map/ppermute | solution.py:41
  54.8 2.7 %collective-permute-start.8 = (f32[2,8,2,256]{3,2,1,0:T(2,128)S(1)}, f32[2,8,2,256]{3,2,1,0:T(2,128)S(1)}, u32[]{:S(2)}, u32[]{:S(2)}) collective-permute-start(f32[2,8,2,256]{3,2,1,0:T(2,128)S(1)} %collective-permute-done.7), channel_id=1, source_target_pairs={{0,256},{32,288},{64,320},{96,352},{128,384},{160,416},{192,448},{... | collective-permute-start | bytes 98312 | tf_op jit(solution)/shard_map/ppermute | solution.py:41
  57.8 0.9 copy.85
  59.4 0.8 copy.81
  60.3 1.8 collective-permute-done.8
  64.7 0.9 fusion.128
  66.2 5.8 %collective-permute-start.10 = (f32[2,8,32,2]{3,2,1,0:T(8,128)S(1)}, f32[2,8,32,2]{3,2,1,0:T(8,128)S(1)}, u32[]{:S(2)}, u32[]{:S(2)}) collective-permute-start(f32[2,8,32,2]{3,2,1,0:T(8,128)S(1)} %get-tuple-element.39), channel_id=1, source_target_pairs={{0,32},{32,64},{64,96},{96,128},{128,160},{160,192},{192,224},{224... | collective-permute-start | bytes 12296 | tf_op jit(solution)/shard_map/ppermute | solution.py:29
  72.0 3.4 %collective-permute-start.11 = (f32[2,8,32,2]{3,2,1,0:T(8,128)S(1)}, f32[2,8,32,2]{3,2,1,0:T(8,128)S(1)}, u32[]{:S(2)}, u32[]{:S(2)}) collective-permute-start(f32[2,8,32,2]{3,2,1,0:T(8,128)S(1)} %get-tuple-element.38), channel_id=1, source_target_pairs={{32,0},{64,32},{96,64},{128,96},{160,128},{192,160},{224,192},{256... | collective-permute-start | bytes 12296 | tf_op jit(solution)/shard_map/ppermute | solution.py:31
  76.0 7.5 %collective-permute-start.13 = (f32[2,8,2,256]{3,2,1,0:T(2,128)}, f32[2,8,2,256]{3,2,1,0:T(2,128)S(1)}, u32[]{:S(2)}, u32[]{:S(2)}) collective-permute-start(f32[2,8,2,256]{3,2,1,0:T(2,128)} %get-tuple-element.41), channel_id=1, source_target_pairs={{0,32},{32,0},{64,96},{96,64},{128,160},{160,128},{192,224},{224,1... | collective-permute-start | bytes 98312 | tf_op jit(solution)/shard_map/ppermute | solution.py:41
  83.5 1.9 collective-permute-start.12
  85.4 5.8 %collective-permute-start.17 = (f32[2,8,2,256]{3,2,1,0:T(2,128)}, f32[2,8,2,256]{3,2,1,0:T(2,128)}, u32[]{:S(2)}, u32[]{:S(2)}) collective-permute-start(f32[2,8,2,256]{3,2,1,0:T(2,128)} %get-tuple-element.40), channel_id=1, source_target_pairs={{1,0},{2,1},{3,2},{4,3},{5,4},{6,5},{7,6},{8,7},{9,8},{10,9},{11,1... | collective-permute-start | bytes 98312 | tf_op jit(solution)/shard_map/ppermute | solution.py:31
  91.6 1.9 collective-permute-start.14
  93.7 4.6 %collective-permute-done.14 = f32[2,8,2,256]{3,2,1,0:T(2,128)S(1)} collective-permute-done((f32[2,8,2,256]{3,2,1,0:T(2,128)S(1)}, f32[2,8,2,256]{3,2,1,0:T(2,128)S(1)}, u32[]{:S(2)}, u32[]{:S(2)}) %collective-permute-start.14) | collective-permute-done | bytes 32800 | tf_op jit(solution)/shard_map/ppermute | solution.py:41
  98.3 1.9 collective-permute-start.15
  100.4 7.8 %collective-permute-done.15 = f32[2,8,2,256]{3,2,1,0:T(2,128)S(1)} collective-permute-done((f32[2,8,2,256]{3,2,1,0:T(2,128)S(1)}, f32[2,8,2,256]{3,2,1,0:T(2,128)S(1)}, u32[]{:S(2)}, u32[]{:S(2)}) %collective-permute-start.15) | collective-permute-done | bytes 32800 | tf_op jit(solution)/shard_map/ppermute | solution.py:41
  108.1 2.9 %collective-permute-start.16 = (f32[2,8,2,256]{3,2,1,0:T(2,128)S(1)}, f32[2,8,2,256]{3,2,1,0:T(2,128)}, u32[]{:S(2)}, u32[]{:S(2)}) collective-permute-start(f32[2,8,2,256]{3,2,1,0:T(2,128)S(1)} %collective-permute-done.15), channel_id=1, source_target_pairs={{0,256},{32,288},{64,320},{96,352},{128,384},{160,416},{192,448},{... | collective-permute-start | bytes 98312 | tf_op jit(solution)/shard_map/ppermute | solution.py:41
  111.0 2.1 fusion.56
  113.2 2.4 %collective-permute-done.16 = f32[2,8,2,256]{3,2,1,0:T(2,128)} collective-permute-done((f32[2,8,2,256]{3,2,1,0:T(2,128)S(1)}, f32[2,8,2,256]{3,2,1,0:T(2,128)}, u32[]{:S(2)}, u32[]{:S(2)}) %collective-permute-start.16) | collective-permute-done | bytes 32800 | tf_op jit(solution)/shard_map/ppermute | solution.py:41
  115.5 1.0 rev.13
  117.7 0.8 copy-done.4
  118.8 1.0 fusion.120
  120.3 1.9 collective-permute-start.18
  122.2 3.9 %collective-permute-start.19 = (f32[2,8,32,2]{3,2,1,0:T(8,128)S(1)}, f32[2,8,32,2]{3,2,1,0:T(8,128)S(1)}, u32[]{:S(2)}, u32[]{:S(2)}) collective-permute-start(f32[2,8,32,2]{3,2,1,0:T(8,128)S(1)} %get-tuple-element.34), channel_id=1, source_target_pairs={{32,0},{64,32},{96,64},{128,96},{160,128},{192,160},{224,192},{256... | collective-permute-start | bytes 12296 | tf_op jit(solution)/shard_map/ppermute | solution.py:31
  126.2 5.4 %collective-permute-start.21 = (f32[2,8,2,256]{3,2,1,0:T(2,128)S(1)}, f32[2,8,2,256]{3,2,1,0:T(2,128)S(1)}, u32[]{:S(2)}, u32[]{:S(2)}) collective-permute-start(f32[2,8,2,256]{3,2,1,0:T(2,128)S(1)} %get-tuple-element.37), channel_id=1, source_target_pairs={{0,32},{32,0},{64,96},{96,64},{128,160},{160,128},{192,224},{224,1... | collective-permute-start | bytes 98312 | tf_op jit(solution)/shard_map/ppermute | solution.py:41
  131.6 1.9 collective-permute-start.20
  133.5 5.9 %collective-permute-start.25 = (f32[2,8,2,256]{3,2,1,0:T(2,128)S(1)}, f32[2,8,2,256]{3,2,1,0:T(2,128)S(1)}, u32[]{:S(2)}, u32[]{:S(2)}) collective-permute-start(f32[2,8,2,256]{3,2,1,0:T(2,128)S(1)} %get-tuple-element.36), channel_id=1, source_target_pairs={{1,0},{2,1},{3,2},{4,3},{5,4},{6,5},{7,6},{8,7},{9,8},{10,9},{11,1... | collective-permute-start | bytes 98312 | tf_op jit(solution)/shard_map/ppermute | solution.py:31
  139.8 1.9 collective-permute-start.22
  141.9 4.6 %collective-permute-done.22 = f32[2,8,2,256]{3,2,1,0:T(2,128)S(1)} collective-permute-done((f32[2,8,2,256]{3,2,1,0:T(2,128)S(1)}, f32[2,8,2,256]{3,2,1,0:T(2,128)S(1)}, u32[]{:S(2)}, u32[]{:S(2)}) %collective-permute-start.22) | collective-permute-done | bytes 32800 | tf_op jit(solution)/shard_map/ppermute | solution.py:41
  146.5 1.9 collective-permute-start.23
  148.6 7.8 %collective-permute-done.23 = f32[2,8,2,256]{3,2,1,0:T(2,128)S(1)} collective-permute-done((f32[2,8,2,256]{3,2,1,0:T(2,128)S(1)}, f32[2,8,2,256]{3,2,1,0:T(2,128)S(1)}, u32[]{:S(2)}, u32[]{:S(2)}) %collective-permute-start.23) | collective-permute-done | bytes 32800 | tf_op jit(solution)/shard_map/ppermute | solution.py:41
  156.4 2.9 %collective-permute-start.24 = (f32[2,8,2,256]{3,2,1,0:T(2,128)S(1)}, f32[2,8,2,256]{3,2,1,0:T(2,128)S(1)}, u32[]{:S(2)}, u32[]{:S(2)}) collective-permute-start(f32[2,8,2,256]{3,2,1,0:T(2,128)S(1)} %collective-permute-done.23), channel_id=1, source_target_pairs={{0,256},{32,288},{64,320},{96,352},{128,384},{160,416},{192,448},{... | collective-permute-start | bytes 98312 | tf_op jit(solution)/shard_map/ppermute | solution.py:41
  159.3 2.1 fusion.48
  161.4 2.3 %collective-permute-done.24 = f32[2,8,2,256]{3,2,1,0:T(2,128)S(1)} collective-permute-done((f32[2,8,2,256]{3,2,1,0:T(2,128)S(1)}, f32[2,8,2,256]{3,2,1,0:T(2,128)S(1)}, u32[]{:S(2)}, u32[]{:S(2)}) %collective-permute-start.24) | collective-permute-done | bytes 32800 | tf_op jit(solution)/shard_map/ppermute | solution.py:41
  164.4 0.8 copy-done.5
  165.5 1.0 fusion.112
  167.0 1.9 collective-permute-start.26
  168.9 3.9 %collective-permute-start.27 = (f32[2,8,32,2]{3,2,1,0:T(8,128)S(1)}, f32[2,8,32,2]{3,2,1,0:T(8,128)S(1)}, u32[]{:S(2)}, u32[]{:S(2)}) collective-permute-start(f32[2,8,32,2]{3,2,1,0:T(8,128)S(1)} %get-tuple-element.30), channel_id=1, source_target_pairs={{32,0},{64,32},{96,64},{128,96},{160,128},{192,160},{224,192},{256... | collective-permute-start | bytes 12296 | tf_op jit(solution)/shard_map/ppermute | solution.py:31
  173.5 5.4 %collective-permute-start.29 = (f32[2,8,2,256]{3,2,1,0:T(2,128)}, f32[2,8,2,256]{3,2,1,0:T(2,128)S(1)}, u32[]{:S(2)}, u32[]{:S(2)}) collective-permute-start(f32[2,8,2,256]{3,2,1,0:T(2,128)} %get-tuple-element.33), channel_id=1, source_target_pairs={{0,32},{32,0},{64,96},{96,64},{128,160},{160,128},{192,224},{224,1... | collective-permute-start | bytes 98312 | tf_op jit(solution)/shard_map/ppermute | solution.py:41
  178.9 1.9 collective-permute-start.28
  180.8 5.8 %collective-permute-start.33 = (f32[2,8,2,256]{3,2,1,0:T(2,128)}, f32[2,8,2,256]{3,2,1,0:T(2,128)}, u32[]{:S(2)}, u32[]{:S(2)}) collective-permute-start(f32[2,8,2,256]{3,2,1,0:T(2,128)} %get-tuple-element.32), channel_id=1, source_target_pairs={{1,0},{2,1},{3,2},{4,3},{5,4},{6,5},{7,6},{8,7},{9,8},{10,9},{11,1... | collective-permute-start | bytes 98312 | tf_op jit(solution)/shard_map/ppermute | solution.py:31
  187.0 1.9 collective-permute-start.30
  189.1 4.6 %collective-permute-done.30 = f32[2,8,2,256]{3,2,1,0:T(2,128)S(1)} collective-permute-done((f32[2,8,2,256]{3,2,1,0:T(2,128)S(1)}, f32[2,8,2,256]{3,2,1,0:T(2,128)S(1)}, u32[]{:S(2)}, u32[]{:S(2)}) %collective-permute-start.30) | collective-permute-done | bytes 32800 | tf_op jit(solution)/shard_map/ppermute | solution.py:41
  193.7 1.9 collective-permute-start.31
  195.8 7.8 %collective-permute-done.31 = f32[2,8,2,256]{3,2,1,0:T(2,128)S(1)} collective-permute-done((f32[2,8,2,256]{3,2,1,0:T(2,128)S(1)}, f32[2,8,2,256]{3,2,1,0:T(2,128)S(1)}, u32[]{:S(2)}, u32[]{:S(2)}) %collective-permute-start.31) | collective-permute-done | bytes 32800 | tf_op jit(solution)/shard_map/ppermute | solution.py:41
  203.5 2.9 %collective-permute-start.32 = (f32[2,8,2,256]{3,2,1,0:T(2,128)S(1)}, f32[2,8,2,256]{3,2,1,0:T(2,128)}, u32[]{:S(2)}, u32[]{:S(2)}) collective-permute-start(f32[2,8,2,256]{3,2,1,0:T(2,128)S(1)} %collective-permute-done.31), channel_id=1, source_target_pairs={{0,256},{32,288},{64,320},{96,352},{128,384},{160,416},{192,448},{... | collective-permute-start | bytes 98312 | tf_op jit(solution)/shard_map/ppermute | solution.py:41
  206.4 2.1 fusion.40
  208.5 2.4 %collective-permute-done.32 = f32[2,8,2,256]{3,2,1,0:T(2,128)} collective-permute-done((f32[2,8,2,256]{3,2,1,0:T(2,128)S(1)}, f32[2,8,2,256]{3,2,1,0:T(2,128)}, u32[]{:S(2)}, u32[]{:S(2)}) %collective-permute-start.32) | collective-permute-done | bytes 32800 | tf_op jit(solution)/shard_map/ppermute | solution.py:41
  210.9 1.0 rev.15
  214.2 1.0 fusion.104
  (140 shorter events, 16.8 us)
Async XLA Ops:
  0.6 16.4 %copy-start.26 = (s32[8,32,256]{2,1,0:T(8,128)S(1)}, s32[8,32,256]{2,1,0:T(8,128)}, u32[]{:S(2)}) copy-start(s32[8,32,256]{2,1,0:T(8,128)} %param.16) | copy-start | bytes 786436
  0.6 16.4 %copy-start.23 = (f32[8,32,256]{2,1,0:T(8,128)S(1)}, f32[8,32,256]{2,1,0:T(8,128)}, u32[]{:S(2)}) copy-start(f32[8,32,256]{2,1,0:T(8,128)} %param.13) | copy-start | bytes 786436
  0.7 16.4 %copy-start.25 = (f32[8,32,256]{2,1,0:T(8,128)S(1)}, f32[8,32,256]{2,1,0:T(8,128)}, u32[]{:S(2)}) copy-start(f32[8,32,256]{2,1,0:T(8,128)} %param.11) | copy-start | bytes 786436
  0.7 16.4 %copy-start.24 = (f32[8,32,256]{2,1,0:T(8,128)S(1)}, f32[8,32,256]{2,1,0:T(8,128)}, u32[]{:S(2)}) copy-start(f32[8,32,256]{2,1,0:T(8,128)} %param.14) | copy-start | bytes 786436
  2.3 36.0 %collective-permute-start.5 = (f32[2,8,2,256]{3,2,1,0:T(2,128)}, f32[2,8,2,256]{3,2,1,0:T(2,128)S(1)}, u32[]{:S(2)}, u32[]{:S(2)}) collective-permute-start(f32[2,8,2,256]{3,2,1,0:T(2,128)} %get-tuple-element.49), channel_id=1, source_target_pairs={{0,32},{32,0},{64,96},{96,64},{128,160},{160,128},{192,224},{224,1... | collective-permute-start | bytes 98312 | tf_op jit(solution)/shard_map/ppermute | solution.py:41
  4.2 58.9 %collective-permute-start.4 = (f32[2,8,2,256]{3,2,1,0:T(2,128)}, f32[2,8,2,256]{3,2,1,0:T(2,128)S(1)}, u32[]{:S(2)}, u32[]{:S(2)}) collective-permute-start(f32[2,8,2,256]{3,2,1,0:T(2,128)} %get-tuple-element.49), channel_id=1, source_target_pairs={{0,1},{1,2},{2,3},{3,4},{4,5},{5,6},{6,7},{7,8},{8,9},{9,10},{10,1... | collective-permute-start | bytes 98312 | tf_op jit(solution)/shard_map/ppermute | solution.py:29
  8.1 13.3 %copy-start.27 = (s32[8,32,256]{2,1,0:T(8,128)S(1)}, s32[8,32,256]{2,1,0:T(8,128)}, u32[]{:S(2)}) copy-start(s32[8,32,256]{2,1,0:T(8,128)} %param.17) | copy-start | bytes 786436
  8.1 25.3 %collective-permute-start.1 = (f32[2,8,32,2]{3,2,1,0:T(8,128)}, f32[2,8,32,2]{3,2,1,0:T(8,128)S(1)}, u32[]{:S(2)}, u32[]{:S(2)}) collective-permute-start(f32[2,8,32,2]{3,2,1,0:T(8,128)} %get-tuple-element.45), channel_id=1, source_target_pairs={{0,32},{32,64},{64,96},{96,128},{128,160},{160,192},{192,224},{224... | collective-permute-start | bytes 12296 | tf_op jit(solution)/shard_map/ppermute | solution.py:29
  14.9 6.6 %copy-start.28 = (f32[8,32,256]{2,1,0:T(8,128)S(1)}, f32[8,32,256]{2,1,0:T(8,128)}, u32[]{:S(2)}) copy-start(f32[8,32,256]{2,1,0:T(8,128)} %param.15) | copy-start | bytes 786436
  14.9 6.6 %copy-start.29 = (f32[8,32,256]{2,1,0:T(8,128)S(1)}, f32[8,32,256]{2,1,0:T(8,128)}, u32[]{:S(2)}) copy-start(f32[8,32,256]{2,1,0:T(8,128)} %param.12) | copy-start | bytes 786436
  14.9 20.5 %collective-permute-start.2 = (f32[2,8,32,2]{3,2,1,0:T(8,128)}, f32[2,8,32,2]{3,2,1,0:T(8,128)S(1)}, u32[]{:S(2)}, u32[]{:S(2)}) collective-permute-start(f32[2,8,32,2]{3,2,1,0:T(8,128)} %get-tuple-element.44), channel_id=1, source_target_pairs={{32,0},{64,32},{96,64},{128,96},{160,128},{192,160},{224,192},{256... | collective-permute-start | bytes 12296 | tf_op jit(solution)/shard_map/ppermute | solution.py:31
  17.5 9.7 %collective-permute-start = (f32[4,8,32]{2,1,0:T(8,128)S(1)}, f32[4,8,32]{2,1,0:T(8,128)S(1)}, u32[]{:S(2)}, u32[]{:S(2)}) collective-permute-start(f32[4,8,32]{2,1,0:T(8,128)S(1)} %bitcast.106), channel_id=1, source_target_pairs={{0,32},{32,64},{64,96},{96,128},{128,160},{160,192},{192,224},{224... | collective-permute-start | bytes 12296 | tf_op jit(solution)/shard_map/ppermute | solution.py:12
  27.2 35.2 %collective-permute-start.9 = (f32[2,8,2,256]{3,2,1,0:T(2,128)}, f32[2,8,2,256]{3,2,1,0:T(2,128)}, u32[]{:S(2)}, u32[]{:S(2)}) collective-permute-start(f32[2,8,2,256]{3,2,1,0:T(2,128)} %get-tuple-element.48), channel_id=1, source_target_pairs={{1,0},{2,1},{3,2},{4,3},{5,4},{6,5},{7,6},{8,7},{9,8},{10,9},{11,1... | collective-permute-start | bytes 98312 | tf_op jit(solution)/shard_map/ppermute | solution.py:31
  33.1 2.2 %copy-start = (f32[8,32,256]{2,1,0:T(8,128)S(1)}, f32[8,32,256]{2,1,0:T(8,128)}, u32[]{:S(2)}) copy-start(f32[8,32,256]{2,1,0:T(8,128)} %param.10) | copy-start | bytes 786436
  33.2 2.2 %copy-start.1 = (f32[8,32,256]{2,1,0:T(8,128)S(1)}, f32[8,32,256]{2,1,0:T(8,128)}, u32[]{:S(2)}) copy-start(f32[8,32,256]{2,1,0:T(8,128)} %param.9) | copy-start | bytes 786436
  33.5 8.3 %collective-permute-start.3 = (f32[4,8,256]{2,1,0:T(8,128)S(1)}, f32[4,8,256]{2,1,0:T(8,128)S(1)}, u32[]{:S(2)}, u32[]{:S(2)}) collective-permute-start(f32[4,8,256]{2,1,0:T(8,128)S(1)} %bitcast.104), channel_id=1, source_target_pairs={{0,1},{1,2},{2,3},{3,4},{4,5},{5,6},{6,7},{7,8},{8,9},{9,10},{10,1... | collective-permute-start | bytes 98312 | tf_op jit(solution)/shard_map/ppermute | solution.py:18
  36.4 5.3 %copy-start.2 = (f32[4,8,32,256]{3,1,2,0:T(8,128)S(1)}, f32[4,8,32,256]{3,1,2,0:T(8,128)}, u32[]{:S(2)}) copy-start(f32[4,8,32,256]{3,1,2,0:T(8,128)} %copy.79) | copy-start | bytes 3145732
  38.4 6.7 %collective-permute-start.6 = (f32[2,8,2,256]{3,2,1,0:T(2,128)S(1)}, f32[2,8,2,256]{3,2,1,0:T(2,128)S(1)}, u32[]{:S(2)}, u32[]{:S(2)}) collective-permute-start(f32[2,8,2,256]{3,2,1,0:T(2,128)S(1)} %collective-permute-done.5), channel_id=1, source_target_pairs={{0,64},{32,96},{64,0},{96,32},{128,192},{160,224},{192,128},{224,1... | collective-permute-start | bytes 98312 | tf_op jit(solution)/shard_map/ppermute | solution.py:41
  45.0 9.7 %collective-permute-start.7 = (f32[2,8,2,256]{3,2,1,0:T(2,128)S(1)}, f32[2,8,2,256]{3,2,1,0:T(2,128)S(1)}, u32[]{:S(2)}, u32[]{:S(2)}) collective-permute-start(f32[2,8,2,256]{3,2,1,0:T(2,128)S(1)} %collective-permute-done.6), channel_id=1, source_target_pairs={{0,128},{32,160},{64,192},{96,224},{128,0},{160,32},{192,64},{224,... | collective-permute-start | bytes 98312 | tf_op jit(solution)/shard_map/ppermute | solution.py:41
  54.8 7.3 %collective-permute-start.8 = (f32[2,8,2,256]{3,2,1,0:T(2,128)S(1)}, f32[2,8,2,256]{3,2,1,0:T(2,128)S(1)}, u32[]{:S(2)}, u32[]{:S(2)}) collective-permute-start(f32[2,8,2,256]{3,2,1,0:T(2,128)S(1)} %collective-permute-done.7), channel_id=1, source_target_pairs={{0,256},{32,288},{64,320},{96,352},{128,384},{160,416},{192,448},{... | collective-permute-start | bytes 98312 | tf_op jit(solution)/shard_map/ppermute | solution.py:41
  57.8 5.9 %copy-start.3 = (f32[8,33,256]{2,1,0:T(8,128)}, f32[8,33,256]{2,1,0:T(8,128)S(1)}, u32[]{:S(2)}) copy-start(f32[8,33,256]{2,1,0:T(8,128)S(1)} %copy.84) | copy-start | bytes 811012
  63.5 1.0 copy-start.7
  63.5 1.1 copy-start.11
  63.5 1.2 copy-start.15
  64.7 1.1 copy-start.22
  66.2 25.0 %collective-permute-start.10 = (f32[2,8,32,2]{3,2,1,0:T(8,128)S(1)}, f32[2,8,32,2]{3,2,1,0:T(8,128)S(1)}, u32[]{:S(2)}, u32[]{:S(2)}) collective-permute-start(f32[2,8,32,2]{3,2,1,0:T(8,128)S(1)} %get-tuple-element.39), channel_id=1, source_target_pairs={{0,32},{32,64},{64,96},{96,128},{128,160},{160,192},{192,224},{224... | collective-permute-start | bytes 12296 | tf_op jit(solution)/shard_map/ppermute | solution.py:29
  72.0 19.3 %collective-permute-start.11 = (f32[2,8,32,2]{3,2,1,0:T(8,128)S(1)}, f32[2,8,32,2]{3,2,1,0:T(8,128)S(1)}, u32[]{:S(2)}, u32[]{:S(2)}) collective-permute-start(f32[2,8,32,2]{3,2,1,0:T(8,128)S(1)} %get-tuple-element.38), channel_id=1, source_target_pairs={{32,0},{64,32},{96,64},{128,96},{160,128},{192,160},{224,192},{256... | collective-permute-start | bytes 12296 | tf_op jit(solution)/shard_map/ppermute | solution.py:31
  76.0 15.6 %collective-permute-start.13 = (f32[2,8,2,256]{3,2,1,0:T(2,128)}, f32[2,8,2,256]{3,2,1,0:T(2,128)S(1)}, u32[]{:S(2)}, u32[]{:S(2)}) collective-permute-start(f32[2,8,2,256]{3,2,1,0:T(2,128)} %get-tuple-element.41), channel_id=1, source_target_pairs={{0,32},{32,0},{64,96},{96,64},{128,160},{160,128},{192,224},{224,1... | collective-permute-start | bytes 98312 | tf_op jit(solution)/shard_map/ppermute | solution.py:41
  83.5 33.8 %collective-permute-start.12 = (f32[2,8,2,256]{3,2,1,0:T(2,128)}, f32[2,8,2,256]{3,2,1,0:T(2,128)S(1)}, u32[]{:S(2)}, u32[]{:S(2)}) collective-permute-start(f32[2,8,2,256]{3,2,1,0:T(2,128)} %get-tuple-element.41), channel_id=1, source_target_pairs={{0,1},{1,2},{2,3},{3,4},{4,5},{5,6},{6,7},{7,8},{8,9},{9,10},{10,1... | collective-permute-start | bytes 98312 | tf_op jit(solution)/shard_map/ppermute | solution.py:29
  85.4 31.1 %collective-permute-start.17 = (f32[2,8,2,256]{3,2,1,0:T(2,128)}, f32[2,8,2,256]{3,2,1,0:T(2,128)}, u32[]{:S(2)}, u32[]{:S(2)}) collective-permute-start(f32[2,8,2,256]{3,2,1,0:T(2,128)} %get-tuple-element.40), channel_id=1, source_target_pairs={{1,0},{2,1},{3,2},{4,3},{5,4},{6,5},{7,6},{8,7},{9,8},{10,9},{11,1... | collective-permute-start | bytes 98312 | tf_op jit(solution)/shard_map/ppermute | solution.py:31
  91.6 6.7 %collective-permute-start.14 = (f32[2,8,2,256]{3,2,1,0:T(2,128)S(1)}, f32[2,8,2,256]{3,2,1,0:T(2,128)S(1)}, u32[]{:S(2)}, u32[]{:S(2)}) collective-permute-start(f32[2,8,2,256]{3,2,1,0:T(2,128)S(1)} %collective-permute-done.13), channel_id=1, source_target_pairs={{0,64},{32,96},{64,0},{96,32},{128,192},{160,224},{192,128},{224,1... | collective-permute-start | bytes 98312 | tf_op jit(solution)/shard_map/ppermute | solution.py:41
  98.3 9.9 %collective-permute-start.15 = (f32[2,8,2,256]{3,2,1,0:T(2,128)S(1)}, f32[2,8,2,256]{3,2,1,0:T(2,128)S(1)}, u32[]{:S(2)}, u32[]{:S(2)}) collective-permute-start(f32[2,8,2,256]{3,2,1,0:T(2,128)S(1)} %collective-permute-done.14), channel_id=1, source_target_pairs={{0,128},{32,160},{64,192},{96,224},{128,0},{160,32},{192,64},{224,... | collective-permute-start | bytes 98312 | tf_op jit(solution)/shard_map/ppermute | solution.py:41
  108.1 7.4 %collective-permute-start.16 = (f32[2,8,2,256]{3,2,1,0:T(2,128)S(1)}, f32[2,8,2,256]{3,2,1,0:T(2,128)}, u32[]{:S(2)}, u32[]{:S(2)}) collective-permute-start(f32[2,8,2,256]{3,2,1,0:T(2,128)S(1)} %collective-permute-done.15), channel_id=1, source_target_pairs={{0,256},{32,288},{64,320},{96,352},{128,384},{160,416},{192,448},{... | collective-permute-start | bytes 98312 | tf_op jit(solution)/shard_map/ppermute | solution.py:41
  117.5 1.0 copy-start.4
  117.5 1.1 copy-start.8
  117.5 1.2 copy-start.12
  117.6 1.2 copy-start.16
  118.8 1.1 copy-start.20
  120.3 19.2 %collective-permute-start.18 = (f32[2,8,32,2]{3,2,1,0:T(8,128)S(1)}, f32[2,8,32,2]{3,2,1,0:T(8,128)S(1)}, u32[]{:S(2)}, u32[]{:S(2)}) collective-permute-start(f32[2,8,32,2]{3,2,1,0:T(8,128)S(1)} %get-tuple-element.35), channel_id=1, source_target_pairs={{0,32},{32,64},{64,96},{96,128},{128,160},{160,192},{192,224},{224... | collective-permute-start | bytes 12296 | tf_op jit(solution)/shard_map/ppermute | solution.py:29
  122.2 17.2 %collective-permute-start.19 = (f32[2,8,32,2]{3,2,1,0:T(8,128)S(1)}, f32[2,8,32,2]{3,2,1,0:T(8,128)S(1)}, u32[]{:S(2)}, u32[]{:S(2)}) collective-permute-start(f32[2,8,32,2]{3,2,1,0:T(8,128)S(1)} %get-tuple-element.34), channel_id=1, source_target_pairs={{32,0},{64,32},{96,64},{128,96},{160,128},{192,160},{224,192},{256... | collective-permute-start | bytes 12296 | tf_op jit(solution)/shard_map/ppermute | solution.py:31
  126.2 13.6 %collective-permute-start.21 = (f32[2,8,2,256]{3,2,1,0:T(2,128)S(1)}, f32[2,8,2,256]{3,2,1,0:T(2,128)S(1)}, u32[]{:S(2)}, u32[]{:S(2)}) collective-permute-start(f32[2,8,2,256]{3,2,1,0:T(2,128)S(1)} %get-tuple-element.37), channel_id=1, source_target_pairs={{0,32},{32,0},{64,96},{96,64},{128,160},{160,128},{192,224},{224,1... | collective-permute-start | bytes 98312 | tf_op jit(solution)/shard_map/ppermute | solution.py:41
  131.6 32.5 %collective-permute-start.20 = (f32[2,8,2,256]{3,2,1,0:T(2,128)S(1)}, f32[2,8,2,256]{3,2,1,0:T(2,128)S(1)}, u32[]{:S(2)}, u32[]{:S(2)}) collective-permute-start(f32[2,8,2,256]{3,2,1,0:T(2,128)S(1)} %get-tuple-element.37), channel_id=1, source_target_pairs={{0,1},{1,2},{2,3},{3,4},{4,5},{5,6},{6,7},{7,8},{8,9},{9,10},{10,1... | collective-permute-start | bytes 98312 | tf_op jit(solution)/shard_map/ppermute | solution.py:29
  133.5 30.5 %collective-permute-start.25 = (f32[2,8,2,256]{3,2,1,0:T(2,128)S(1)}, f32[2,8,2,256]{3,2,1,0:T(2,128)S(1)}, u32[]{:S(2)}, u32[]{:S(2)}) collective-permute-start(f32[2,8,2,256]{3,2,1,0:T(2,128)S(1)} %get-tuple-element.36), channel_id=1, source_target_pairs={{1,0},{2,1},{3,2},{4,3},{5,4},{6,5},{7,6},{8,7},{9,8},{10,9},{11,1... | collective-permute-start | bytes 98312 | tf_op jit(solution)/shard_map/ppermute | solution.py:31
  139.8 6.7 %collective-permute-start.22 = (f32[2,8,2,256]{3,2,1,0:T(2,128)S(1)}, f32[2,8,2,256]{3,2,1,0:T(2,128)S(1)}, u32[]{:S(2)}, u32[]{:S(2)}) collective-permute-start(f32[2,8,2,256]{3,2,1,0:T(2,128)S(1)} %collective-permute-done.21), channel_id=1, source_target_pairs={{0,64},{32,96},{64,0},{96,32},{128,192},{160,224},{192,128},{224,1... | collective-permute-start | bytes 98312 | tf_op jit(solution)/shard_map/ppermute | solution.py:41
  146.5 9.9 %collective-permute-start.23 = (f32[2,8,2,256]{3,2,1,0:T(2,128)S(1)}, f32[2,8,2,256]{3,2,1,0:T(2,128)S(1)}, u32[]{:S(2)}, u32[]{:S(2)}) collective-permute-start(f32[2,8,2,256]{3,2,1,0:T(2,128)S(1)} %collective-permute-done.22), channel_id=1, source_target_pairs={{0,128},{32,160},{64,192},{96,224},{128,0},{160,32},{192,64},{224,... | collective-permute-start | bytes 98312 | tf_op jit(solution)/shard_map/ppermute | solution.py:41
  156.4 7.3 %collective-permute-start.24 = (f32[2,8,2,256]{3,2,1,0:T(2,128)S(1)}, f32[2,8,2,256]{3,2,1,0:T(2,128)S(1)}, u32[]{:S(2)}, u32[]{:S(2)}) collective-permute-start(f32[2,8,2,256]{3,2,1,0:T(2,128)S(1)} %collective-permute-done.23), channel_id=1, source_target_pairs={{0,256},{32,288},{64,320},{96,352},{128,384},{160,416},{192,448},{... | collective-permute-start | bytes 98312 | tf_op jit(solution)/shard_map/ppermute | solution.py:41
  164.2 1.0 copy-start.5
  164.2 1.1 copy-start.9
  164.3 1.2 copy-start.13
  164.3 1.2 copy-start.17
  165.5 1.1 copy-start.21
  167.0 19.6 %collective-permute-start.26 = (f32[2,8,32,2]{3,2,1,0:T(8,128)S(1)}, f32[2,8,32,2]{3,2,1,0:T(8,128)S(1)}, u32[]{:S(2)}, u32[]{:S(2)}) collective-permute-start(f32[2,8,32,2]{3,2,1,0:T(8,128)S(1)} %get-tuple-element.31), channel_id=1, source_target_pairs={{0,32},{32,64},{64,96},{96,128},{128,160},{160,192},{192,224},{224... | collective-permute-start | bytes 12296 | tf_op jit(solution)/shard_map/ppermute | solution.py:29
  168.9 17.7 %collective-permute-start.27 = (f32[2,8,32,2]{3,2,1,0:T(8,128)S(1)}, f32[2,8,32,2]{3,2,1,0:T(8,128)S(1)}, u32[]{:S(2)}, u32[]{:S(2)}) collective-permute-start(f32[2,8,32,2]{3,2,1,0:T(8,128)S(1)} %get-tuple-element.30), channel_id=1, source_target_pairs={{32,0},{64,32},{96,64},{128,96},{160,128},{192,160},{224,192},{256... | collective-permute-start | bytes 12296 | tf_op jit(solution)/shard_map/ppermute | solution.py:31
  173.5 13.4 %collective-permute-start.29 = (f32[2,8,2,256]{3,2,1,0:T(2,128)}, f32[2,8,2,256]{3,2,1,0:T(2,128)S(1)}, u32[]{:S(2)}, u32[]{:S(2)}) collective-permute-start(f32[2,8,2,256]{3,2,1,0:T(2,128)} %get-tuple-element.33), channel_id=1, source_target_pairs={{0,32},{32,0},{64,96},{96,64},{128,160},{160,128},{192,224},{224,1... | collective-permute-start | bytes 98312 | tf_op jit(solution)/shard_map/ppermute | solution.py:41
  178.9 33.8 %collective-permute-start.28 = (f32[2,8,2,256]{3,2,1,0:T(2,128)}, f32[2,8,2,256]{3,2,1,0:T(2,128)S(1)}, u32[]{:S(2)}, u32[]{:S(2)}) collective-permute-start(f32[2,8,2,256]{3,2,1,0:T(2,128)} %get-tuple-element.33), channel_id=1, source_target_pairs={{0,1},{1,2},{2,3},{3,4},{4,5},{5,6},{6,7},{7,8},{8,9},{9,10},{10,1... | collective-permute-start | bytes 98312 | tf_op jit(solution)/shard_map/ppermute | solution.py:29
  180.8 31.1 %collective-permute-start.33 = (f32[2,8,2,256]{3,2,1,0:T(2,128)}, f32[2,8,2,256]{3,2,1,0:T(2,128)}, u32[]{:S(2)}, u32[]{:S(2)}) collective-permute-start(f32[2,8,2,256]{3,2,1,0:T(2,128)} %get-tuple-element.32), channel_id=1, source_target_pairs={{1,0},{2,1},{3,2},{4,3},{5,4},{6,5},{7,6},{8,7},{9,8},{10,9},{11,1... | collective-permute-start | bytes 98312 | tf_op jit(solution)/shard_map/ppermute | solution.py:31
  187.0 6.7 %collective-permute-start.30 = (f32[2,8,2,256]{3,2,1,0:T(2,128)S(1)}, f32[2,8,2,256]{3,2,1,0:T(2,128)S(1)}, u32[]{:S(2)}, u32[]{:S(2)}) collective-permute-start(f32[2,8,2,256]{3,2,1,0:T(2,128)S(1)} %collective-permute-done.29), channel_id=1, source_target_pairs={{0,64},{32,96},{64,0},{96,32},{128,192},{160,224},{192,128},{224,1... | collective-permute-start | bytes 98312 | tf_op jit(solution)/shard_map/ppermute | solution.py:41
  193.7 9.9 %collective-permute-start.31 = (f32[2,8,2,256]{3,2,1,0:T(2,128)S(1)}, f32[2,8,2,256]{3,2,1,0:T(2,128)S(1)}, u32[]{:S(2)}, u32[]{:S(2)}) collective-permute-start(f32[2,8,2,256]{3,2,1,0:T(2,128)S(1)} %collective-permute-done.30), channel_id=1, source_target_pairs={{0,128},{32,160},{64,192},{96,224},{128,0},{160,32},{192,64},{224,... | collective-permute-start | bytes 98312 | tf_op jit(solution)/shard_map/ppermute | solution.py:41
  203.5 7.4 %collective-permute-start.32 = (f32[2,8,2,256]{3,2,1,0:T(2,128)S(1)}, f32[2,8,2,256]{3,2,1,0:T(2,128)}, u32[]{:S(2)}, u32[]{:S(2)}) collective-permute-start(f32[2,8,2,256]{3,2,1,0:T(2,128)S(1)} %collective-permute-done.31), channel_id=1, source_target_pairs={{0,256},{32,288},{64,320},{96,352},{128,384},{160,416},{192,448},{... | collective-permute-start | bytes 98312 | tf_op jit(solution)/shard_map/ppermute | solution.py:41
  212.9 1.0 copy-start.6
  212.9 1.1 copy-start.10
  212.9 1.2 copy-start.14
  212.9 1.2 copy-start.18
  214.2 1.1 copy-start.19
where the time goes:
time: 218 us; the launch traced here: 216 us
  starting transfers between devices  117 us (54%)
  waiting for transfers between devices  57.9 us (27%)
  other arithmetic  23.4 us (11%)
  local copies, waits for them, and re-layouts  16.1 us (7%)
    ppermute x16, waiting for transfers between devices, from_partner(): return lax.ppermute(value, axis, pairs)  53.9 us
    ppermute x16, starting transfers between devices, from_partner(): return lax.ppermute(value, axis, pairs)  51.4 us
    ppermute x8, starting transfers between devices, padded(): lax.ppermute(head, axis, [((i + 1) % count, i) for i in range(ends)])  35.9 us
    ppermute x8, starting transfers between devices, padded(): lax.ppermute(tail, axis, [(i, (i + 1) % count) for i in range(ends)])  24.1 us
    mul x10, other arithmetic, face_flux(): return wetness * (advected - diffused)  12.5 us
    unnamed x62, local copies, waits for them, and re-layouts  5.37 us
  transfers between devices with their start and end apart: 34, of which 13 were waited for; matrix products, arithmetic and copies ran while one was open for 12% of the time, Pallas kernels for 0%

commit v1 on v0

v1 whole, which is shorter than its diff:
```python
import functools

import jax
import jax.numpy as jnp
from jax import lax
from jax.experimental import pallas as pl
from jax.experimental.pallas import tpu as pltpu
from jax.sharding import PartitionSpec as P

STEPS = 4
HALO = 2 * STEPS
LEVELS = 8
HEIGHT = 32
WIDTH = 256
EXT = HEIGHT + 2 * HALO
TOP = HALO + HEIGHT - 1
F32 = jnp.float32
VMEM = pl.BlockSpec(memory_space=pltpu.VMEM)
SMEM = pl.BlockSpec(memory_space=pltpu.SMEM)
PARAMS = pltpu.CompilerParams(vmem_limit_bytes=48 * 2**20)

TRACERS, XF, YF = (0, 1), (2, 3, 4), (5, 6, 7)
MESSAGE = 2 * 8 + 3 * 6 + 3 * 7


def slot(field, k):
    if field < 2:
        return field * 8 + k
    if field < 5:
        return 16 + (field - 2) * 6 + k
    return 34 + (field - 5) * 7 + k


def rows_of(field):
    return 8 if field < 2 else 6 if field < 5 else 7


def level_major(x):
    x = x.reshape(LEVELS, HEIGHT // 8, 8, WIDTH // 128, 128)
    return x.transpose(0, 1, 3, 2, 4).reshape(-1, 128)


def from_level_major(x):
    x = x.reshape(LEVELS, HEIGHT // 8, WIDTH // 128, 8, 128)
    return x.transpose(0, 1, 3, 2, 4).reshape(LEVELS, HEIGHT, WIDTH)


def places(j):
    start = (j // 8) * 16 + j % 8
    return [pl.ds(start + 8 * c, LEVELS, stride=2 * HEIGHT) for c in range(2)]


def load_row(ref, j):
    return jnp.concatenate([ref[at, :] for at in places(j)], axis=1)


def lanes(width):
    return lax.broadcasted_iota(jnp.int32, (LEVELS, width), 1)


def roll(x, by):
    return pltpu.roll(x, by % x.shape[-1], 1)


def pack_kernel(flags, temp, salt, u, v, diff, sx, sy, mu, mv, rows, odd_msg, even_msg):
    def one(j, _):
        def at(ref):
            return load_row(ref, j)

        wet_u, wet_v = at(mu).astype(F32), at(mv).astype(F32)
        r = at(diff)
        rows[0, j] = at(temp)
        rows[1, j] = at(salt)
        rows[2, j] = at(u) * wet_u
        rows[3, j] = r * wet_u
        rows[4, j] = at(sx)
        rows[5, j] = at(v) * wet_v
        rows[6, j] = r * wet_v
        rows[7, j] = at(sy)
        return 0

    lax.fori_loop(0, HEIGHT, one, 0, unroll=4)
    odd = flags[0]
    for f in range(8):
        n = rows_of(f)
        north = HEIGHT - n
        for k in range(n):
            odd_msg[slot(f, k)] = rows[f, odd * north + k]
            even_msg[slot(f, k)] = rows[f, (1 - odd) * north + k]


def mirrored(x):
    n = x.shape[-1] // 128
    back = 127 - lanes(128)
    parts = [x[:, 128 * i : 128 * (i + 1)] for i in range(n)]
    return jnp.concatenate([jnp.take_along_axis(p, back, axis=1) for p in reversed(parts)], axis=1)


def ghost_kernel(flags, rows, odd_msg, even_msg, ghost, odd_strip, even_strip):
    odd, top, lon_odd = flags[0], flags[1], flags[2]
    is_odd = odd == 1
    for f in range(8):
        n = rows_of(f)
        for k in range(n):
            a, b = odd_msg[slot(f, k)], even_msg[slot(f, k)]
            ghost[f, HALO - n + k] = jnp.where(is_odd, b, a)
            if k < n - (f >= 5):
                ghost[f, HALO + k] = jnp.where(is_odd, a, b)
        if f >= 5:
            ghost[f, 0] = rows[f, HEIGHT - 1]

    @pl.when(top == 1)
    def _():
        for f in range(8):
            n = rows_of(f)
            sign = -1.0 if f in (2, 4, 5, 7) else 1.0
            for k in range(n):
                x = mirrored(odd_msg[slot(f, n - 1 - k)]) * sign
                if f < 5:
                    ghost[f, HALO + k] = x
                elif k == 0:
                    ghost[f, 0] = x
                else:
                    ghost[f, HALO + k - 1] = x

    lane = lanes(128)
    swap = lon_odd == 1
    for r in range(EXT // 2):
        even_out = jnp.zeros((LEVELS, 128), F32)
        odd_out = jnp.zeros((LEVELS, 128), F32)
        for half in range(2):
            idx = r + half * (EXT // 2)
            for f in range(8):
                if idx < HALO:
                    x = ghost[f, idx]
                elif idx <= TOP:
                    x = rows[f, idx - HALO]
                else:
                    x = ghost[f, idx - HEIGHT]
                s = 8 * (f + 8 * half)
                west, east = roll(x[:, :128], s), roll(x[:, 128:], s + 8)
                here = (lane >= s) & (lane < s + 8)
                even_out = jnp.where(here, jnp.where(swap, west, east), even_out)
                odd_out = jnp.where(here, jnp.where(swap, east, west), odd_out)
        even_strip[r] = even_out
        odd_strip[r] = odd_out


def minmod(p, t):
    return jnp.maximum(jnp.minimum(p, t), jnp.minimum(jnp.maximum(p, t), 0.0))


def vertical(q):
    level = lax.broadcasted_iota(jnp.int32, q.shape, 0)
    e = jnp.where(level == 0, 0.0, q - pltpu.roll(q, 1, 0))
    return e + pltpu.roll(e, LEVELS - 1, 0)


def coefficients(c, r, s):
    plus, minus = jnp.maximum(c, 0.0), jnp.minimum(c, 0.0)
    return (
        plus + r,
        0.5 * plus * (1.0 - plus),
        0.25 * r * s,
        minus - r,
        -0.5 * minus * (1.0 + minus),
    )


def store_x(cx, idx, c, r, s):
    p, lp, t, e, ln = coefficients(c, r, s)
    for n, x in enumerate((p, lp, t, roll(e, 1), roll(ln, 1), roll(t, 1))):
        cx[n, idx] = x


def store_y(cy, idx, c, r, s):
    for n, x in enumerate(coefficients(c, r, s)):
        cy[n, idx] = x


def sweep(read, write, cx, cy, lo, hi, streams):
    def face(idx, q0, q1, m0, m1, g0, g1):
        return (
            cy[0, idx] * q0 + cy[3, idx] * q1 + (cy[1, idx] * m0 + cy[4, idx] * m1)
            + cy[2, idx] * (g0 + g1)
        )

    def row(idx, carry, seam=False):
        out = []
        for n in range(streams):
            q0, q1, d0, m0, g0, south = carry[n]
            q2 = read(n, idx + 2)
            d1 = q2 - q1
            m1 = minmod(d0, d1)
            g1 = vertical(q1)
            north = face(idx, q0, q1, m0, m1, g0, g1)
            d = roll(q0, -1) - q0
            m = minmod(d, roll(d, 1))
            a = cx[0, idx] * q0 + cx[1, idx] * m + cx[2, idx] * g0
            b = cx[3, idx] * q0 + cx[4, idx] * m + cx[5, idx] * g0
            write(n, idx, q0 + ((b - a) + (roll(a, 1) - roll(b, -1))) + (south - north))
            if seam:
                north = face(0, q0, q1, m0, m1, g0, g1)
            out.append((q1, q2, d1, m1, g1, north))
        return tuple(out)

    carry = []
    for n in range(streams):
        q = [read(n, lo - 2 + k) for k in range(4)]
        d = [q[k + 1] - q[k] for k in range(3)]
        m0, m1 = minmod(d[0], d[1]), minmod(d[1], d[2])
        g0, g1 = vertical(q[1]), vertical(q[2])
        carry.append((q[2], q[3], d[2], m1, g1, face(lo - 1, q[1], q[2], m0, m1, g0, g1)))
    carry = tuple(carry)
    if hi <= TOP:
        lax.fori_loop(lo, hi + 1, row, carry)
        return
    carry = lax.fori_loop(lo, TOP, row, carry)
    carry = row(TOP, carry, seam=True)
    lax.fori_loop(TOP + 1, hi + 1, row, carry)


def main_kernel(flags, rows, ghost, result, qa, qb, cx, cy):
    top = flags[1] == 1
    for n in TRACERS:
        for k in range(HALO):
            qa[n, k] = ghost[n, k]
            qa[n, TOP + 1 + k] = ghost[n, HALO + k]

        def copy(j, _):
            qa[n, HALO + j] = rows[n, j]
            return 0

        lax.fori_loop(0, HEIGHT, copy, 0, unroll=4)

    def faces(j, _):
        store_x(cx, HALO + j, *(rows[f, j] for f in XF))
        store_y(cy, HALO + j, *(rows[f, j] for f in YF))
        return 0

    lax.fori_loop(0, HEIGHT, faces, 0, unroll=2)

    def low(k, _):
        store_x(cx, k, *(ghost[f, k] for f in XF))
        return 0

    lax.fori_loop(2, HALO, low, 0)

    def high(k, _):
        x = [ghost[f, HALO + k] for f in XF]
        store_x(cx, TOP + 1 + k, *(jnp.where(top, roll(y, -1), y) for y in x))
        store_y(cy, TOP + 1 + k, *(ghost[f, HALO + k] for f in YF))
        return 0

    lax.fori_loop(0, HALO - 2, high, 0)

    def low_y(k, _):
        store_y(cy, k, *(ghost[f, k] for f in YF))
        return 0

    lax.fori_loop(0, HALO, low_y, 0)
    for step in range(STEPS):
        src, dst = (qa, qb) if step % 2 == 0 else (qb, qa)
        lo, hi = 2 * (step + 1), EXT - 1 - 2 * (step + 1)
        last = step == STEPS - 1

        def read(n, idx, src=src):
            return src[n, idx]

        def write(n, idx, x, dst=dst, last=last):
            if last:
                result[n, idx - HALO] = x
            else:
                dst[n, idx] = x

        sweep(read, write, cx, cy, lo, hi, 2)


def edge_kernel(flags, rows, ghost, odd_strip, even_strip, result, temp, salt, qa, qb, cx, cy):
    top, swap = flags[1] == 1, flags[2] == 1
    lane = lanes(128)
    first = lane < 64

    def within(lo, hi):
        return (lane >= lo) & (lane < hi)

    in_left, in_w, in_e, in_right = within(8, 16), within(16, 32), within(32, 48), within(48, 56)
    for idx in range(EXT):
        r, half = idx % (EXT // 2), idx // (EXT // 2)
        a, b = odd_strip[r], even_strip[r]
        left, right = jnp.where(swap, b, a), jnp.where(swap, a, b)
        base = []
        for f in range(8):
            if idx < HALO:
                x = ghost[f, idx]
            elif idx <= TOP:
                x = rows[f, idx - HALO]
            else:
                x = ghost[f, idx - HEIGHT]
            s = 8 * (f + 8 * half)
            y = jnp.where(in_w, roll(x[:, :128], 16), roll(x[:, 128:], 48))
            y = jnp.where(in_left, roll(left, 8 - s), y)
            y = jnp.where(in_right, roll(right, 48 - s), y)
            base.append(y)
        qa[0, idx] = jnp.where(first, base[0], roll(base[1], 64))

        def both(y):
            return jnp.where(first, y, roll(y, 64))

        if 2 <= idx < EXT - 2:
            x = [both(base[f]) for f in XF]
            if idx > TOP:
                x = [jnp.where(top, roll(y, -1), y) for y in x]
            store_x(cx, idx, *x)
        if idx < EXT - 2:
            store_y(cy, idx, *(both(base[f]) for f in YF))
    for step in range(STEPS):
        src, dst = (qa, qb) if step % 2 == 0 else (qb, qa)
        lo, hi = 2 * (step + 1), EXT - 1 - 2 * (step + 1)

        def read(n, idx, src=src):
            return src[n, idx]

        def write(n, idx, x, dst=dst):
            dst[n, idx] = x

        sweep(read, write, cx, cy, lo, hi, 1)

    def patch(j, _):
        e = qa[0, HALO + j]
        for n, out in enumerate((temp, salt)):
            x = result[n, j]
            w = jnp.where(lane < 8, roll(e, -16 - 64 * n), x[:, :128])
            z = jnp.where(lane >= 120, roll(e, 80 - 64 * n), x[:, 128:])
            for at, y in zip(places(j), (w, z)):
                out[at, :] = y
        return 0

    lax.fori_loop(0, HEIGHT, patch, 0, unroll=4)


def call(kernel, outs, args, scratch=()):
    return pl.pallas_call(
        kernel,
        out_shape=[jax.ShapeDtypeStruct(s, F32) for s in outs],
        in_specs=[SMEM] + [VMEM] * (len(args) - 1),
        out_specs=[VMEM] * len(outs),
        scratch_shapes=[pltpu.VMEM(s, F32) for s in scratch],
        compiler_params=PARAMS,
    )(*args)


def on_device(lon_count, lat_count, *args):
    lon, lat = lax.axis_index("lon"), lax.axis_index("lat")
    flags = jnp.stack([lat % 2, (lat == lat_count - 1).astype(jnp.int32), lon % 2])
    flat = [level_major(x) for x in args]

    def index(i, j):
        return i * lat_count + j

    lons, lats = range(lon_count), range(lat_count)
    lat_even = [(index(i, j), index(i, j ^ 1)) for i in lons for j in lats]
    lat_odd = [
        (index(i, j), index(lon_count - 1 - i, j) if j == lat_count - 1 else index(i, j + 1 if j % 2 else j - 1))
        for i in lons
        for j in lats
        if j > 0
    ]
    lon_even = [(i, i ^ 1) for i in lons]
    lon_odd = [(i, (i + 1 if i % 2 else i - 1) % lon_count) for i in lons]
    row = (LEVELS, WIDTH)
    rows, odd_msg, even_msg = call(
        pack_kernel, [(8, HEIGHT, *row), (MESSAGE, *row), (MESSAGE, *row)], [flags, *flat]
    )
    odd_in = lax.ppermute(odd_msg, ("lon", "lat"), lat_odd)
    even_in = lax.ppermute(even_msg, ("lon", "lat"), lat_even)
    strip = (EXT // 2, LEVELS, 128)
    ghost, odd_strip, even_strip = call(
        ghost_kernel, [(8, 2 * HALO, *row), strip, strip], [flags, rows, odd_in, even_in]
    )
    odd_strip = lax.ppermute(odd_strip, "lon", lon_odd)
    even_strip = lax.ppermute(even_strip, "lon", lon_even)
    state = (2, EXT, *row)
    (result,) = call(
        main_kernel,
        [(2, HEIGHT, *row)],
        [flags, rows, ghost],
        [state, state, (6, EXT, *row), (5, EXT, *row)],
    )
    tile = (LEVELS, 128)
    temp, salt = call(
        edge_kernel,
        [(2 * LEVELS * HEIGHT, 128)] * 2,
        [flags, rows, ghost, odd_strip, even_strip, result],
        [(1, EXT, *tile), (1, EXT, *tile), (6, EXT, *tile), (5, EXT, *tile)],
    )
    return from_level_major(temp), from_level_major(salt)


def solution(mesh):
    spec = P(None, "lat", "lon")
    return jax.shard_map(
        functools.partial(on_device, mesh.shape["lon"], mesh.shape["lat"]),
        mesh=mesh,
        in_specs=(spec,) * 9,
        out_specs=(spec, spec),
        check_vma=False,
    )
```

time: 218 us -> 125 us (0.57)
  the two profiles are of different devices: /device:TPU:66 before, /device:TPU:59 now
where the time goes in v1:
time: 125 us; the launch traced here: 124 us
  Pallas kernels  83.4 us (67%)
  starting transfers between devices  23.1 us (18%)
  waiting for transfers between devices  8.66 us (7%)
  local copies, waits for them, and re-layouts  8.55 us (7%)
    pallas_call x4, Pallas kernels, call(): pl.pallas_call(kernel, out_shape=[jax.ShapeDtypeStruct(s, F32) for s in o...  83.4 us
    ppermute x1, starting transfers between devices, on_device(): odd_in = lax.ppermute(odd_msg, ('lon', 'lat'), lat_odd)  12.2 us
    ppermute x1, waiting for transfers between devices, on_device(): odd_in = lax.ppermute(odd_msg, ('lon', 'lat'), lat_odd)  8.65 us
    unnamed x18, local copies, waits for them, and re-layouts  8.55 us
    ppermute x1, starting transfers between devices, on_device(): odd_strip = lax.ppermute(odd_strip, 'lon', lon_odd)  6.99 us
  transfers between devices with their start and end apart: 4, of which 1 were waited for; matrix products, arithmetic and copies ran while one was open for 0% of the time, Pallas kernels for 30%

profile of v1, /device:TPU:59, one launch (start us, length us, event | category | flops | bytes accessed | tf_op | source)
XLA Modules:
  0.0 124.5 jit_solution(2153300430189145457)
XLA Ops:
  0.6 0.1 pad_add_fusion.flags
  0.7 0.0 copy-start
  0.7 0.9 copy-done
  1.7 0.0 copy-start.1
  1.7 0.9 copy-done.1
  2.6 0.0 copy-start.2
  2.6 0.9 copy-done.2
  3.6 0.0 copy-start.3
  3.6 0.9 copy-done.3
  4.5 0.0 copy-start.4
  4.5 0.9 copy-done.4
  5.5 0.0 copy-start.5
  5.5 0.9 copy-done.5
  6.4 0.0 copy-start.6
  6.4 0.9 copy-done.6
  7.4 0.0 copy-start.7
  7.4 0.9 copy-done.7
  8.3 0.0 copy-start.8
  8.3 0.9 copy-done.8
  9.3 2.0 %shard_map.104 = (f32[8,32,8,256]{3,2,1,0:T(8,128)S(1)}, f32[55,8,256]{2,1,0:T(8,128)S(1)}, f32[55,8,256]{2,1,0:T(8,128)S(1)}) custom-call(s32[3]{0:T(128)S(1)} %pad_add_fusion.flags, f32[512,128]{1,0:T(8,128)S(1)} %bitcast.58, f32[512,128]{1,0:T(8,128)S(1)} %bitcast.59, f32[512,128]{1,0:T(8,128)S(1)} %bitcast.60, f32[512,128]{1,0:T(8,128)S(1)} %bitcast.61, ...), custom_call_target="tpu_custom_call" | custom-call | tf_op jit(solution)/shard_map/pallas_call | solution.py:343
  11.3 12.2 %collective-permute-start = (f32[55,8,256]{2,1,0:T(8,128)S(1)}, f32[55,8,256]{2,1,0:T(8,128)S(1)}, u32[]{:S(2)}, u32[]{:S(2)}) collective-permute-start(f32[55,8,256]{2,1,0:T(8,128)S(1)} %get-tuple-element.11), channel_id=1, source_target_pairs={{1,2},{2,1},{3,4},{4,3},{5,6},{6,5},{7,8},{8,7},{9,10},{10,9},{11,... | collective-permute-start | bytes 1351688 | tf_op jit(solution)/shard_map/ppermute | solution.py:375
  23.6 1.9 %collective-permute-start.1 = (f32[55,8,256]{2,1,0:T(8,128)S(1)}, f32[55,8,256]{2,1,0:T(8,128)S(1)}, u32[]{:S(2)}, u32[]{:S(2)}) collective-permute-start(f32[55,8,256]{2,1,0:T(8,128)S(1)} %get-tuple-element.12), channel_id=1, source_target_pairs={{0,1},{1,0},{2,3},{3,2},{4,5},{5,4},{6,7},{7,6},{8,9},{9,8},{10,11... | collective-permute-start | bytes 1351688 | tf_op jit(solution)/shard_map/ppermute | solution.py:376
  25.5 8.7 %collective-permute-done.odd_msg = f32[55,8,256]{2,1,0:T(8,128)S(1)} collective-permute-done((f32[55,8,256]{2,1,0:T(8,128)S(1)}, f32[55,8,256]{2,1,0:T(8,128)S(1)}, u32[]{:S(2)}, u32[]{:S(2)}) %collective-permute-start) | collective-permute-done | bytes 450592 | tf_op jit(solution)/shard_map/ppermute | solution.py:375
  34.2 0.0 collective-permute-done.1.even_msg
  34.2 1.6 %shard_map.105 = (f32[8,16,8,256]{3,2,1,0:T(8,128)S(1)}, f32[24,8,128]{2,1,0:T(8,128)S(1)}, f32[24,8,128]{2,1,0:T(8,128)S(1)}) custom-call(s32[3]{0:T(128)S(1)} %pad_add_fusion.flags, f32[8,32,8,256]{3,2,1,0:T(8,128)S(1)} %get-tuple-element.10.rows, f32[55,8,256]{2,1,0:T(8,128)S(1)} %collective-permute-done.odd_msg, ...), custom_call_target="tpu_custom_call" | custom-call | tf_op jit(solution)/shard_map/pallas_call | solution.py:343
  35.8 7.0 %collective-permute-start.2 = (f32[24,8,128]{2,1,0:T(8,128)S(1)}, f32[24,8,128]{2,1,0:T(8,128)S(1)}, u32[]{:S(2)}, u32[]{:S(2)}) collective-permute-start(f32[24,8,128]{2,1,0:T(8,128)S(1)} %get-tuple-element.14), channel_id=1, source_target_pairs={{0,480},{32,64},{64,32},{96,128},{128,96},{160,192},{192,160},{224... | collective-permute-start | bytes 294920 | tf_op jit(solution)/shard_map/ppermute | solution.py:381
  42.8 1.9 %collective-permute-start.3 = (f32[24,8,128]{2,1,0:T(8,128)S(1)}, f32[24,8,128]{2,1,0:T(8,128)S(1)}, u32[]{:S(2)}, u32[]{:S(2)}) collective-permute-start(f32[24,8,128]{2,1,0:T(8,128)S(1)} %get-tuple-element.15), channel_id=1, source_target_pairs={{0,32},{32,0},{64,96},{96,64},{128,160},{160,128},{192,224},{224,1... | collective-permute-start | bytes 294920 | tf_op jit(solution)/shard_map/ppermute | solution.py:382
  44.7 37.5 %shard_map.106.result = f32[2,32,8,256]{3,2,1,0:T(8,128)S(1)} custom-call(s32[3]{0:T(128)S(1)} %pad_add_fusion.flags, f32[8,32,8,256]{3,2,1,0:T(8,128)S(1)} %get-tuple-element.10.rows, f32[8,16,8,256]{3,2,1,0:T(8,128)S(1)} %get-tuple-element.13.ghost), custom_call_target="tpu_custom_call" | custom-call | tf_op jit(solution)/shard_map/pallas_call | solution.py:343
  82.2 0.0 collective-permute-done.2.odd_strip
  82.2 0.0 collective-permute-done.3.even_strip
  82.2 42.2 %shard_map.107 = (f32[512,128]{1,0:T(8,128)}, f32[512,128]{1,0:T(8,128)}) custom-call(s32[3]{0:T(128)S(1)} %pad_add_fusion.flags, f32[8,32,8,256]{3,2,1,0:T(8,128)S(1)} %get-tuple-element.10.rows, f32[8,16,8,256]{3,2,1,0:T(8,128)S(1)} %get-tuple-element.13.ghost, f32[24,8,128]{2,1,0:T(8,128)S(1)} %collective-permute-done.2.odd_strip, ...), custom_call_target="tpu_custom_call" | custom-call | tf_op jit(solution)/shard_map/pallas_call | solution.py:343
Async XLA Ops:
  0.7 1.0 copy-start
  1.7 0.9 copy-start.1
  2.6 0.9 copy-start.2
  3.6 0.9 copy-start.3
  4.5 0.9 copy-start.4
  5.5 0.9 copy-start.5
  6.4 0.9 copy-start.6
  7.4 0.9 copy-start.7
  8.3 0.9 copy-start.8
  11.3 22.8 %collective-permute-start = (f32[55,8,256]{2,1,0:T(8,128)S(1)}, f32[55,8,256]{2,1,0:T(8,128)S(1)}, u32[]{:S(2)}, u32[]{:S(2)}) collective-permute-start(f32[55,8,256]{2,1,0:T(8,128)S(1)} %get-tuple-element.11), channel_id=1, source_target_pairs={{1,2},{2,1},{3,4},{4,3},{5,6},{6,5},{7,8},{8,7},{9,10},{10,9},{11,... | collective-permute-start | bytes 1351688 | tf_op jit(solution)/shard_map/ppermute | solution.py:375
  23.6 10.6 %collective-permute-start.1 = (f32[55,8,256]{2,1,0:T(8,128)S(1)}, f32[55,8,256]{2,1,0:T(8,128)S(1)}, u32[]{:S(2)}, u32[]{:S(2)}) collective-permute-start(f32[55,8,256]{2,1,0:T(8,128)S(1)} %get-tuple-element.12), channel_id=1, source_target_pairs={{0,1},{1,0},{2,3},{3,2},{4,5},{5,4},{6,7},{7,6},{8,9},{9,8},{10,11... | collective-permute-start | bytes 1351688 | tf_op jit(solution)/shard_map/ppermute | solution.py:376
  35.8 46.5 %collective-permute-start.2 = (f32[24,8,128]{2,1,0:T(8,128)S(1)}, f32[24,8,128]{2,1,0:T(8,128)S(1)}, u32[]{:S(2)}, u32[]{:S(2)}) collective-permute-start(f32[24,8,128]{2,1,0:T(8,128)S(1)} %get-tuple-element.14), channel_id=1, source_target_pairs={{0,480},{32,64},{64,32},{96,128},{128,96},{160,192},{192,160},{224... | collective-permute-start | bytes 294920 | tf_op jit(solution)/shard_map/ppermute | solution.py:381
  42.8 39.5 %collective-permute-start.3 = (f32[24,8,128]{2,1,0:T(8,128)S(1)}, f32[24,8,128]{2,1,0:T(8,128)S(1)}, u32[]{:S(2)}, u32[]{:S(2)}) collective-permute-start(f32[24,8,128]{2,1,0:T(8,128)S(1)} %get-tuple-element.15), channel_id=1, source_target_pairs={{0,32},{32,0},{64,96},{96,64},{128,160},{160,128},{192,224},{224,1... | collective-permute-start | bytes 294920 | tf_op jit(solution)/shard_map/ppermute | solution.py:382

commit v2 on v1

v2 whole, which is shorter than its diff:
```python
import functools

import jax
import jax.numpy as jnp
from jax import lax
from jax.experimental import pallas as pl
from jax.experimental.pallas import tpu as pltpu
from jax.sharding import PartitionSpec as P

STEPS = 4
HALO = 2 * STEPS
LEVELS = 8
HEIGHT = 32
WIDTH = 256
EXT = HEIGHT + 2 * HALO
TOP = HALO + HEIGHT - 1
F32 = jnp.float32
VMEM = pl.BlockSpec(memory_space=pltpu.VMEM)
SMEM = pl.BlockSpec(memory_space=pltpu.SMEM)
PARAMS = pltpu.CompilerParams(vmem_limit_bytes=20 * 2**20)
COST = pl.CostEstimate(flops=50_000_000, bytes_accessed=8_000_000, transcendentals=0)

TRACERS, XF, YF = (0, 1), (2, 3, 4), (5, 6, 7)
MESSAGE = 2 * 8 + 3 * 6 + 3 * 7


def slot(field, k):
    if field < 2:
        return field * 8 + k
    if field < 5:
        return 16 + (field - 2) * 6 + k
    return 34 + (field - 5) * 7 + k


def rows_of(field):
    return 8 if field < 2 else 6 if field < 5 else 7


def level_major(x):
    x = x.reshape(LEVELS, HEIGHT // 8, 8, WIDTH // 128, 128)
    return x.transpose(0, 1, 3, 2, 4).reshape(-1, 128)


def from_level_major(x):
    x = x.reshape(LEVELS, HEIGHT // 8, WIDTH // 128, 8, 128)
    return x.transpose(0, 1, 3, 2, 4).reshape(LEVELS, HEIGHT, WIDTH)


def places(j):
    start = (j // 8) * 16 + j % 8
    return [pl.ds(start + 8 * c, LEVELS, stride=2 * HEIGHT) for c in range(2)]


def load_row(ref, j):
    return jnp.concatenate([ref[at, :] for at in places(j)], axis=1)


def lanes(width):
    return lax.broadcasted_iota(jnp.int32, (LEVELS, width), 1)


def roll(x, by):
    return pltpu.roll(x, by % x.shape[-1], 1)


def pack_kernel(flags, *refs):
    args, (rows, odd_msg, even_msg), held, sems = refs[:9], refs[9:12], refs[12:21], refs[21]
    copies = [pltpu.make_async_copy(x, y, sems.at[n]) for n, (x, y) in enumerate(zip(args, held))]
    for copy in copies:
        copy.start()
    for copy in copies:
        copy.wait()
    temp, salt, u, v, diff, sx, sy, mu, mv = held

    def one(j, _):
        wet_u, wet_v = load_row(mu, j).astype(F32), load_row(mv, j).astype(F32)
        r = load_row(diff, j)
        rows[0, j] = load_row(temp, j)
        rows[1, j] = load_row(salt, j)
        rows[2, j] = load_row(u, j) * wet_u
        rows[3, j] = r * wet_u
        rows[4, j] = load_row(sx, j)
        rows[5, j] = load_row(v, j) * wet_v
        rows[6, j] = r * wet_v
        rows[7, j] = load_row(sy, j)
        return 0

    lax.fori_loop(0, HEIGHT, one, 0, unroll=4)
    odd = flags[0]
    for f in range(8):
        n = rows_of(f)
        north = HEIGHT - n

        def two(k, _, f=f, north=north):
            odd_msg[slot(f, k)] = rows[f, odd * north + k]
            even_msg[slot(f, k)] = rows[f, (1 - odd) * north + k]
            return 0

        lax.fori_loop(0, n, two, 0, unroll=n)


def mirrored(x):
    n = x.shape[-1] // 128
    back = 127 - lanes(128)
    parts = [x[:, 128 * i : 128 * (i + 1)] for i in range(n)]
    return jnp.concatenate([jnp.take_along_axis(p, back, axis=1) for p in reversed(parts)], axis=1)


def ghost_kernel(flags, rows, odd_msg, even_msg, _, ghost, odd_strip, even_strip):
    odd, top, lon_odd = flags[0], flags[1], flags[2]
    is_odd = odd == 1
    for f in range(8):
        n = rows_of(f)
        for k in range(n):
            a, b = odd_msg[slot(f, k)], even_msg[slot(f, k)]
            ghost[f, HALO - n + k] = jnp.where(is_odd, b, a)
            if k < n - (f >= 5):
                ghost[f, HALO + k] = jnp.where(is_odd, a, b)
        if f >= 5:
            ghost[f, 0] = rows[f, HEIGHT - 1]

    @pl.when(top == 1)
    def _():
        for f in range(8):
            n = rows_of(f)
            sign = -1.0 if f in (2, 4, 5, 7) else 1.0
            for k in range(n):
                x = mirrored(odd_msg[slot(f, n - 1 - k)]) * sign
                if f < 5:
                    ghost[f, HALO + k] = x
                elif k == 0:
                    ghost[f, 0] = x
                else:
                    ghost[f, HALO + k - 1] = x

    lane = lanes(128)
    swap = lon_odd == 1
    for r in range(EXT // 2):
        even_out = jnp.zeros((LEVELS, 128), F32)
        odd_out = jnp.zeros((LEVELS, 128), F32)
        for half in range(2):
            idx = r + half * (EXT // 2)
            for f in range(8):
                if idx < HALO:
                    x = ghost[f, idx]
                elif idx <= TOP:
                    x = rows[f, idx - HALO]
                else:
                    x = ghost[f, idx - HEIGHT]
                s = 8 * (f + 8 * half)
                west, east = roll(x[:, :128], s), roll(x[:, 128:], s + 8)
                here = (lane >= s) & (lane < s + 8)
                even_out = jnp.where(here, jnp.where(swap, west, east), even_out)
                odd_out = jnp.where(here, jnp.where(swap, east, west), odd_out)
        even_strip[r] = even_out
        odd_strip[r] = odd_out


def minmod(p, t):
    return jnp.maximum(jnp.minimum(p, t), jnp.minimum(jnp.maximum(p, t), 0.0))


def vertical(q):
    level = lax.broadcasted_iota(jnp.int32, q.shape, 0)
    up = jnp.where(level == LEVELS - 1, q, pltpu.roll(q, LEVELS - 1, 0))
    down = jnp.where(level == 0, q, pltpu.roll(q, 1, 0))
    return up - down


def shifted(tiles, by):
    lane = lanes(128)
    rolled = [roll(t, by) for t in tiles]
    if len(tiles) == 1:
        return rolled
    seam = lane == (0 if by == 1 else 127)
    return [jnp.where(seam, rolled[1 - n], rolled[n]) for n in range(2)]


def coefficients(c, r, s):
    plus, minus = jnp.maximum(c, 0.0), jnp.minimum(c, 0.0)
    return (
        plus + r,
        0.5 * plus * (1.0 - plus),
        0.25 * r * s,
        minus - r,
        -0.5 * minus * (1.0 + minus),
    )


def store_x(cx, idx, c, r, s):
    p, lp, t, e, ln = coefficients(c, r, s)
    for n, x in enumerate((p, lp, t, roll(e, 1), roll(ln, 1), roll(t, 1))):
        cx[n, idx] = x


def store_y(cy, idx, c, r, s):
    for n, x in enumerate(coefficients(c, r, s)):
        cy[n, idx] = x


def sweep(read, write, cx, cy, first, count, streams, tiles, chunk, seam):
    every = [(n, t) for n in range(streams) for t in range(tiles)]

    def at(ref, n, idx, t):
        return ref[n, idx, :, 128 * t : 128 * (t + 1)]

    def face(idx, t, q0, q1, m0, m1, g0, g1):
        c = [at(cy, n, idx, t) for n in range(5)]
        return (c[0] * q0 + c[3] * q1) + (c[1] * m0 + c[4] * m1) + c[2] * (g0 + g1)

    def row(idx, carry):
        out = []
        for n in range(streams):
            q0 = [carry[n * tiles + t][0] for t in range(tiles)]
            d = [x - y for x, y in zip(shifted(q0, -1), q0)]
            m = [minmod(x, y) for x, y in zip(d, shifted(d, 1))]
            a, b = [], []
            for t in range(tiles):
                g0 = carry[n * tiles + t][4]
                c = [at(cx, k, idx, t) for k in range(6)]
                a.append(c[0] * q0[t] + c[1] * m[t] + c[2] * g0)
                b.append(c[3] * q0[t] + c[4] * m[t] + c[5] * g0)
            x = [(b[t] - a[t]) + (p - r) for t, (p, r) in enumerate(zip(shifted(a, 1), shifted(b, -1)))]
            for t in range(tiles):
                q0, q1, d0, m0, g0, south = carry[n * tiles + t]
                q2 = read(n, idx + 2, t)
                d1 = q2 - q1
                m1 = minmod(d0, d1)
                g1 = vertical(q1)
                north = face(idx, t, q0, q1, m0, m1, g0, g1)
                write(n, idx, t, q0 + x[t] + (south - north))
                if seam and idx == TOP:
                    north = face(0, t, q0, q1, m0, m1, g0, g1)
                out.append((q1, q2, d1, m1, g1, north))
        return tuple(out)

    carry = []
    for n, t in every:
        q = [read(n, first - 2 + k, t) for k in range(4)]
        d = [q[k + 1] - q[k] for k in range(3)]
        m0, m1 = minmod(d[0], d[1]), minmod(d[1], d[2])
        g0, g1 = vertical(q[1]), vertical(q[2])
        carry.append((q[2], q[3], d[2], m1, g1, face(first - 1, t, q[1], q[2], m0, m1, g0, g1)))

    def several(i, carry):
        for k in range(chunk):
            carry = row(first + i * chunk + k, carry)
        return carry

    if count == 1:
        several(0, tuple(carry))
    else:
        lax.fori_loop(0, count, several, tuple(carry))


def window(src, dst, cx, cy, first, count, streams, tiles, chunk, seam=False):
    def read(n, idx, t):
        return src[n, idx, :, 128 * t : 128 * (t + 1)]

    def write(n, idx, t, x):
        dst[n, idx, :, 128 * t : 128 * (t + 1)] = x

    sweep(read, write, cx, cy, first, count, streams, tiles, chunk, seam)


def inner_kernel(rows, s1, s2, s3, s4, s0, cx, cy):
    def own(j, _):
        for n in TRACERS:
            s0[n, HALO + j] = rows[n, j]
        store_x(cx, HALO + j, *(rows[f, j] for f in XF))
        store_y(cy, HALO + j, *(rows[f, j] for f in YF))
        return 0

    lax.fori_loop(0, HEIGHT, own, 0, unroll=4)
    for src, dst, first, count in ((s0, s1, 0, 4), (s1, s2, 4, 3), (s2, s3, 4, 3), (s3, s4, 8, 2)):
        window(src, dst, cx, cy, HALO + first, count, 2, 2, 8)


def edges_of(x, in_w):
    return jnp.where(in_w, roll(x[:, :128], 16), roll(x[:, 128:], 48))


def within(lo, hi):
    lane = lanes(128)
    return (lane >= lo) & (lane < hi)


def outer_kernel(flags, rows, ghost, i1, i2, i3, i4, result, base, s0, s1, s2, s3, s4, cx, cy):
    top = flags[1] == 1
    in_w = within(16, 32)

    def near(k, _):
        for f in range(8):
            base[f, HALO + k] = edges_of(rows[f, k], in_w)
        for start in (0, HEIGHT - HALO):
            j = start + k
            for n in TRACERS:
                s0[n, HALO + j] = rows[n, j]
            store_x(cx, HALO + j, *(rows[f, j] for f in XF))
            store_y(cy, HALO + j, *(rows[f, j] for f in YF))
        return 0

    lax.fori_loop(0, HALO, near, 0, unroll=2)
    store_y(cy, TOP - HALO, *(rows[f, HEIGHT - HALO - 1] for f in YF))

    def beyond(k, _):
        to = jnp.where(k < HALO, k, HEIGHT + k)
        for f in range(8):
            base[f, to] = edges_of(ghost[f, k], in_w)
        for n in TRACERS:
            s0[n, to] = ghost[n, k]
        x = [ghost[f, k] for f in XF]
        turn = top & (k >= HALO)
        store_x(cx, to, *(jnp.where(turn, roll(y, -1), y) for y in x))
        store_y(cy, to, *(ghost[f, k] for f in YF))
        return 0

    lax.fori_loop(0, 2 * HALO, beyond, 0, unroll=2)

    def rest(j, _):
        for f in range(8):
            base[f, HALO + j] = edges_of(rows[f, j], in_w)
        return 0

    lax.fori_loop(HALO, HEIGHT, rest, 0, unroll=4)
    states = (s0, s1, s2, s3, s4)
    inner = (None, i1, i2, i3, None)
    for step in range(1, STEPS + 1):
        src, dst = states[step - 1], states[step]
        if inner[step - 1] is not None:
            for n in TRACERS:
                for k in range(4):
                    low = 2 * step + HALO - 2 + k
                    high = EXT - 1 - low
                    src[n, low] = inner[step - 1][n, low]
                    src[n, high] = inner[step - 1][n, high]
        window(src, dst, cx, cy, 2 * step, 1, 2, 2, 8)
        window(src, dst, cx, cy, EXT - 8 - 2 * step, 1, 2, 2, 8, seam=step < STEPS)

    def out(j, _):
        for n in TRACERS:
            result[n, j] = s4[n, HALO + j]
            result[n, HEIGHT - HALO + j] = s4[n, HEIGHT + j]
            result[n, HALO + j] = i4[n, 2 * HALO + j]
            result[n, 2 * HALO + j] = i4[n, 3 * HALO + j]
        return 0

    lax.fori_loop(0, HALO, out, 0, unroll=2)


def edge_kernel(flags, base, odd_strip, even_strip, result, temp, salt, qa, qb, cx, cy):
    top, swap = flags[1] == 1, flags[2] == 1
    lane = lanes(128)
    first = lane < 64
    in_left, in_right = within(8, 16), within(48, 56)

    def both(y):
        return jnp.where(first, y, roll(y, 64))

    half_rows = EXT // 2

    def assemble(r, _):
        a, b = odd_strip[r], even_strip[r]
        left, right = jnp.where(swap, b, a), jnp.where(swap, a, b)
        for half in range(2):
            to = r + half * half_rows
            y = []
            for f in range(8):
                s = 8 * (f + 8 * half)
                x = jnp.where(in_left, roll(left, 8 - s), base[f, to])
                y.append(jnp.where(in_right, roll(right, 48 - s), x))
            qa[0, to] = jnp.where(first, y[0], roll(y[1], 64))
            x = [both(y[f]) for f in XF]
            if half == 1:
                turn = top & (to > TOP)
                x = [jnp.where(turn, roll(z, -1), z) for z in x]
            store_x(cx, to, *x)
            store_y(cy, to, *(both(y[f]) for f in YF))
        return 0

    lax.fori_loop(0, half_rows, assemble, 0, unroll=2)

    def two(_, c):
        for src, dst in ((qa, qb), (qb, qa)):
            window(src, dst, cx, cy, 2, 1, 1, 1, EXT - 4, seam=True)
        return c

    lax.fori_loop(0, STEPS // 2, two, 0)

    def patch(j, _):
        e = qa[0, HALO + j]
        for n, out in enumerate((temp, salt)):
            x = result[n, j]
            w = jnp.where(lane < 8, roll(e, -16 - 64 * n), x[:, :128])
            z = jnp.where(lane >= 120, roll(e, 80 - 64 * n), x[:, 128:])
            for at, y in zip(places(j), (w, z)):
                out[at, :] = y
        return 0

    lax.fori_loop(0, HEIGHT, patch, 0, unroll=4)


def call(kernel, outs, args, scratch=(), args_in=VMEM, flags=None):
    first = [] if flags is None else [flags]
    return pl.pallas_call(
        kernel,
        out_shape=[jax.ShapeDtypeStruct(s, F32) for s in outs],
        in_specs=[SMEM] * len(first) + [args_in] * len(args),
        out_specs=[VMEM] * len(outs),
        scratch_shapes=[pltpu.VMEM(s, F32) if isinstance(s, tuple) else s for s in scratch],
        compiler_params=PARAMS,
        cost_estimate=COST,
    )(*first, *args)


ROW = (LEVELS, WIDTH)
TILE = (LEVELS, 128)
STRIP = (EXT // 2, *TILE)
STATE = (2, EXT, *ROW)
FLAT = (2 * LEVELS * HEIGHT, 128)


def pack(flags, args):
    held = [pltpu.VMEM(FLAT, x.dtype) for x in args]
    return call(
        pack_kernel,
        [(8, HEIGHT, *ROW), (MESSAGE, *ROW), (MESSAGE, *ROW)],
        args,
        [*held, pltpu.SemaphoreType.DMA((9,))],
        pl.BlockSpec(memory_space=pltpu.HBM),
        flags,
    )


def inner(rows):
    return call(inner_kernel, [STATE] * 4, [rows], [STATE, (6, EXT, *ROW), (5, EXT, *ROW)])


def fill_ghost(flags, rows, odd_in, even_in, after):
    return call(ghost_kernel, [(8, 2 * HALO, *ROW), STRIP, STRIP], [rows, odd_in, even_in, after], flags=flags)


def outer(flags, rows, ghost, states):
    return call(
        outer_kernel,
        [(2, HEIGHT, *ROW), (8, EXT, *TILE)],
        [rows, ghost, *states],
        [STATE] * 5 + [(6, EXT, *ROW), (5, EXT, *ROW)],
        flags=flags,
    )


def edge(flags, base, odd_strip, even_strip, result):
    return call(
        edge_kernel,
        [FLAT] * 2,
        [base, odd_strip, even_strip, result],
        [(1, EXT, *TILE)] * 2 + [(6, EXT, *TILE), (5, EXT, *TILE)],
        flags=flags,
    )


def on_device(lon_count, lat_count, *args):
    lon, lat = lax.axis_index("lon"), lax.axis_index("lat")
    flags = jnp.stack([lat % 2, (lat == lat_count - 1).astype(jnp.int32), lon % 2])
    flat = [level_major(x) for x in args]

    def index(i, j):
        return i * lat_count + j

    lons, lats = range(lon_count), range(lat_count)
    lat_even = [(index(i, j), index(i, j ^ 1)) for i in lons for j in lats]
    lat_odd = [
        (index(i, j), index(lon_count - 1 - i, j) if j == lat_count - 1 else index(i, j + 1 if j % 2 else j - 1))
        for i in lons
        for j in lats
        if j > 0
    ]
    lon_even = [(i, i ^ 1) for i in lons]
    lon_odd = [(i, (i + 1 if i % 2 else i - 1) % lon_count) for i in lons]
    flat = [pltpu.with_memory_space_constraint(x, pltpu.HBM) for x in flat]
    rows, odd_msg, even_msg = pack(flags, flat)
    odd_in = lax.ppermute(odd_msg, ("lon", "lat"), lat_odd)
    even_in = lax.ppermute(even_msg, ("lon", "lat"), lat_even)
    states = inner(rows)
    ghost, odd_strip, even_strip = fill_ghost(flags, rows, odd_in, even_in, states[3])
    odd_strip = lax.ppermute(odd_strip, "lon", lon_odd)
    even_strip = lax.ppermute(even_strip, "lon", lon_even)
    result, base = outer(flags, rows, ghost, states)
    temp, salt = edge(flags, base, odd_strip, even_strip, result)
    return from_level_major(temp), from_level_major(salt)


def solution(mesh):
    spec = P(None, "lat", "lon")
    return jax.shard_map(
        functools.partial(on_device, mesh.shape["lon"], mesh.shape["lat"]),
        mesh=mesh,
        in_specs=(spec,) * 9,
        out_specs=(spec, spec),
        check_vma=False,
    )
```

time: 125 us -> 62.8 us (0.50)
  Pallas kernels: 83.4 us -> 34.7 us
  local copies, waits for them, and re-layouts: 8.55 us -> 0 us
  waiting for transfers between devices: 8.66 us -> 4.04 us
    pallas_call x4 -> x5, Pallas kernels: 83.4 us -> 34.7 us  [call(): pl.pallas_call(kernel, out_shape=[jax.ShapeDtypeStruct(s, F32) for s in o...]
    unnamed x18 -> x0, local copies, waits for them, and re-layouts: 8.55 us -> none
    ppermute x1, waiting for transfers between devices: 8.65 us -> 4.03 us  [on_device(): odd_in = lax.ppermute(odd_msg, ('lon', 'lat'), lat_odd)]
  transfers between devices with their start and end apart: 4 -> 4, of which waited for: 1 -> 1; matrix products, arithmetic and copies ran while one was open for 0% -> 0% of each run, Pallas kernels for 30% -> 34%
where the time goes in v2:
time: 62.8 us; the launch traced here: 62.6 us
  Pallas kernels  34.7 us (55%)
  starting transfers between devices  23.1 us (37%)
  waiting for transfers between devices  4.04 us (6%)
  between operations  0.73 us (1%)
    pallas_call x5, Pallas kernels, call(): pl.pallas_call(kernel, out_shape=[jax.ShapeDtypeStruct(s, F32) for s in o...  34.7 us
    ppermute x1, starting transfers between devices, on_device(): odd_in = lax.ppermute(odd_msg, ('lon', 'lat'), lat_odd)  12.2 us
    ppermute x1, starting transfers between devices, on_device(): odd_strip = lax.ppermute(odd_strip, 'lon', lon_odd)  6.99 us
    ppermute x1, waiting for transfers between devices, on_device(): odd_in = lax.ppermute(odd_msg, ('lon', 'lat'), lat_odd)  4.03 us
    ppermute x1, starting transfers between devices, on_device(): even_in = lax.ppermute(even_msg, ('lon', 'lat'), lat_even)  1.92 us
    ppermute x1, starting transfers between devices, on_device(): even_strip = lax.ppermute(even_strip, 'lon', lon_even)  1.92 us
  transfers between devices with their start and end apart: 4, of which 1 were waited for; matrix products, arithmetic and copies ran while one was open for 0% of the time, Pallas kernels for 34%

profile of v2, /device:TPU:59, one launch (start us, length us, event | category | flops | bytes accessed | tf_op | source)
XLA Modules:
  0.0 62.6 jit_solution(5929880618647013435)
XLA Ops:
  0.6 0.1 pad_add_fusion.flags
  0.7 3.7 %shard_map.104 = (f32[8,32,8,256]{3,2,1,0:T(8,128)S(1)}, f32[55,8,256]{2,1,0:T(8,128)S(1)}, f32[55,8,256]{2,1,0:T(8,128)S(1)}) custom-call(s32[3]{0:T(128)S(1)} %pad_add_fusion.flags, f32[512,128]{1,0:T(8,128)} %bitcast.58, f32[512,128]{1,0:T(8,128)} %bitcast.59, f32[512,128]{1,0:T(8,128)} %bitcast.60, f32[512,128]{1,0:T(8,128)} %bitcast.61, ...), custom_call_target="tpu_custom_call" | custom-call | flops 50000000 | bytes 8000000 | tf_op jit(solution)/shard_map/pallas_call | solution.py:405
  4.4 12.2 %collective-permute-start = (f32[55,8,256]{2,1,0:T(8,128)S(1)}, f32[55,8,256]{2,1,0:T(8,128)S(1)}, u32[]{:S(2)}, u32[]{:S(2)}) collective-permute-start(f32[55,8,256]{2,1,0:T(8,128)S(1)} %get-tuple-element.17), channel_id=1, source_target_pairs={{1,2},{2,1},{3,4},{4,3},{5,6},{6,5},{7,8},{8,7},{9,10},{10,9},{11,... | collective-permute-start | bytes 1351688 | tf_op jit(solution)/shard_map/ppermute | solution.py:483
  16.7 1.9 %collective-permute-start.1 = (f32[55,8,256]{2,1,0:T(8,128)S(1)}, f32[55,8,256]{2,1,0:T(8,128)S(1)}, u32[]{:S(2)}, u32[]{:S(2)}) collective-permute-start(f32[55,8,256]{2,1,0:T(8,128)S(1)} %get-tuple-element.18), channel_id=1, source_target_pairs={{0,1},{1,0},{2,3},{3,2},{4,5},{5,4},{6,7},{7,6},{8,9},{9,8},{10,11... | collective-permute-start | bytes 1351688 | tf_op jit(solution)/shard_map/ppermute | solution.py:484
  18.6 4.6 %shard_map.105 = (f32[2,48,8,256]{3,2,1,0:T(8,128)S(1)}, f32[2,48,8,256]{3,2,1,0:T(8,128)S(1)}, f32[2,48,8,256]{3,2,1,0:T(8,128)S(1)}, f32[2,48,8,256]{3,2,1,0:T(8,128)S(1)}) custom-call(f32[8,32,8,256]{3,2,1,0:T(8,128)S(1)} %get-tuple-element.16.rows), custom_call_target="tpu_custom_call" | custom-call | flops 50000000 | bytes 8000000 | tf_op jit(solution)/shard_map/pallas_call | solution.py:405
  23.2 4.0 %collective-permute-done.odd_msg = f32[55,8,256]{2,1,0:T(8,128)S(1)} collective-permute-done((f32[55,8,256]{2,1,0:T(8,128)S(1)}, f32[55,8,256]{2,1,0:T(8,128)S(1)}, u32[]{:S(2)}, u32[]{:S(2)}) %collective-permute-start) | collective-permute-done | bytes 450592 | tf_op jit(solution)/shard_map/ppermute | solution.py:483
  27.2 0.0 collective-permute-done.1.even_msg
  27.2 1.6 %shard_map.106 = (f32[8,16,8,256]{3,2,1,0:T(8,128)S(1)}, f32[24,8,128]{2,1,0:T(8,128)S(1)}, f32[24,8,128]{2,1,0:T(8,128)S(1)}) custom-call(s32[3]{0:T(128)S(1)} %pad_add_fusion.flags, f32[8,32,8,256]{3,2,1,0:T(8,128)S(1)} %get-tuple-element.16.rows, f32[55,8,256]{2,1,0:T(8,128)S(1)} %collective-permute-done.odd_msg, ...), custom_call_target="tpu_custom_call" | custom-call | flops 50000000 | bytes 8000000 | tf_op jit(solution)/shard_map/pallas_call | solution.py:405
  28.9 7.0 %collective-permute-start.2 = (f32[24,8,128]{2,1,0:T(8,128)S(1)}, f32[24,8,128]{2,1,0:T(8,128)S(1)}, u32[]{:S(2)}, u32[]{:S(2)}) collective-permute-start(f32[24,8,128]{2,1,0:T(8,128)S(1)} %get-tuple-element.25), channel_id=1, source_target_pairs={{0,480},{32,64},{64,32},{96,128},{128,96},{160,192},{192,160},{224... | collective-permute-start | bytes 294920 | tf_op jit(solution)/shard_map/ppermute | solution.py:487
  35.8 1.9 %collective-permute-start.3 = (f32[24,8,128]{2,1,0:T(8,128)S(1)}, f32[24,8,128]{2,1,0:T(8,128)S(1)}, u32[]{:S(2)}, u32[]{:S(2)}) collective-permute-start(f32[24,8,128]{2,1,0:T(8,128)S(1)} %get-tuple-element.26), channel_id=1, source_target_pairs={{0,32},{32,0},{64,96},{96,64},{128,160},{160,128},{192,224},{224,1... | collective-permute-start | bytes 294920 | tf_op jit(solution)/shard_map/ppermute | solution.py:488
  37.8 16.7 %shard_map.107 = (f32[2,32,8,256]{3,2,1,0:T(8,128)S(1)}, f32[8,48,8,128]{3,2,1,0:T(8,128)S(1)}) custom-call(s32[3]{0:T(128)S(1)} %pad_add_fusion.flags, f32[8,32,8,256]{3,2,1,0:T(8,128)S(1)} %get-tuple-element.16.rows, f32[8,16,8,256]{3,2,1,0:T(8,128)S(1)} %get-tuple-element.20.ghost, f32[2,48,8,256]{3,2,1,0:T(8,128)S(1)} %get-tuple-element.21.i1, ...), custom_call_target="tpu_custom_call" | custom-call | flops 50000000 | bytes 8000000 | tf_op jit(solution)/shard_map/pallas_call | solution.py:405
  54.5 0.0 collective-permute-done.2.odd_strip
  54.5 0.0 collective-permute-done.3.even_strip
  54.5 8.1 %shard_map.108 = (f32[512,128]{1,0:T(8,128)}, f32[512,128]{1,0:T(8,128)}) custom-call(s32[3]{0:T(128)S(1)} %pad_add_fusion.flags, f32[8,48,8,128]{3,2,1,0:T(8,128)S(1)} %get-tuple-element.24.base, f32[24,8,128]{2,1,0:T(8,128)S(1)} %collective-permute-done.2.odd_strip, f32[24,8,128]{2,1,0:T(8,128)S(1)} %collective-permute-done.3.even_strip, ...), custom_call_target="tpu_custom_call" | custom-call | flops 50000000 | bytes 8000000 | tf_op jit(solution)/shard_map/pallas_call | solution.py:405
Async XLA Ops:
  4.4 22.8 %collective-permute-start = (f32[55,8,256]{2,1,0:T(8,128)S(1)}, f32[55,8,256]{2,1,0:T(8,128)S(1)}, u32[]{:S(2)}, u32[]{:S(2)}) collective-permute-start(f32[55,8,256]{2,1,0:T(8,128)S(1)} %get-tuple-element.17), channel_id=1, source_target_pairs={{1,2},{2,1},{3,4},{4,3},{5,6},{6,5},{7,8},{8,7},{9,10},{10,9},{11,... | collective-permute-start | bytes 1351688 | tf_op jit(solution)/shard_map/ppermute | solution.py:483
  16.7 10.6 %collective-permute-start.1 = (f32[55,8,256]{2,1,0:T(8,128)S(1)}, f32[55,8,256]{2,1,0:T(8,128)S(1)}, u32[]{:S(2)}, u32[]{:S(2)}) collective-permute-start(f32[55,8,256]{2,1,0:T(8,128)S(1)} %get-tuple-element.18), channel_id=1, source_target_pairs={{0,1},{1,0},{2,3},{3,2},{4,5},{5,4},{6,7},{7,6},{8,9},{9,8},{10,11... | collective-permute-start | bytes 1351688 | tf_op jit(solution)/shard_map/ppermute | solution.py:484
  28.9 25.6 %collective-permute-start.2 = (f32[24,8,128]{2,1,0:T(8,128)S(1)}, f32[24,8,128]{2,1,0:T(8,128)S(1)}, u32[]{:S(2)}, u32[]{:S(2)}) collective-permute-start(f32[24,8,128]{2,1,0:T(8,128)S(1)} %get-tuple-element.25), channel_id=1, source_target_pairs={{0,480},{32,64},{64,32},{96,128},{128,96},{160,192},{192,160},{224... | collective-permute-start | bytes 294920 | tf_op jit(solution)/shard_map/ppermute | solution.py:487
  35.8 18.7 %collective-permute-start.3 = (f32[24,8,128]{2,1,0:T(8,128)S(1)}, f32[24,8,128]{2,1,0:T(8,128)S(1)}, u32[]{:S(2)}, u32[]{:S(2)}) collective-permute-start(f32[24,8,128]{2,1,0:T(8,128)S(1)} %get-tuple-element.26), channel_id=1, source_target_pairs={{0,32},{32,0},{64,96},{96,64},{128,160},{160,128},{192,224},{224,1... | collective-permute-start | bytes 294920 | tf_op jit(solution)/shard_map/ppermute | solution.py:488

commit v3 on v2

v3 whole, which is shorter than its diff:
```python
import functools

import jax
import jax.numpy as jnp
from jax import lax
from jax.experimental import pallas as pl
from jax.experimental.pallas import tpu as pltpu
from jax.sharding import PartitionSpec as P

STEPS = 4
HALO = 2 * STEPS
PAD = 4
LEVELS = 8
HEIGHT = 32
WIDTH = 256
EXT = HEIGHT + 2 * HALO
TOP = HALO + HEIGHT - 1
EDGE_DEPTH = EXT + 2 * PAD
F32 = jnp.float32
VMEM = pl.BlockSpec(memory_space=pltpu.VMEM)
SMEM = pl.BlockSpec(memory_space=pltpu.SMEM)
PARAMS = pltpu.CompilerParams(vmem_limit_bytes=20 * 2**20)
COST = pl.CostEstimate(flops=50_000_000, bytes_accessed=8_000_000, transcendentals=0)

TRACERS, XF, YF = (0, 1), (2, 3, 4), (5, 6, 7)
MESSAGE = 2 * 8 + 3 * 6 + 3 * 7


def slot(field, k):
    if field < 2:
        return field * 8 + k
    if field < 5:
        return 16 + (field - 2) * 6 + k
    return 34 + (field - 5) * 7 + k


def rows_of(field):
    return 8 if field < 2 else 6 if field < 5 else 7


def level_major(x):
    x = x.reshape(LEVELS, HEIGHT // 8, 8, WIDTH // 128, 128)
    return x.transpose(0, 1, 3, 2, 4).reshape(-1, 128)


def from_level_major(x):
    x = x.reshape(LEVELS, HEIGHT // 8, WIDTH // 128, 8, 128)
    return x.transpose(0, 1, 3, 2, 4).reshape(LEVELS, HEIGHT, WIDTH)


def places(j):
    start = (j // 8) * 16 + j % 8
    return [pl.ds(start + 8 * c, LEVELS, stride=2 * HEIGHT) for c in range(2)]


def load_row(ref, j):
    return jnp.concatenate([ref[at, :] for at in places(j)], axis=1)


def lanes(width):
    return lax.broadcasted_iota(jnp.int32, (LEVELS, width), 1)


def within(lo, hi):
    lane = lanes(128)
    return (lane >= lo) & (lane < hi)


def roll(x, by):
    return pltpu.roll(x, by % x.shape[-1], 1)


def pack_kernel(flags, *refs):
    args, (rows, odd_msg, even_msg), held, sems = refs[:9], refs[9:12], refs[12:21], refs[21]
    copies = [pltpu.make_async_copy(x, y, sems.at[n]) for n, (x, y) in enumerate(zip(args, held))]
    for copy in copies:
        copy.start()
    for copy in copies:
        copy.wait()
    temp, salt, u, v, diff, sx, sy, mu, mv = held

    def one(j, _):
        wet_u, wet_v = load_row(mu, j).astype(F32), load_row(mv, j).astype(F32)
        r = load_row(diff, j)
        rows[0, j] = load_row(temp, j)
        rows[1, j] = load_row(salt, j)
        rows[2, j] = load_row(u, j) * wet_u
        rows[3, j] = r * wet_u
        rows[4, j] = load_row(sx, j)
        rows[5, j] = load_row(v, j) * wet_v
        rows[6, j] = r * wet_v
        rows[7, j] = load_row(sy, j)
        return 0

    lax.fori_loop(0, HEIGHT, one, 0, unroll=4)
    odd = flags[0]
    for f in range(8):
        n = rows_of(f)
        north = HEIGHT - n

        def two(k, _, f=f, north=north):
            odd_msg[slot(f, k)] = rows[f, odd * north + k]
            even_msg[slot(f, k)] = rows[f, (1 - odd) * north + k]
            return 0

        lax.fori_loop(0, n, two, 0, unroll=n)


def mirrored(x):
    n = x.shape[-1] // 128
    back = 127 - lanes(128)
    parts = [x[:, 128 * i : 128 * (i + 1)] for i in range(n)]
    return jnp.concatenate([jnp.take_along_axis(p, back, axis=1) for p in reversed(parts)], axis=1)


def ghost_kernel(flags, rows, odd_msg, even_msg, _, ghost, odd_strip, even_strip):
    odd, top, lon_odd = flags[0], flags[1], flags[2]
    is_odd = odd == 1
    for f in range(8):
        n = rows_of(f)
        for k in range(n):
            a, b = odd_msg[slot(f, k)], even_msg[slot(f, k)]
            ghost[f, HALO - n + k] = jnp.where(is_odd, b, a)
            if k < n - (f >= 5):
                ghost[f, HALO + k] = jnp.where(is_odd, a, b)
        if f >= 5:
            ghost[f, 0] = rows[f, HEIGHT - 1]

    @pl.when(top == 1)
    def _():
        for f in range(8):
            n = rows_of(f)
            sign = -1.0 if f in (2, 4, 5, 7) else 1.0
            for k in range(n):
                x = mirrored(odd_msg[slot(f, n - 1 - k)]) * sign
                if f < 5:
                    ghost[f, HALO + k] = x
                elif k == 0:
                    ghost[f, 0] = x
                else:
                    ghost[f, HALO + k - 1] = x

    swap = lon_odd == 1
    for r in range(EXT // 2):
        east, west = jnp.zeros((LEVELS, 128), F32), jnp.zeros((LEVELS, 128), F32)
        for half in range(2):
            idx = r + half * (EXT // 2)
            for f in range(8):
                if idx < HALO:
                    x = ghost[f, idx]
                elif idx <= TOP:
                    x = rows[f, idx - HALO]
                else:
                    x = ghost[f, idx - HEIGHT]
                to = 8 * f + 64 * half
                east = jnp.where(within(to, to + 8), roll(x[:, 128:], to + 8), east)
                to = 8 * f + 64 * (1 - half)
                west = jnp.where(within(to, to + 8), roll(x[:, :128], to), west)
        even_strip[r] = jnp.where(swap, west, east)
        odd_strip[r] = jnp.where(swap, east, west)


def minmod(p, t):
    return jnp.maximum(jnp.minimum(p, t), jnp.minimum(jnp.maximum(p, t), 0.0))


def vertical(q):
    level = lax.broadcasted_iota(jnp.int32, q.shape, 0)
    up = jnp.where(level == LEVELS - 1, q, pltpu.roll(q, LEVELS - 1, 0))
    down = jnp.where(level == 0, q, pltpu.roll(q, 1, 0))
    return up - down


def shifted(tiles, by):
    lane = lanes(128)
    rolled = [roll(t, by) for t in tiles]
    if len(tiles) == 1:
        return rolled
    seam = lane == (0 if by == 1 else 127)
    return [jnp.where(seam, rolled[1 - n], rolled[n]) for n in range(2)]


def coefficients(c, r, s):
    plus, minus = jnp.maximum(c, 0.0), jnp.minimum(c, 0.0)
    return (
        plus + r,
        0.5 * plus * (1.0 - plus),
        0.25 * r * s,
        minus - r,
        -0.5 * minus * (1.0 + minus),
    )


def store_x(cx, idx, c, r, s):
    p, lp, t, e, ln = coefficients(c, r, s)
    for n, x in enumerate((p, lp, t, roll(e, 1), roll(ln, 1), roll(t, 1))):
        cx[n, idx] = x


def store_y(cy, idx, c, r, s):
    for n, x in enumerate(coefficients(c, r, s)):
        cy[n, idx] = x


def rows_forward(src, dst, cx, cy, first, chunk, streams, tiles, seam=False, pad=0):
    def at(ref, n, idx, t):
        return ref[n, pad + idx, :, 128 * t : 128 * (t + 1)]

    def face(idx, t, q0, q1, m0, m1, g0, g1):
        c = [at(cy, n, idx, t) for n in range(5)]
        return (c[0] * q0 + c[3] * q1) + (c[1] * m0 + c[4] * m1) + c[2] * (g0 + g1)

    south = jnp.where(first == TOP + 1, 0, first - 1)
    carry = []
    for n in range(streams):
        for t in range(tiles):
            q = [at(src, n, first - 2 + k, t) for k in range(4)]
            d = [q[k + 1] - q[k] for k in range(3)]
            m0, m1 = minmod(d[0], d[1]), minmod(d[1], d[2])
            g0, g1 = vertical(q[1]), vertical(q[2])
            carry.append((q[2], q[3], d[2], m1, g1, face(south, t, q[1], q[2], m0, m1, g0, g1)))
    for k in range(chunk):
        idx = first + k
        out = []
        for n in range(streams):
            q0 = [carry[n * tiles + t][0] for t in range(tiles)]
            d = [x - y for x, y in zip(shifted(q0, -1), q0)]
            m = [minmod(x, y) for x, y in zip(d, shifted(d, 1))]
            a, b = [], []
            for t in range(tiles):
                g0 = carry[n * tiles + t][4]
                c = [at(cx, i, idx, t) for i in range(6)]
                a.append(c[0] * q0[t] + c[1] * m[t] + c[2] * g0)
                b.append(c[3] * q0[t] + c[4] * m[t] + c[5] * g0)
            x = [(b[t] - a[t]) + (p - r) for t, (p, r) in enumerate(zip(shifted(a, 1), shifted(b, -1)))]
            for t in range(tiles):
                q0, q1, d0, m0, g0, south = carry[n * tiles + t]
                q2 = at(src, n, idx + 2, t)
                d1 = q2 - q1
                m1 = minmod(d0, d1)
                g1 = vertical(q1)
                north = face(idx, t, q0, q1, m0, m1, g0, g1)
                dst[n, pad + idx, :, 128 * t : 128 * (t + 1)] = q0 + x[t] + (south - north)
                if isinstance(idx, int):
                    if idx == TOP and seam:
                        north = face(0, t, q0, q1, m0, m1, g0, g1)
                elif seam and k % 2 == 1 and k < chunk - 1:
                    at_seam = jnp.full((LEVELS, 128), idx, jnp.int32) == TOP
                    north = jnp.where(at_seam, face(0, t, q0, q1, m0, m1, g0, g1), north)
                out.append((q1, q2, d1, m1, g1, north))
        carry = out


def loop(count, body, unroll=1):
    def step(i, _):
        body(i)
        return 0

    lax.fori_loop(0, count, step, 0, unroll=unroll)


SALT = 24


def edges_of(x):
    return jnp.where(within(16, 32), roll(x[:, :128], 16), roll(x[:, 128:], 72))


def inner_kernel(rows, cuts, mid, base, s0, s1, s2, s3, s4, cx, cy):
    def own(j):
        for n in TRACERS:
            s0[n, HALO + j] = rows[n, j]
        x = [rows[f, j] for f in range(8)]
        store_x(cx, HALO + j, *(x[f] for f in XF))
        store_y(cy, HALO + j, *(x[f] for f in YF))
        for f in range(8):
            base[f, j] = edges_of(x[f])

    loop(HEIGHT, own, 4)
    for src, dst, first, count in ((s0, s1, 0, 4), (s1, s2, 4, 3), (s2, s3, 4, 3), (s3, s4, 8, 2)):
        loop(count, lambda i: rows_forward(src, dst, cx, cy, HALO + first + 8 * i, 8, 2, 2))
    for n in TRACERS:
        for step, s in enumerate((s1, s2, s3), 1):
            low = HALO + 2 * step
            for k in range(4):
                cuts[step - 1, n, k] = s[n, low + k]
                cuts[step - 1, n, 4 + k] = s[n, EXT - 4 - low + k]

        def out(j, n=n):
            mid[n, j] = s4[n, 2 * HALO + j]

        loop(2 * HALO, out, 4)


def outer_kernel(flags, rows, ghost, cuts, mid, result, base, qa, qb, cx, cy):
    top = flags[1] == 1

    def near(k):
        for start in (0, HEIGHT - HALO):
            j = start + k
            for n in TRACERS:
                qa[n, HALO + j] = rows[n, j]
            store_x(cx, HALO + j, *(rows[f, j] for f in XF))
            store_y(cy, HALO + j, *(rows[f, j] for f in YF))

    loop(HALO, near, 4)
    store_y(cy, TOP - HALO, *(rows[f, HEIGHT - HALO - 1] for f in YF))

    def beyond(k):
        to = jnp.where(k < HALO, k, HEIGHT + k)
        x = [ghost[f, k] for f in range(8)]
        for f in range(8):
            base[f, k] = edges_of(x[f])
        for n in TRACERS:
            qa[n, to] = x[n]
        turn = top & (k >= HALO)
        store_x(cx, to, *(jnp.where(turn, roll(x[f], -1), x[f]) for f in XF))
        store_y(cy, to, *(x[f] for f in YF))

    loop(2 * HALO, beyond, 4)

    def one(src, dst, step):
        low = HALO + 2 * step
        for n in TRACERS:
            for k in range(4):
                dst[n, low + k] = cuts[step - 1, n, k]
                dst[n, EXT - 4 - low + k] = cuts[step - 1, n, 4 + k]
        loop(2, lambda w: rows_forward(src, dst, cx, cy, 2 * step + w * (EXT - 8 - 4 * step), 8, 2, 2, seam=True))

    def two(i):
        one(qa, qb, 2 * i + 1)
        one(qb, qa, 2 * i + 2)

    loop(STEPS // 2, two)

    def out(j):
        for n in TRACERS:
            result[n, j] = qa[n, HALO + j]
            result[n, HEIGHT - HALO + j] = qa[n, HEIGHT + j]
            result[n, HALO + j] = mid[n, j]
            result[n, 2 * HALO + j] = mid[n, HALO + j]

    loop(HALO, out, 2)


def edge_kernel(flags, base, beyond, odd_strip, even_strip, result, temp, salt, qa, qb, cx, cy):
    top = flags[1] == 1
    lane = lanes(128)
    from_odd = (lane < 64).astype(jnp.int32) != flags[2]
    is_temp = within(8, 32) | within(56, 80)
    beside = within(8, 16) | within(72, 80)

    def both(y):
        return jnp.where(is_temp, y, roll(y, SALT))

    def assemble(ref, k, r, half, turn=None):
        a, b = odd_strip[r], even_strip[r]
        halo = jnp.where(from_odd, a, b) if half == 0 else jnp.where(from_odd, b, a)
        y = [jnp.where(beside, roll(halo, 8 - 8 * f - 64 * half), ref[f, k]) for f in range(8)]
        to = PAD + r + half * (EXT // 2)
        qa[0, to] = jnp.where(is_temp, y[0], roll(y[1], SALT))
        x = [both(y[f]) for f in XF]
        if turn is not None:
            x = [jnp.where(turn, roll(z, -1), z) for z in x]
        store_x(cx, to, *x)
        store_y(cy, to, *(both(y[f]) for f in YF))

    def ghosts(k):
        assemble(beyond, k, k, 0)
        assemble(beyond, HALO + k, 2 * HALO + k, 1, top)

    loop(HALO, ghosts, 4)

    def own(k):
        assemble(base, k, HALO + k, 0)
        assemble(base, 2 * HALO + k, k, 1)

    loop(2 * HALO, own, 4)

    def two(_):
        for src, dst in ((qa, qb), (qb, qa)):
            rows_forward(src, dst, cx, cy, 2, EXT - 4, 1, 1, seam=True, pad=PAD)

    loop(STEPS // 2, two)

    def patch(j):
        e = qa[0, PAD + HALO + j]
        for n, out in enumerate((temp, salt)):
            x = result[n, j]
            w = jnp.where(lane < 8, roll(e, -16 - SALT * n), x[:, :128])
            z = jnp.where(lane >= 120, roll(e, 56 - SALT * n), x[:, 128:])
            for at, y in zip(places(j), (w, z)):
                out[at, :] = y

    loop(HEIGHT, patch, 8)


def call(kernel, outs, args, scratch=(), args_in=VMEM, flags=None):
    first = [] if flags is None else [flags]
    return pl.pallas_call(
        kernel,
        out_shape=[jax.ShapeDtypeStruct(s, F32) for s in outs],
        in_specs=[SMEM] * len(first) + [args_in] * len(args),
        out_specs=[VMEM] * len(outs),
        scratch_shapes=[pltpu.VMEM(s, F32) if isinstance(s, tuple) else s for s in scratch],
        compiler_params=PARAMS,
        cost_estimate=COST,
    )(*first, *args)


ROW = (LEVELS, WIDTH)
TILE = (LEVELS, 128)
STRIP = (EXT // 2, *TILE)
STATE = (2, EXT, *ROW)
FLAT = (2 * LEVELS * HEIGHT, 128)


def pack(flags, args):
    held = [pltpu.VMEM(FLAT, x.dtype) for x in args]
    return call(
        pack_kernel,
        [(8, HEIGHT, *ROW), (MESSAGE, *ROW), (MESSAGE, *ROW)],
        args,
        [*held, pltpu.SemaphoreType.DMA((9,))],
        pl.BlockSpec(memory_space=pltpu.HBM),
        flags,
    )


def inner(rows):
    return call(
        inner_kernel,
        [(STEPS, 2, 8, *ROW), (2, 2 * HALO, *ROW), (8, HEIGHT, *TILE)],
        [rows],
        [STATE] * 5 + [(6, EXT, *ROW), (5, EXT, *ROW)],
    )


def fill_ghost(flags, rows, odd_in, even_in, after):
    return call(
        ghost_kernel, [(8, 2 * HALO, *ROW), STRIP, STRIP], [rows, odd_in, even_in, after], flags=flags
    )


def outer(flags, rows, ghost, cuts, mid):
    return call(
        outer_kernel,
        [(2, HEIGHT, *ROW), (8, 2 * HALO, *TILE)],
        [rows, ghost, cuts, mid],
        [STATE] * 2 + [(6, EXT, *ROW), (5, EXT, *ROW)],
        flags=flags,
    )


def edge(flags, base, beyond, odd_strip, even_strip, result):
    return call(
        edge_kernel,
        [FLAT] * 2,
        [base, beyond, odd_strip, even_strip, result],
        [(1, EDGE_DEPTH, *TILE)] * 2 + [(6, EDGE_DEPTH, *TILE), (5, EDGE_DEPTH, *TILE)],
        flags=flags,
    )


def on_device(lon_count, lat_count, *args):
    lon, lat = lax.axis_index("lon"), lax.axis_index("lat")
    flags = jnp.stack([lat % 2, (lat == lat_count - 1).astype(jnp.int32), lon % 2])
    flat = [level_major(x) for x in args]

    def index(i, j):
        return i * lat_count + j

    lons, lats = range(lon_count), range(lat_count)
    lat_even = [(index(i, j), index(i, j ^ 1)) for i in lons for j in lats]
    lat_odd = [
        (index(i, j), index(lon_count - 1 - i, j) if j == lat_count - 1 else index(i, j + 1 if j % 2 else j - 1))
        for i in lons
        for j in lats
        if j > 0
    ]
    lon_even = [(i, i ^ 1) for i in lons]
    lon_odd = [(i, (i + 1 if i % 2 else i - 1) % lon_count) for i in lons]
    flat = [pltpu.with_memory_space_constraint(x, pltpu.HBM) for x in flat]
    rows, odd_msg, even_msg = pack(flags, flat)
    odd_in = lax.ppermute(odd_msg, ("lon", "lat"), lat_odd)
    even_in = lax.ppermute(even_msg, ("lon", "lat"), lat_even)
    cuts, mid, base = inner(rows)
    ghost, odd_strip, even_strip = fill_ghost(flags, rows, odd_in, even_in, mid)
    odd_strip = lax.ppermute(odd_strip, "lon", lon_odd)
    even_strip = lax.ppermute(even_strip, "lon", lon_even)
    result, beyond = outer(flags, rows, ghost, cuts, mid)
    temp, salt = edge(flags, base, beyond, odd_strip, even_strip, result)
    return from_level_major(temp), from_level_major(salt)


def solution(mesh):
    spec = P(None, "lat", "lon")
    return jax.shard_map(
        functools.partial(on_device, mesh.shape["lon"], mesh.shape["lat"]),
        mesh=mesh,
        in_specs=(spec,) * 9,
        out_specs=(spec, spec),
        check_vma=False,
    )
```

time: 62.8 us -> 48.8 us (0.78)
  Pallas kernels: 34.7 us -> 21.3 us
    pallas_call x5, Pallas kernels: 34.7 us -> 21.3 us  [call(): pl.pallas_call(kernel, out_shape=[jax.ShapeDtypeStruct(s, F32) for s in o...]
  transfers between devices with their start and end apart: 4 -> 4, of which waited for: 1 -> 1; matrix products, arithmetic and copies ran while one was open for 0% -> 0% of each run, Pallas kernels for 34% -> 20%
where the time goes in v3:
time: 48.8 us; the launch traced here: 48.6 us
  starting transfers between devices  23.1 us (47%)
  Pallas kernels  21.3 us (44%)
  waiting for transfers between devices  3.45 us (7%)
  between operations  0.73 us (1%)
    pallas_call x5, Pallas kernels, call(): pl.pallas_call(kernel, out_shape=[jax.ShapeDtypeStruct(s, F32) for s in o...  21.3 us
    ppermute x1, starting transfers between devices, on_device(): odd_in = lax.ppermute(odd_msg, ('lon', 'lat'), lat_odd)  12.2 us
    ppermute x1, starting transfers between devices, on_device(): odd_strip = lax.ppermute(odd_strip, 'lon', lon_odd)  6.99 us
    ppermute x1, waiting for transfers between devices, on_device(): odd_in = lax.ppermute(odd_msg, ('lon', 'lat'), lat_odd)  3.44 us
    ppermute x1, starting transfers between devices, on_device(): even_in = lax.ppermute(even_msg, ('lon', 'lat'), lat_even)  1.92 us
    ppermute x1, starting transfers between devices, on_device(): even_strip = lax.ppermute(even_strip, 'lon', lon_even)  1.92 us
  transfers between devices with their start and end apart: 4, of which 1 were waited for; matrix products, arithmetic and copies ran while one was open for 0% of the time, Pallas kernels for 20%

profile of v3, /device:TPU:59, one launch (start us, length us, event | category | flops | bytes accessed | tf_op | source)
XLA Modules:
  0.0 48.6 jit_solution(8088572445034625315)
XLA Ops:
  0.6 0.1 pad_add_fusion.flags
  0.7 3.7 %shard_map.104 = (f32[8,32,8,256]{3,2,1,0:T(8,128)S(1)}, f32[55,8,256]{2,1,0:T(8,128)S(1)}, f32[55,8,256]{2,1,0:T(8,128)S(1)}) custom-call(s32[3]{0:T(128)S(1)} %pad_add_fusion.flags, f32[512,128]{1,0:T(8,128)} %bitcast.58, f32[512,128]{1,0:T(8,128)} %bitcast.59, f32[512,128]{1,0:T(8,128)} %bitcast.60, f32[512,128]{1,0:T(8,128)} %bitcast.61, ...), custom_call_target="tpu_custom_call" | custom-call | flops 50000000 | bytes 8000000 | tf_op jit(solution)/shard_map/pallas_call | solution.py:400
  4.4 12.2 %collective-permute-start = (f32[55,8,256]{2,1,0:T(8,128)S(1)}, f32[55,8,256]{2,1,0:T(8,128)S(1)}, u32[]{:S(2)}, u32[]{:S(2)}) collective-permute-start(f32[55,8,256]{2,1,0:T(8,128)S(1)} %get-tuple-element.17), channel_id=1, source_target_pairs={{1,2},{2,1},{3,4},{4,3},{5,6},{6,5},{7,8},{8,7},{9,10},{10,9},{11,... | collective-permute-start | bytes 1351688 | tf_op jit(solution)/shard_map/ppermute | solution.py:485
  16.7 1.9 %collective-permute-start.1 = (f32[55,8,256]{2,1,0:T(8,128)S(1)}, f32[55,8,256]{2,1,0:T(8,128)S(1)}, u32[]{:S(2)}, u32[]{:S(2)}) collective-permute-start(f32[55,8,256]{2,1,0:T(8,128)S(1)} %get-tuple-element.18), channel_id=1, source_target_pairs={{0,1},{1,0},{2,3},{3,2},{4,5},{5,4},{6,7},{7,6},{8,9},{9,8},{10,11... | collective-permute-start | bytes 1351688 | tf_op jit(solution)/shard_map/ppermute | solution.py:486
  18.6 5.2 %shard_map.105 = (f32[4,2,8,8,256]{4,3,2,1,0:T(8,128)S(1)}, f32[2,16,8,256]{3,2,1,0:T(8,128)S(1)}, f32[8,32,8,128]{3,2,1,0:T(8,128)S(1)}) custom-call(f32[8,32,8,256]{3,2,1,0:T(8,128)S(1)} %get-tuple-element.15.rows), custom_call_target="tpu_custom_call" | custom-call | flops 50000000 | bytes 8000000 | tf_op jit(solution)/shard_map/pallas_call | solution.py:400
  23.8 3.4 %collective-permute-done.odd_msg = f32[55,8,256]{2,1,0:T(8,128)S(1)} collective-permute-done((f32[55,8,256]{2,1,0:T(8,128)S(1)}, f32[55,8,256]{2,1,0:T(8,128)S(1)}, u32[]{:S(2)}, u32[]{:S(2)}) %collective-permute-start) | collective-permute-done | bytes 450592 | tf_op jit(solution)/shard_map/ppermute | solution.py:485
  27.2 0.0 collective-permute-done.1.even_msg
  27.2 1.6 %shard_map.106 = (f32[8,16,8,256]{3,2,1,0:T(8,128)S(1)}, f32[24,8,128]{2,1,0:T(8,128)S(1)}, f32[24,8,128]{2,1,0:T(8,128)S(1)}) custom-call(s32[3]{0:T(128)S(1)} %pad_add_fusion.flags, f32[8,32,8,256]{3,2,1,0:T(8,128)S(1)} %get-tuple-element.15.rows, f32[55,8,256]{2,1,0:T(8,128)S(1)} %collective-permute-done.odd_msg, ...), custom_call_target="tpu_custom_call" | custom-call | flops 50000000 | bytes 8000000 | tf_op jit(solution)/shard_map/pallas_call | solution.py:400
  28.9 7.0 %collective-permute-start.2 = (f32[24,8,128]{2,1,0:T(8,128)S(1)}, f32[24,8,128]{2,1,0:T(8,128)S(1)}, u32[]{:S(2)}, u32[]{:S(2)}) collective-permute-start(f32[24,8,128]{2,1,0:T(8,128)S(1)} %get-tuple-element.23), channel_id=1, source_target_pairs={{0,480},{32,64},{64,32},{96,128},{128,96},{160,192},{192,160},{224... | collective-permute-start | bytes 294920 | tf_op jit(solution)/shard_map/ppermute | solution.py:489
  35.8 1.9 %collective-permute-start.3 = (f32[24,8,128]{2,1,0:T(8,128)S(1)}, f32[24,8,128]{2,1,0:T(8,128)S(1)}, u32[]{:S(2)}, u32[]{:S(2)}) collective-permute-start(f32[24,8,128]{2,1,0:T(8,128)S(1)} %get-tuple-element.24), channel_id=1, source_target_pairs={{0,32},{32,0},{64,96},{96,64},{128,160},{160,128},{192,224},{224,1... | collective-permute-start | bytes 294920 | tf_op jit(solution)/shard_map/ppermute | solution.py:490
  37.8 4.6 %shard_map.107 = (f32[2,32,8,256]{3,2,1,0:T(8,128)S(1)}, f32[8,16,8,128]{3,2,1,0:T(8,128)S(1)}) custom-call(s32[3]{0:T(128)S(1)} %pad_add_fusion.flags, f32[8,32,8,256]{3,2,1,0:T(8,128)S(1)} %get-tuple-element.15.rows, f32[8,16,8,256]{3,2,1,0:T(8,128)S(1)} %get-tuple-element.20.ghost, f32[4,2,8,8,256]{4,3,2,1,0:T(8,128)S(1)} %get-tuple-element.21.cuts, ...), custom_call_target="tpu_custom_call" | custom-call | flops 50000000 | bytes 8000000 | tf_op jit(solution)/shard_map/pallas_call | solution.py:400
  42.3 0.0 collective-permute-done.2.odd_strip
  42.3 0.0 collective-permute-done.3.even_strip
  42.4 6.2 %shard_map.108 = (f32[512,128]{1,0:T(8,128)}, f32[512,128]{1,0:T(8,128)}) custom-call(s32[3]{0:T(128)S(1)} %pad_add_fusion.flags, f32[8,32,8,128]{3,2,1,0:T(8,128)S(1)} %get-tuple-element.16.base, f32[8,16,8,128]{3,2,1,0:T(8,128)S(1)} %get-tuple-element.22.beyond, f32[24,8,128]{2,1,0:T(8,128)S(1)} %collective-permute-done.2.odd_strip, ...), custom_call_target="tpu_custom_call" | custom-call | flops 50000000 | bytes 8000000 | tf_op jit(solution)/shard_map/pallas_call | solution.py:400
Async XLA Ops:
  4.4 22.8 %collective-permute-start = (f32[55,8,256]{2,1,0:T(8,128)S(1)}, f32[55,8,256]{2,1,0:T(8,128)S(1)}, u32[]{:S(2)}, u32[]{:S(2)}) collective-permute-start(f32[55,8,256]{2,1,0:T(8,128)S(1)} %get-tuple-element.17), channel_id=1, source_target_pairs={{1,2},{2,1},{3,4},{4,3},{5,6},{6,5},{7,8},{8,7},{9,10},{10,9},{11,... | collective-permute-start | bytes 1351688 | tf_op jit(solution)/shard_map/ppermute | solution.py:485
  16.7 10.6 %collective-permute-start.1 = (f32[55,8,256]{2,1,0:T(8,128)S(1)}, f32[55,8,256]{2,1,0:T(8,128)S(1)}, u32[]{:S(2)}, u32[]{:S(2)}) collective-permute-start(f32[55,8,256]{2,1,0:T(8,128)S(1)} %get-tuple-element.18), channel_id=1, source_target_pairs={{0,1},{1,0},{2,3},{3,2},{4,5},{5,4},{6,7},{7,6},{8,9},{9,8},{10,11... | collective-permute-start | bytes 1351688 | tf_op jit(solution)/shard_map/ppermute | solution.py:486
  28.9 13.5 %collective-permute-start.2 = (f32[24,8,128]{2,1,0:T(8,128)S(1)}, f32[24,8,128]{2,1,0:T(8,128)S(1)}, u32[]{:S(2)}, u32[]{:S(2)}) collective-permute-start(f32[24,8,128]{2,1,0:T(8,128)S(1)} %get-tuple-element.23), channel_id=1, source_target_pairs={{0,480},{32,64},{64,32},{96,128},{128,96},{160,192},{192,160},{224... | collective-permute-start | bytes 294920 | tf_op jit(solution)/shard_map/ppermute | solution.py:489
  35.8 6.5 %collective-permute-start.3 = (f32[24,8,128]{2,1,0:T(8,128)S(1)}, f32[24,8,128]{2,1,0:T(8,128)S(1)}, u32[]{:S(2)}, u32[]{:S(2)}) collective-permute-start(f32[24,8,128]{2,1,0:T(8,128)S(1)} %get-tuple-element.24), channel_id=1, source_target_pairs={{0,32},{32,0},{64,96},{96,64},{128,160},{160,128},{192,224},{224,1... | collective-permute-start | bytes 294920 | tf_op jit(solution)/shard_map/ppermute | solution.py:490

commit v4 on v3

--- a/solution.py
+++ b/solution.py
@@ -10,6 +10,8 @@
 STEPS = 4
 HALO = 2 * STEPS
 PAD = 4
+INNER_FIRST = 4
+OUTER_FIRST = 3
 LEVELS = 8
 HEIGHT = 32
 WIDTH = 256
@@ -19,10 +21,11 @@
 F32 = jnp.float32
 VMEM = pl.BlockSpec(memory_space=pltpu.VMEM)
 SMEM = pl.BlockSpec(memory_space=pltpu.SMEM)
-PARAMS = pltpu.CompilerParams(vmem_limit_bytes=20 * 2**20)
+PARAMS = pltpu.CompilerParams(vmem_limit_bytes=24 * 2**20)
 COST = pl.CostEstimate(flops=50_000_000, bytes_accessed=8_000_000, transcendentals=0)
 
 TRACERS, XF, YF = (0, 1), (2, 3, 4), (5, 6, 7)
+FLIPPED = (2, 4, 5, 7)
 MESSAGE = 2 * 8 + 3 * 6 + 3 * 7
 
 
@@ -70,40 +73,78 @@
     return pltpu.roll(x, by % x.shape[-1], 1)
 
 
+def fields(held, at):
+    temp, salt, u, v, diff, sx, sy, mu, mv = (at(ref) for ref in held)
+    wet_u, wet_v = mu.astype(F32), mv.astype(F32)
+    return temp, salt, u * wet_u, diff * wet_u, sx, v * wet_v, diff * wet_v, sy
+
+
 def pack_kernel(flags, *refs):
-    args, (rows, odd_msg, even_msg), held, sems = refs[:9], refs[9:12], refs[12:21], refs[21]
+    args, (odd_msg, even_msg, sides), held, sems = refs[:9], refs[9:12], refs[12:21], refs[21]
+    copies = []
+    for n, (x, y) in enumerate(zip(args, held)):
+        for part, start in enumerate((0, 2 * HEIGHT - 16)):
+            copies.append(pltpu.make_async_copy(x.at[:, pl.ds(start, 16), :], y.at[part], sems.at[n, part]))
+    for copy in copies:
+        copy.start()
+    for copy in copies:
+        copy.wait()
+
+    def fill(part, msg):
+        for k in range(8):
+
+            def at(ref):
+                flat = ref.at[part].reshape(LEVELS * 16, 128)
+                return jnp.concatenate([flat[pl.ds(8 * c + k, LEVELS, stride=16), :] for c in range(2)], axis=1)
+
+            for f, x in enumerate(fields(held, at)):
+                to = k - (8 - rows_of(f)) * part
+                if 0 <= to < rows_of(f):
+                    msg[slot(f, to)] = x
+
+    @pl.when(flags[0] == 1)
+    def _():
+        fill(1, odd_msg)
+        fill(0, even_msg)
+
+    @pl.when(flags[0] == 0)
+    def _():
+        fill(0, odd_msg)
+        fill(1, even_msg)
+
+    @pl.when(flags[1] == 1)
+    def _():
+        for m in range(9):
+            out = jnp.zeros((LEVELS, 128), F32)
+            for f in range(8):
+                k = 7 - m if f < 2 else 5 - m if m < 8 else 6
+                if k < 0 or (m == 8 and f < 5):
+                    continue
+                x = odd_msg[slot(f, k)]
+                west, east = 8 * (7 - f), 8 * (15 - f)
+                out = jnp.where(within(west, west + 8), roll(x[:, :128], west), out)
+                out = jnp.where(within(east, east + 8), roll(x[:, 128:], -8 * f), out)
+            sides[m] = out
+
+
+def rows_kernel(flags, *refs):
+    args, _, outs, held, sems = refs[:9], refs[9], refs[10:14], refs[14:23], refs[23]
+    rows, cuts, mid, base = outs
     copies = [pltpu.make_async_copy(x, y, sems.at[n]) for n, (x, y) in enumerate(zip(args, held))]
     for copy in copies:
         copy.start()
     for copy in copies:
         copy.wait()
-    temp, salt, u, v, diff, sx, sy, mu, mv = held
-
-    def one(j, _):
-        wet_u, wet_v = load_row(mu, j).astype(F32), load_row(mv, j).astype(F32)
-        r = load_row(diff, j)
-        rows[0, j] = load_row(temp, j)
-        rows[1, j] = load_row(salt, j)
-        rows[2, j] = load_row(u, j) * wet_u
-        rows[3, j] = r * wet_u
-        rows[4, j] = load_row(sx, j)
-        rows[5, j] = load_row(v, j) * wet_v
-        rows[6, j] = r * wet_v
-        rows[7, j] = load_row(sy, j)
-        return 0
-
-    lax.fori_loop(0, HEIGHT, one, 0, unroll=4)
-    odd = flags[0]
-    for f in range(8):
-        n = rows_of(f)
-        north = HEIGHT - n
-
-        def two(k, _, f=f, north=north):
-            odd_msg[slot(f, k)] = rows[f, odd * north + k]
-            even_msg[slot(f, k)] = rows[f, (1 - odd) * north + k]
-            return 0
-
-        lax.fori_loop(0, n, two, 0, unroll=n)
+
+    def one(j):
+        for f, x in enumerate(fields(held, lambda ref: load_row(ref, j))):
+            rows[f, j] = x
+
+    loop(HEIGHT, one, 4)
+
+    @pl.when(flags[3] == 1)
+    def _():
+        inner_part(rows, cuts, mid, base, *refs[24:])
 
 
 def mirrored(x):
@@ -113,9 +154,22 @@
     return jnp.concatenate([jnp.take_along_axis(p, back, axis=1) for p in reversed(parts)], axis=1)
 
 
-def ghost_kernel(flags, rows, odd_msg, even_msg, _, ghost, odd_strip, even_strip):
-    odd, top, lon_odd = flags[0], flags[1], flags[2]
-    is_odd = odd == 1
+def fold_rows(msg, ghost):
+    for f in range(8):
+        n = rows_of(f)
+        sign = -1.0 if f in FLIPPED else 1.0
+        for k in range(n):
+            x = mirrored(msg[slot(f, n - 1 - k)]) * sign
+            if f < 5:
+                ghost[f, HALO + k] = x
+            elif k == 0:
+                ghost[f, 0] = x
+            else:
+                ghost[f, HALO + k - 1] = x
+
+
+def ghost_kernel(flags, rows, odd_msg, even_msg, sides, cuts, mid, ghost, odd_strip, even_strip, result, base, *scratch):
+    is_odd = flags[0] == 1
     for f in range(8):
         n = rows_of(f)
         for k in range(n):
@@ -126,21 +180,7 @@
         if f >= 5:
             ghost[f, 0] = rows[f, HEIGHT - 1]
 
-    @pl.when(top == 1)
-    def _():
-        for f in range(8):
-            n = rows_of(f)
-            sign = -1.0 if f in (2, 4, 5, 7) else 1.0
-            for k in range(n):
-                x = mirrored(odd_msg[slot(f, n - 1 - k)]) * sign
-                if f < 5:
-                    ghost[f, HALO + k] = x
-                elif k == 0:
-                    ghost[f, 0] = x
-                else:
-                    ghost[f, HALO + k - 1] = x
-
-    swap = lon_odd == 1
+    swap = flags[2] == 1
     for r in range(EXT // 2):
         east, west = jnp.zeros((LEVELS, 128), F32), jnp.zeros((LEVELS, 128), F32)
         for half in range(2):
@@ -158,6 +198,29 @@
                 west = jnp.where(within(to, to + 8), roll(x[:, :128], to), west)
         even_strip[r] = jnp.where(swap, west, east)
         odd_strip[r] = jnp.where(swap, east, west)
+
+    @pl.when(flags[1] == 1)
+    def _():
+        lane = lanes(128)
+        field = (lane // 8) % 8
+        flip = (field == 2) | (field == 4) | (field == 5) | (field == 7)
+        for m in range(9):
+            x = jnp.take_along_axis(sides[m], 127 - lane, axis=1)
+            x = jnp.where(flip, -x, x)
+            r = 2 * HALO + m
+            in_east, in_west = lane >= 64, lane < 64
+            if m == 8:
+                r, x = 0, roll(x, 64)
+                in_east, in_west = within(40, 64), within(104, 128)
+            a, b = even_strip[r], odd_strip[r]
+            east = jnp.where(in_east, x, jnp.where(swap, b, a))
+            west = jnp.where(in_west, x, jnp.where(swap, a, b))
+            even_strip[r] = jnp.where(swap, west, east)
+            odd_strip[r] = jnp.where(swap, east, west)
+
+    @pl.when(flags[4] == 1)
+    def _():
+        outer_part(flags, rows, ghost, cuts, mid, result, base, *scratch)
 
 
 def minmod(p, t):
@@ -266,7 +329,7 @@
     return jnp.where(within(16, 32), roll(x[:, :128], 16), roll(x[:, 128:], 72))
 
 
-def inner_kernel(rows, cuts, mid, base, s0, s1, s2, s3, s4, cx, cy):
+def inner_part(rows, cuts, mid, base, s0, s1, s2, s3, s4, cx, cy):
     def own(j):
         for n in TRACERS:
             s0[n, HALO + j] = rows[n, j]
@@ -292,7 +355,7 @@
         loop(2 * HALO, out, 4)
 
 
-def outer_kernel(flags, rows, ghost, cuts, mid, result, base, qa, qb, cx, cy):
+def outer_part(flags, rows, ghost, cuts, mid, result, base, qa, qb, cx, cy):
     top = flags[1] == 1
 
     def near(k):
@@ -343,8 +406,41 @@
     loop(HALO, out, 2)
 
 
-def edge_kernel(flags, base, beyond, odd_strip, even_strip, result, temp, salt, qa, qb, cx, cy):
-    top = flags[1] == 1
+def late_kernel(flags, rows, ghost, fold, cuts, mid, result, base, beyond, gh, my_cuts, my_mid, *scratch):
+    states, (cx, cy) = scratch[:5], scratch[5:]
+
+    @pl.when(flags[3] == 0)
+    def _():
+        inner_part(rows, my_cuts, my_mid, base, *states, cx, cy)
+
+    @pl.when(flags[4] == 0)
+    def _():
+        @pl.when(flags[3] == 1)
+        def _():
+            def copy(k):
+                for n in TRACERS:
+                    for step in range(STEPS - 1):
+                        my_cuts[step, n, k] = cuts[step, n, k]
+                    my_mid[n, k] = mid[n, k]
+                    my_mid[n, 8 + k] = mid[n, 8 + k]
+
+            loop(8, copy, 4)
+
+        def copy(k):
+            for f in range(8):
+                gh[f, k] = ghost[f, k]
+
+        loop(2 * HALO, copy, 4)
+
+        @pl.when(flags[1] == 1)
+        def _():
+            fold_rows(fold, gh)
+
+        outer_part(flags, rows, gh, my_cuts, my_mid, result, beyond, *states[:2], cx, cy)
+
+
+def edge_kernel(flags, base1, base2, beyond1, beyond2, odd_strip, even_strip, result1, result2, temp, salt, qa, qb, cx, cy):
+    top, inner_first, outer_first = flags[1] == 1, flags[3] == 1, flags[4] == 1
     lane = lanes(128)
     from_odd = (lane < 64).astype(jnp.int32) != flags[2]
     is_temp = within(8, 32) | within(56, 80)
@@ -353,10 +449,16 @@
     def both(y):
         return jnp.where(is_temp, y, roll(y, SALT))
 
-    def assemble(ref, k, r, half, turn=None):
+    def base(f, k):
+        return jnp.where(inner_first, base1[f, k], base2[f, k])
+
+    def beyond(f, k):
+        return jnp.where(outer_first, beyond1[f, k], beyond2[f, k])
+
+    def assemble(either, k, r, half, turn=None):
         a, b = odd_strip[r], even_strip[r]
         halo = jnp.where(from_odd, a, b) if half == 0 else jnp.where(from_odd, b, a)
-        y = [jnp.where(beside, roll(halo, 8 - 8 * f - 64 * half), ref[f, k]) for f in range(8)]
+        y = [jnp.where(beside, roll(halo, 8 - 8 * f - 64 * half), either(f, k)) for f in range(8)]
         to = PAD + r + half * (EXT // 2)
         qa[0, to] = jnp.where(is_temp, y[0], roll(y[1], SALT))
         x = [both(y[f]) for f in XF]
@@ -386,7 +488,7 @@
     def patch(j):
         e = qa[0, PAD + HALO + j]
         for n, out in enumerate((temp, salt)):
-            x = result[n, j]
+            x = jnp.where(outer_first, result1[n, j], result2[n, j])
             w = jnp.where(lane < 8, roll(e, -16 - SALT * n), x[:, :128])
             z = jnp.where(lane >= 120, roll(e, 56 - SALT * n), x[:, 128:])
             for at, y in zip(places(j), (w, z)):
@@ -395,12 +497,12 @@
     loop(HEIGHT, patch, 8)
 
 
-def call(kernel, outs, args, scratch=(), args_in=VMEM, flags=None):
+def call(kernel, outs, args, scratch=(), args_in=None, flags=None):
     first = [] if flags is None else [flags]
     return pl.pallas_call(
         kernel,
         out_shape=[jax.ShapeDtypeStruct(s, F32) for s in outs],
-        in_specs=[SMEM] * len(first) + [args_in] * len(args),
+        in_specs=[SMEM] * len(first) + (args_in or [VMEM] * len(args)),
         out_specs=[VMEM] * len(outs),
         scratch_shapes=[pltpu.VMEM(s, F32) if isinstance(s, tuple) else s for s in scratch],
         compiler_params=PARAMS,
@@ -415,48 +517,65 @@
 FLAT = (2 * LEVELS * HEIGHT, 128)
 
 
+STATES = [STATE] * 5 + [(6, EXT, *ROW), (5, EXT, *ROW)]
+OUTER = [STATE] * 2 + [(6, EXT, *ROW), (5, EXT, *ROW)]
+RESULT = (2, HEIGHT, *ROW)
+CUTS, MID, BASE, BEYOND = (STEPS, 2, 8, *ROW), (2, 2 * HALO, *ROW), (8, HEIGHT, *TILE), (8, 2 * HALO, *TILE)
+GHOST = (8, 2 * HALO, *ROW)
+IN_HBM = pl.BlockSpec(memory_space=pltpu.HBM)
+
+
 def pack(flags, args):
-    held = [pltpu.VMEM(FLAT, x.dtype) for x in args]
+    held = [pltpu.VMEM((2, LEVELS, 16, 128), x.dtype) for x in args]
+    args = [pltpu.with_memory_space_constraint(x.reshape(LEVELS, -1, 128), pltpu.HBM) for x in args]
     return call(
         pack_kernel,
-        [(8, HEIGHT, *ROW), (MESSAGE, *ROW), (MESSAGE, *ROW)],
+        [(MESSAGE, *ROW), (MESSAGE, *ROW), (9, *TILE)],
         args,
-        [*held, pltpu.SemaphoreType.DMA((9,))],
-        pl.BlockSpec(memory_space=pltpu.HBM),
+        [*held, pltpu.SemaphoreType.DMA((9, 2))],
+        [IN_HBM] * 9,
         flags,
     )
 
 
-def inner(rows):
+def transpose(flags, args, after):
+    held = [pltpu.VMEM(FLAT, x.dtype) for x in args]
+    args = [pltpu.with_memory_space_constraint(x, pltpu.HBM) for x in args]
     return call(
-        inner_kernel,
-        [(STEPS, 2, 8, *ROW), (2, 2 * HALO, *ROW), (8, HEIGHT, *TILE)],
-        [rows],
-        [STATE] * 5 + [(6, EXT, *ROW), (5, EXT, *ROW)],
+        rows_kernel,
+        [(8, HEIGHT, *ROW), CUTS, MID, BASE],
+        [*args, after],
+        [*held, pltpu.SemaphoreType.DMA((9,)), *STATES],
+        [IN_HBM] * 9 + [VMEM],
+        flags,
     )
 
 
-def fill_ghost(flags, rows, odd_in, even_in, after):
+def fill_ghost(flags, rows, odd_in, even_in, sides, cuts, mid):
     return call(
-        ghost_kernel, [(8, 2 * HALO, *ROW), STRIP, STRIP], [rows, odd_in, even_in, after], flags=flags
-    )
-
-
-def outer(flags, rows, ghost, cuts, mid):
-    return call(
-        outer_kernel,
-        [(2, HEIGHT, *ROW), (8, 2 * HALO, *TILE)],
-        [rows, ghost, cuts, mid],
-        [STATE] * 2 + [(6, EXT, *ROW), (5, EXT, *ROW)],
+        ghost_kernel,
+        [GHOST, STRIP, STRIP, RESULT, BEYOND],
+        [rows, odd_in, even_in, sides, cuts, mid],
+        OUTER,
         flags=flags,
     )
 
 
-def edge(flags, base, beyond, odd_strip, even_strip, result):
+def late(flags, rows, ghost, fold, cuts, mid):
+    return call(
+        late_kernel,
+        [RESULT, BASE, BEYOND],
+        [rows, ghost, fold, cuts, mid],
+        [GHOST, CUTS, MID, *STATES],
+        flags=flags,
+    )
+
+
+def edge(flags, *args):
     return call(
         edge_kernel,
         [FLAT] * 2,
-        [base, beyond, odd_strip, even_strip, result],
+        args,
         [(1, EDGE_DEPTH, *TILE)] * 2 + [(6, EDGE_DEPTH, *TILE), (5, EDGE_DEPTH, *TILE)],
         flags=flags,
     )
@@ -464,7 +583,11 @@
 
 def on_device(lon_count, lat_count, *args):
     lon, lat = lax.axis_index("lon"), lax.axis_index("lat")
-    flags = jnp.stack([lat % 2, (lat == lat_count - 1).astype(jnp.int32), lon % 2])
+    top = (lat == lat_count - 1).astype(jnp.int32)
+    place = lon % 8
+    inner_first = (place < INNER_FIRST).astype(jnp.int32)
+    outer_first = (place < OUTER_FIRST).astype(jnp.int32) * (1 - top)
+    flags = jnp.stack([lat % 2, top, lon % 2, inner_first, outer_first])
     flat = [level_major(x) for x in args]
 
     def index(i, j):
@@ -473,23 +596,23 @@
     lons, lats = range(lon_count), range(lat_count)
     lat_even = [(index(i, j), index(i, j ^ 1)) for i in lons for j in lats]
     lat_odd = [
-        (index(i, j), index(lon_count - 1 - i, j) if j == lat_count - 1 else index(i, j + 1 if j % 2 else j - 1))
-        for i in lons
-        for j in lats
-        if j > 0
+        (index(i, j), index(i, j + 1 if j % 2 else j - 1)) for i in lons for j in range(1, lat_count - 1)
     ]
+    fold = [(index(i, lat_count - 1), index(lon_count - 1 - i, lat_count - 1)) for i in lons]
     lon_even = [(i, i ^ 1) for i in lons]
     lon_odd = [(i, (i + 1 if i % 2 else i - 1) % lon_count) for i in lons]
-    flat = [pltpu.with_memory_space_constraint(x, pltpu.HBM) for x in flat]
-    rows, odd_msg, even_msg = pack(flags, flat)
-    odd_in = lax.ppermute(odd_msg, ("lon", "lat"), lat_odd)
-    even_in = lax.ppermute(even_msg, ("lon", "lat"), lat_even)
-    cuts, mid, base = inner(rows)
-    ghost, odd_strip, even_strip = fill_ghost(flags, rows, odd_in, even_in, mid)
+    both = ("lon", "lat")
+    odd_msg, even_msg, sides = pack(flags, flat)
+    fold_in = lax.ppermute(odd_msg, both, fold)
+    odd_in = lax.ppermute(odd_msg, both, lat_odd)
+    even_in = lax.ppermute(even_msg, both, lat_even)
+    sides = lax.ppermute(sides, both, fold)
+    rows, cuts, mid, base1 = transpose(flags, flat, odd_msg)
+    ghost, odd_strip, even_strip, result1, beyond1 = fill_ghost(flags, rows, odd_in, even_in, sides, cuts, mid)
     odd_strip = lax.ppermute(odd_strip, "lon", lon_odd)
     even_strip = lax.ppermute(even_strip, "lon", lon_even)
-    result, beyond = outer(flags, rows, ghost, cuts, mid)
-    temp, salt = edge(flags, base, beyond, odd_strip, even_strip, result)
+    result2, base2, beyond2 = late(flags, rows, ghost, fold_in, cuts, mid)
+    temp, salt = edge(flags, base1, base2, beyond1, beyond2, odd_strip, even_strip, result1, result2)
     return from_level_major(temp), from_level_major(salt)
 
 

time: 48.8 us -> 51.9 us (1.064)
  starting transfers between devices: 23.1 us -> 26.2 us
  waiting for transfers between devices: 3.45 us -> 0.62 us
  Pallas kernels: 21.3 us -> 23.9 us
    ppermute x2 -> x4, starting transfers between devices: 14.1 us -> 17.3 us  [the longest x1 12.2 us: on_device(): fold_in = lax.ppermute(odd_msg, both, fold)]
    ppermute x2 -> x4, waiting for transfers between devices: 3.44 us -> 0.62 us  [the longest x1 0.61 us: on_device(): sides = lax.ppermute(sides, both, fold)]
    pallas_call x5, Pallas kernels: 21.3 us -> 23.9 us  [call(): pl.pallas_call(kernel, out_shape=[jax.ShapeDtypeStruct(s, F32) for s in o...]
  transfers between devices with their start and end apart: 4 -> 6, of which waited for: 1 -> 1; matrix products, arithmetic and copies ran while one was open for 0% -> 0% of each run, Pallas kernels for 20% -> 29%
where the time goes in v4:
time: 51.9 us; the launch traced here: 51.6 us
  starting transfers between devices  26.2 us (50%)
  Pallas kernels  23.9 us (46%)
  between operations  0.76 us (1%)
  waiting for transfers between devices  0.62 us (1%)
    pallas_call x5, Pallas kernels, call(): pl.pallas_call(kernel, out_shape=[jax.ShapeDtypeStruct(s, F32) for s in o...  23.9 us
    ppermute x1, starting transfers between devices, on_device(): fold_in = lax.ppermute(odd_msg, both, fold)  12.2 us
    ppermute x1, starting transfers between devices, on_device(): odd_strip = lax.ppermute(odd_strip, 'lon', lon_odd)  6.98 us
    ppermute x1, starting transfers between devices, on_device(): even_in = lax.ppermute(even_msg, both, lat_even)  2.41 us
    ppermute x1, starting transfers between devices, on_device(): sides = lax.ppermute(sides, both, fold)  1.92 us
    ppermute x1, starting transfers between devices, on_device(): even_strip = lax.ppermute(even_strip, 'lon', lon_even)  1.92 us
  transfers between devices with their start and end apart: 6, of which 1 were waited for; matrix products, arithmetic and copies ran while one was open for 0% of the time, Pallas kernels for 29%

profile of v4, /device:TPU:59, one launch (start us, length us, event | category | flops | bytes accessed | tf_op | source)
XLA Modules:
  0.0 51.6 jit_solution(6098473174361200876)
XLA Ops:
  0.7 0.1 stack.27.flags
  0.7 2.5 %shard_map.104 = (f32[55,8,256]{2,1,0:T(8,128)S(1)}, f32[55,8,256]{2,1,0:T(8,128)S(1)}, f32[9,8,128]{2,1,0:T(8,128)S(1)}) custom-call(s32[5]{0:T(128)S(1)} %stack.27.flags, f32[8,64,128]{2,1,0:T(8,128)} %bitcast.78, f32[8,64,128]{2,1,0:T(8,128)} %bitcast.80, f32[8,64,128]{2,1,0:T(8,128)} %bitcast.82, f32[8,64,128]{2,1,0:T(8,128)} %bitcast.84, ...), custom_call_target="tpu_custom_call" | custom-call | flops 50000000 | bytes 8000000 | tf_op jit(solution)/shard_map/pallas_call | solution.py:502
  3.2 2.4 %collective-permute-start.1 = (f32[55,8,256]{2,1,0:T(8,128)S(1)}, f32[55,8,256]{2,1,0:T(8,128)S(1)}, u32[]{:S(2)}, u32[]{:S(2)}) collective-permute-start(f32[55,8,256]{2,1,0:T(8,128)S(1)} %get-tuple-element.22), channel_id=1, source_target_pairs={{0,1},{1,0},{2,3},{3,2},{4,5},{5,4},{6,7},{7,6},{8,9},{9,8},{10,11... | collective-permute-start | bytes 1351688 | tf_op jit(solution)/shard_map/ppermute | solution.py:608
  5.6 0.7 %collective-permute-start = (f32[55,8,256]{2,1,0:T(8,128)S(1)}, f32[55,8,256]{2,1,0:T(8,128)S(1)}, u32[]{:S(2)}, u32[]{:S(2)}) collective-permute-start(f32[55,8,256]{2,1,0:T(8,128)S(1)} %get-tuple-element.19.refs_9_), channel_id=1, source_target_pairs={{1,2},{2,1},{3,4},{4,3},{5,6},{6,5},{7,8},{8,7},{9,10},{10,9},{11,... | collective-permute-start | bytes 1351688 | tf_op jit(solution)/shard_map/ppermute | solution.py:607
  6.3 12.2 %collective-permute-start.3 = (f32[55,8,256]{2,1,0:T(8,128)S(1)}, f32[55,8,256]{2,1,0:T(8,128)S(1)}, u32[]{:S(2)}, u32[]{:S(2)}) collective-permute-start(f32[55,8,256]{2,1,0:T(8,128)S(1)} %get-tuple-element.19.refs_9_), channel_id=1, source_target_pairs={{31,511},{63,479},{95,447},{127,415},{159,383},{191,351},{223,319}... | collective-permute-start | bytes 1351688 | tf_op jit(solution)/shard_map/ppermute | solution.py:606
  18.6 1.9 %collective-permute-start.2 = (f32[9,8,128]{2,1,0:T(8,128)S(1)}, f32[9,8,128]{2,1,0:T(8,128)S(1)}, u32[]{:S(2)}, u32[]{:S(2)}) collective-permute-start(f32[9,8,128]{2,1,0:T(8,128)S(1)} %get-tuple-element.23), channel_id=1, source_target_pairs={{31,511},{63,479},{95,447},{127,415},{159,383},{191,351},{223,319}... | collective-permute-start | bytes 110600 | tf_op jit(solution)/shard_map/ppermute | solution.py:609
  20.5 8.8 %shard_map.105 = (f32[8,32,8,256]{3,2,1,0:T(8,128)S(1)}, f32[4,2,8,8,256]{4,3,2,1,0:T(8,128)S(1)}, f32[2,16,8,256]{3,2,1,0:T(8,128)S(1)}, f32[8,32,8,128]{3,2,1,0:T(8,128)S(1)}) custom-call(s32[5]{0:T(128)S(1)} %stack.27.flags, f32[512,128]{1,0:T(8,128)} %bitcast.79, f32[512,128]{1,0:T(8,128)} %bitcast.81, f32[512,128]{1,0:T(8,128)} %bitcast.83, ...), custom_call_target="tpu_custom_call" | custom-call | flops 50000000 | bytes 8000000 | tf_op jit(solution)/shard_map/pallas_call | solution.py:502
  29.3 0.6 %collective-permute-done.2.sides = f32[9,8,128]{2,1,0:T(8,128)S(1)} collective-permute-done((f32[9,8,128]{2,1,0:T(8,128)S(1)}, f32[9,8,128]{2,1,0:T(8,128)S(1)}, u32[]{:S(2)}, u32[]{:S(2)}) %collective-permute-start.2) | collective-permute-done | bytes 36896 | tf_op jit(solution)/shard_map/ppermute | solution.py:609
  29.9 0.0 collective-permute-done.1.even_msg
  30.0 0.0 collective-permute-done.odd_msg
  30.0 1.5 %shard_map.106 = (f32[8,16,8,256]{3,2,1,0:T(8,128)S(1)}, f32[24,8,128]{2,1,0:T(8,128)S(1)}, f32[24,8,128]{2,1,0:T(8,128)S(1)}, f32[2,32,8,256]{3,2,1,0:T(8,128)S(1)}, f32[8,16,8,128]{3,2,1,0:T(8,128)S(1)}) custom-call(s32[5]{0:T(128)S(1)} %stack.27.flags, f32[8,32,8,256]{3,2,1,0:T(8,128)S(1)} %get-tuple-element.21.rows, ...), custom_call_target="tpu_custom_call" | custom-call | flops 50000000 | bytes 8000000 | tf_op jit(solution)/shard_map/pallas_call | solution.py:502
  31.5 7.0 %collective-permute-start.4 = (f32[24,8,128]{2,1,0:T(8,128)S(1)}, f32[24,8,128]{2,1,0:T(8,128)S(1)}, u32[]{:S(2)}, u32[]{:S(2)}) collective-permute-start(f32[24,8,128]{2,1,0:T(8,128)S(1)} %get-tuple-element.30), channel_id=1, source_target_pairs={{0,480},{32,64},{64,32},{96,128},{128,96},{160,192},{192,160},{224... | collective-permute-start | bytes 294920 | tf_op jit(solution)/shard_map/ppermute | solution.py:612
  38.5 1.9 %collective-permute-start.5 = (f32[24,8,128]{2,1,0:T(8,128)S(1)}, f32[24,8,128]{2,1,0:T(8,128)S(1)}, u32[]{:S(2)}, u32[]{:S(2)}) collective-permute-start(f32[24,8,128]{2,1,0:T(8,128)S(1)} %get-tuple-element.31), channel_id=1, source_target_pairs={{0,32},{32,0},{64,96},{96,64},{128,160},{160,128},{192,224},{224,1... | collective-permute-start | bytes 294920 | tf_op jit(solution)/shard_map/ppermute | solution.py:613
  40.4 0.0 collective-permute-done.3.fold
  40.4 4.9 %shard_map.107 = (f32[2,32,8,256]{3,2,1,0:T(8,128)S(1)}, f32[8,32,8,128]{3,2,1,0:T(8,128)S(1)}, f32[8,16,8,128]{3,2,1,0:T(8,128)S(1)}) custom-call(s32[5]{0:T(128)S(1)} %stack.27.flags, f32[8,32,8,256]{3,2,1,0:T(8,128)S(1)} %get-tuple-element.21.rows, f32[8,16,8,256]{3,2,1,0:T(8,128)S(1)} %get-tuple-element.26.ghost, ...), custom_call_target="tpu_custom_call" | custom-call | flops 50000000 | bytes 8000000 | tf_op jit(solution)/shard_map/pallas_call | solution.py:502
  45.3 0.0 collective-permute-done.4.odd_strip
  45.3 0.0 collective-permute-done.5.even_strip
  45.3 6.3 %shard_map.108 = (f32[512,128]{1,0:T(8,128)}, f32[512,128]{1,0:T(8,128)}) custom-call(s32[5]{0:T(128)S(1)} %stack.27.flags, f32[8,32,8,128]{3,2,1,0:T(8,128)S(1)} %get-tuple-element.20.base1, f32[8,32,8,128]{3,2,1,0:T(8,128)S(1)} %get-tuple-element.27.base2, f32[8,16,8,128]{3,2,1,0:T(8,128)S(1)} %get-tuple-element.28.beyond1, ...), custom_call_target="tpu_custom_call" | custom-call | flops 50000000 | bytes 8000000 | tf_op jit(solution)/shard_map/pallas_call | solution.py:502
Async XLA Ops:
  3.2 26.7 %collective-permute-start.1 = (f32[55,8,256]{2,1,0:T(8,128)S(1)}, f32[55,8,256]{2,1,0:T(8,128)S(1)}, u32[]{:S(2)}, u32[]{:S(2)}) collective-permute-start(f32[55,8,256]{2,1,0:T(8,128)S(1)} %get-tuple-element.22), channel_id=1, source_target_pairs={{0,1},{1,0},{2,3},{3,2},{4,5},{5,4},{6,7},{7,6},{8,9},{9,8},{10,11... | collective-permute-start | bytes 1351688 | tf_op jit(solution)/shard_map/ppermute | solution.py:608
  5.6 24.3 %collective-permute-start = (f32[55,8,256]{2,1,0:T(8,128)S(1)}, f32[55,8,256]{2,1,0:T(8,128)S(1)}, u32[]{:S(2)}, u32[]{:S(2)}) collective-permute-start(f32[55,8,256]{2,1,0:T(8,128)S(1)} %get-tuple-element.19.refs_9_), channel_id=1, source_target_pairs={{1,2},{2,1},{3,4},{4,3},{5,6},{6,5},{7,8},{8,7},{9,10},{10,9},{11,... | collective-permute-start | bytes 1351688 | tf_op jit(solution)/shard_map/ppermute | solution.py:607
  6.3 34.0 %collective-permute-start.3 = (f32[55,8,256]{2,1,0:T(8,128)S(1)}, f32[55,8,256]{2,1,0:T(8,128)S(1)}, u32[]{:S(2)}, u32[]{:S(2)}) collective-permute-start(f32[55,8,256]{2,1,0:T(8,128)S(1)} %get-tuple-element.19.refs_9_), channel_id=1, source_target_pairs={{31,511},{63,479},{95,447},{127,415},{159,383},{191,351},{223,319}... | collective-permute-start | bytes 1351688 | tf_op jit(solution)/shard_map/ppermute | solution.py:606
  18.6 11.4 %collective-permute-start.2 = (f32[9,8,128]{2,1,0:T(8,128)S(1)}, f32[9,8,128]{2,1,0:T(8,128)S(1)}, u32[]{:S(2)}, u32[]{:S(2)}) collective-permute-start(f32[9,8,128]{2,1,0:T(8,128)S(1)} %get-tuple-element.23), channel_id=1, source_target_pairs={{31,511},{63,479},{95,447},{127,415},{159,383},{191,351},{223,319}... | collective-permute-start | bytes 110600 | tf_op jit(solution)/shard_map/ppermute | solution.py:609
  31.5 13.8 %collective-permute-start.4 = (f32[24,8,128]{2,1,0:T(8,128)S(1)}, f32[24,8,128]{2,1,0:T(8,128)S(1)}, u32[]{:S(2)}, u32[]{:S(2)}) collective-permute-start(f32[24,8,128]{2,1,0:T(8,128)S(1)} %get-tuple-element.30), channel_id=1, source_target_pairs={{0,480},{32,64},{64,32},{96,128},{128,96},{160,192},{192,160},{224... | collective-permute-start | bytes 294920 | tf_op jit(solution)/shard_map/ppermute | solution.py:612
  38.5 6.8 %collective-permute-start.5 = (f32[24,8,128]{2,1,0:T(8,128)S(1)}, f32[24,8,128]{2,1,0:T(8,128)S(1)}, u32[]{:S(2)}, u32[]{:S(2)}) collective-permute-start(f32[24,8,128]{2,1,0:T(8,128)S(1)} %get-tuple-element.31), channel_id=1, source_target_pairs={{0,32},{32,0},{64,96},{96,64},{128,160},{160,128},{192,224},{224,1... | collective-permute-start | bytes 294920 | tf_op jit(solution)/shard_map/ppermute | solution.py:613

commit v5 on v4

--- a/solution.py
+++ b/solution.py
@@ -80,7 +80,7 @@
 
 
 def pack_kernel(flags, *refs):
-    args, (odd_msg, even_msg, sides), held, sems = refs[:9], refs[9:12], refs[12:21], refs[21]
+    args, (odd_msg, even_msg), held, sems = refs[:9], refs[9:11], refs[11:20], refs[20]
     copies = []
     for n, (x, y) in enumerate(zip(args, held)):
         for part, start in enumerate((0, 2 * HEIGHT - 16)):
@@ -111,20 +111,6 @@
     def _():
         fill(0, odd_msg)
         fill(1, even_msg)
-
-    @pl.when(flags[1] == 1)
-    def _():
-        for m in range(9):
-            out = jnp.zeros((LEVELS, 128), F32)
-            for f in range(8):
-                k = 7 - m if f < 2 else 5 - m if m < 8 else 6
-                if k < 0 or (m == 8 and f < 5):
-                    continue
-                x = odd_msg[slot(f, k)]
-                west, east = 8 * (7 - f), 8 * (15 - f)
-                out = jnp.where(within(west, west + 8), roll(x[:, :128], west), out)
-                out = jnp.where(within(east, east + 8), roll(x[:, 128:], -8 * f), out)
-            sides[m] = out
 
 
 def rows_kernel(flags, *refs):
@@ -168,7 +154,7 @@
                 ghost[f, HALO + k - 1] = x
 
 
-def ghost_kernel(flags, rows, odd_msg, even_msg, sides, cuts, mid, ghost, odd_strip, even_strip, result, base, *scratch):
+def ghost_kernel(flags, rows, odd_msg, even_msg, cuts, mid, ghost, odd_strip, even_strip, result, base, *scratch):
     is_odd = flags[0] == 1
     for f in range(8):
         n = rows_of(f)
@@ -179,6 +165,10 @@
                 ghost[f, HALO + k] = jnp.where(is_odd, a, b)
         if f >= 5:
             ghost[f, 0] = rows[f, HEIGHT - 1]
+
+    @pl.when(flags[1] == 1)
+    def _():
+        fold_rows(odd_msg, ghost)
 
     swap = flags[2] == 1
     for r in range(EXT // 2):
@@ -198,25 +188,6 @@
                 west = jnp.where(within(to, to + 8), roll(x[:, :128], to), west)
         even_strip[r] = jnp.where(swap, west, east)
         odd_strip[r] = jnp.where(swap, east, west)
-
-    @pl.when(flags[1] == 1)
-    def _():
-        lane = lanes(128)
-        field = (lane // 8) % 8
-        flip = (field == 2) | (field == 4) | (field == 5) | (field == 7)
-        for m in range(9):
-            x = jnp.take_along_axis(sides[m], 127 - lane, axis=1)
-            x = jnp.where(flip, -x, x)
-            r = 2 * HALO + m
-            in_east, in_west = lane >= 64, lane < 64
-            if m == 8:
-                r, x = 0, roll(x, 64)
-                in_east, in_west = within(40, 64), within(104, 128)
-            a, b = even_strip[r], odd_strip[r]
-            east = jnp.where(in_east, x, jnp.where(swap, b, a))
-            west = jnp.where(in_west, x, jnp.where(swap, a, b))
-            even_strip[r] = jnp.where(swap, west, east)
-            odd_strip[r] = jnp.where(swap, east, west)
 
     @pl.when(flags[4] == 1)
     def _():
@@ -406,7 +377,7 @@
     loop(HALO, out, 2)
 
 
-def late_kernel(flags, rows, ghost, fold, cuts, mid, result, base, beyond, gh, my_cuts, my_mid, *scratch):
+def late_kernel(flags, rows, ghost, cuts, mid, result, base, beyond, my_cuts, my_mid, *scratch):
     states, (cx, cy) = scratch[:5], scratch[5:]
 
     @pl.when(flags[3] == 0)
@@ -426,17 +397,7 @@
 
             loop(8, copy, 4)
 
-        def copy(k):
-            for f in range(8):
-                gh[f, k] = ghost[f, k]
-
-        loop(2 * HALO, copy, 4)
-
-        @pl.when(flags[1] == 1)
-        def _():
-            fold_rows(fold, gh)
-
-        outer_part(flags, rows, gh, my_cuts, my_mid, result, beyond, *states[:2], cx, cy)
+        outer_part(flags, rows, ghost, my_cuts, my_mid, result, beyond, *states[:2], cx, cy)
 
 
 def edge_kernel(flags, base1, base2, beyond1, beyond2, odd_strip, even_strip, result1, result2, temp, salt, qa, qb, cx, cy):
@@ -530,7 +491,7 @@
     args = [pltpu.with_memory_space_constraint(x.reshape(LEVELS, -1, 128), pltpu.HBM) for x in args]
     return call(
         pack_kernel,
-        [(MESSAGE, *ROW), (MESSAGE, *ROW), (9, *TILE)],
+        [(MESSAGE, *ROW)] * 2,
         args,
         [*held, pltpu.SemaphoreType.DMA((9, 2))],
         [IN_HBM] * 9,
@@ -551,22 +512,22 @@
     )
 
 
-def fill_ghost(flags, rows, odd_in, even_in, sides, cuts, mid):
+def fill_ghost(flags, rows, odd_in, even_in, cuts, mid):
     return call(
         ghost_kernel,
         [GHOST, STRIP, STRIP, RESULT, BEYOND],
-        [rows, odd_in, even_in, sides, cuts, mid],
+        [rows, odd_in, even_in, cuts, mid],
         OUTER,
         flags=flags,
     )
 
 
-def late(flags, rows, ghost, fold, cuts, mid):
+def late(flags, rows, ghost, cuts, mid):
     return call(
         late_kernel,
         [RESULT, BASE, BEYOND],
-        [rows, ghost, fold, cuts, mid],
-        [GHOST, CUTS, MID, *STATES],
+        [rows, ghost, cuts, mid],
+        [CUTS, MID, *STATES],
         flags=flags,
     )
 
@@ -596,22 +557,22 @@
     lons, lats = range(lon_count), range(lat_count)
     lat_even = [(index(i, j), index(i, j ^ 1)) for i in lons for j in lats]
     lat_odd = [
-        (index(i, j), index(i, j + 1 if j % 2 else j - 1)) for i in lons for j in range(1, lat_count - 1)
+        (index(i, j), index(lon_count - 1 - i, j) if j == lat_count - 1 else index(i, j + 1 if j % 2 else j - 1))
+        for i in lons
+        for j in lats
+        if j > 0
     ]
-    fold = [(index(i, lat_count - 1), index(lon_count - 1 - i, lat_count - 1)) for i in lons]
     lon_even = [(i, i ^ 1) for i in lons]
     lon_odd = [(i, (i + 1 if i % 2 else i - 1) % lon_count) for i in lons]
     both = ("lon", "lat")
-    odd_msg, even_msg, sides = pack(flags, flat)
-    fold_in = lax.ppermute(odd_msg, both, fold)
+    odd_msg, even_msg = pack(flags, flat)
     odd_in = lax.ppermute(odd_msg, both, lat_odd)
     even_in = lax.ppermute(even_msg, both, lat_even)
-    sides = lax.ppermute(sides, both, fold)
     rows, cuts, mid, base1 = transpose(flags, flat, odd_msg)
-    ghost, odd_strip, even_strip, result1, beyond1 = fill_ghost(flags, rows, odd_in, even_in, sides, cuts, mid)
+    ghost, odd_strip, even_strip, result1, beyond1 = fill_ghost(flags, rows, odd_in, even_in, cuts, mid)
     odd_strip = lax.ppermute(odd_strip, "lon", lon_odd)
     even_strip = lax.ppermute(even_strip, "lon", lon_even)
-    result2, base2, beyond2 = late(flags, rows, ghost, fold_in, cuts, mid)
+    result2, base2, beyond2 = late(flags, rows, ghost, cuts, mid)
     temp, salt = edge(flags, base1, base2, beyond1, beyond2, odd_strip, even_strip, result1, result2)
     return from_level_major(temp), from_level_major(salt)
 

time: 51.9 us -> 50.2 us (0.967)
  starting transfers between devices: 26.2 us -> 23.7 us
  waiting for transfers between devices: 0.62 us -> 1.75 us
    ppermute x2 -> x0, starting transfers between devices: 14.1 us -> none  [the longest x1 12.2 us: on_device(): fold_in = lax.ppermute(odd_msg, both, fold)]
    ppermute x1, starting transfers between devices: 0.69 us -> 12.2 us  [on_device(): odd_in = lax.ppermute(odd_msg, both, lat_odd)]
    ppermute x1, waiting for transfers between devices: 0.01 us -> 1.74 us  [on_device(): odd_in = lax.ppermute(odd_msg, both, lat_odd)]
    ppermute x2 -> x0, waiting for transfers between devices: 0.61 us -> none  [the longest x1 0.61 us: on_device(): sides = lax.ppermute(sides, both, fold)]
  transfers between devices with their start and end apart: 6 -> 4, of which waited for: 1 -> 1; matrix products, arithmetic and copies ran while one was open for 0% -> 0% of each run, Pallas kernels for 29% -> 27%
where the time goes in v5:
time: 50.2 us; the launch traced here: 49.9 us
  starting transfers between devices  23.7 us (47%)
  Pallas kernels  23.6 us (47%)
  waiting for transfers between devices  1.75 us (3%)
  between operations  0.75 us (1%)
    pallas_call x5, Pallas kernels, call(): pl.pallas_call(kernel, out_shape=[jax.ShapeDtypeStruct(s, F32) for s in o...  23.6 us
    ppermute x1, starting transfers between devices, on_device(): odd_in = lax.ppermute(odd_msg, both, lat_odd)  12.2 us
    ppermute x1, starting transfers between devices, on_device(): odd_strip = lax.ppermute(odd_strip, 'lon', lon_odd)  6.99 us
    ppermute x1, starting transfers between devices, on_device(): even_in = lax.ppermute(even_msg, both, lat_even)  2.58 us
    ppermute x1, starting transfers between devices, on_device(): even_strip = lax.ppermute(even_strip, 'lon', lon_even)  1.92 us
    ppermute x1, waiting for transfers between devices, on_device(): odd_in = lax.ppermute(odd_msg, both, lat_odd)  1.74 us
  transfers between devices with their start and end apart: 4, of which 1 were waited for; matrix products, arithmetic and copies ran while one was open for 0% of the time, Pallas kernels for 27%

profile of v5, /device:TPU:59, one launch (start us, length us, event | category | flops | bytes accessed | tf_op | source)
XLA Modules:
  0.0 49.9 jit_solution(7767943675876333593)
XLA Ops:
  0.7 0.1 stack.27.flags
  0.7 2.3 %shard_map.104 = (f32[55,8,256]{2,1,0:T(8,128)S(1)}, f32[55,8,256]{2,1,0:T(8,128)S(1)}) custom-call(s32[5]{0:T(128)S(1)} %stack.27.flags, f32[8,64,128]{2,1,0:T(8,128)} %bitcast.78, f32[8,64,128]{2,1,0:T(8,128)} %bitcast.80, f32[8,64,128]{2,1,0:T(8,128)} %bitcast.82, f32[8,64,128]{2,1,0:T(8,128)} %bitcast.84, f32[8,64,128]{2,1,0:T(8,128)} %bitcast.86, ...), custom_call_target="tpu_custom_call" | custom-call | flops 50000000 | bytes 8000000 | tf_op jit(solution)/shard_map/pallas_call | solution.py:463
  3.0 2.6 %collective-permute-start.1 = (f32[55,8,256]{2,1,0:T(8,128)S(1)}, f32[55,8,256]{2,1,0:T(8,128)S(1)}, u32[]{:S(2)}, u32[]{:S(2)}) collective-permute-start(f32[55,8,256]{2,1,0:T(8,128)S(1)} %get-tuple-element.21), channel_id=1, source_target_pairs={{0,1},{1,0},{2,3},{3,2},{4,5},{5,4},{6,7},{7,6},{8,9},{9,8},{10,11... | collective-permute-start | bytes 1351688 | tf_op jit(solution)/shard_map/ppermute | solution.py:570
  5.6 12.2 %collective-permute-start = (f32[55,8,256]{2,1,0:T(8,128)S(1)}, f32[55,8,256]{2,1,0:T(8,128)S(1)}, u32[]{:S(2)}, u32[]{:S(2)}) collective-permute-start(f32[55,8,256]{2,1,0:T(8,128)S(1)} %get-tuple-element.18.refs_9_), channel_id=1, source_target_pairs={{1,2},{2,1},{3,4},{4,3},{5,6},{6,5},{7,8},{8,7},{9,10},{10,9},{11,... | collective-permute-start | bytes 1351688 | tf_op jit(solution)/shard_map/ppermute | solution.py:569
  17.9 8.8 %shard_map.105 = (f32[8,32,8,256]{3,2,1,0:T(8,128)S(1)}, f32[4,2,8,8,256]{4,3,2,1,0:T(8,128)S(1)}, f32[2,16,8,256]{3,2,1,0:T(8,128)S(1)}, f32[8,32,8,128]{3,2,1,0:T(8,128)S(1)}) custom-call(s32[5]{0:T(128)S(1)} %stack.27.flags, f32[512,128]{1,0:T(8,128)} %bitcast.79, f32[512,128]{1,0:T(8,128)} %bitcast.81, f32[512,128]{1,0:T(8,128)} %bitcast.83, ...), custom_call_target="tpu_custom_call" | custom-call | flops 50000000 | bytes 8000000 | tf_op jit(solution)/shard_map/pallas_call | solution.py:463
  26.7 0.0 collective-permute-done.1.even_msg
  26.7 1.7 %collective-permute-done.odd_msg = f32[55,8,256]{2,1,0:T(8,128)S(1)} collective-permute-done((f32[55,8,256]{2,1,0:T(8,128)S(1)}, f32[55,8,256]{2,1,0:T(8,128)S(1)}, u32[]{:S(2)}, u32[]{:S(2)}) %collective-permute-start) | collective-permute-done | bytes 450592 | tf_op jit(solution)/shard_map/ppermute | solution.py:569
  28.5 1.6 %shard_map.106 = (f32[8,16,8,256]{3,2,1,0:T(8,128)S(1)}, f32[24,8,128]{2,1,0:T(8,128)S(1)}, f32[24,8,128]{2,1,0:T(8,128)S(1)}, f32[2,32,8,256]{3,2,1,0:T(8,128)S(1)}, f32[8,16,8,128]{3,2,1,0:T(8,128)S(1)}) custom-call(s32[5]{0:T(128)S(1)} %stack.27.flags, f32[8,32,8,256]{3,2,1,0:T(8,128)S(1)} %get-tuple-element.20.rows, ...), custom_call_target="tpu_custom_call" | custom-call | flops 50000000 | bytes 8000000 | tf_op jit(solution)/shard_map/pallas_call | solution.py:463
  30.1 7.0 %collective-permute-start.2 = (f32[24,8,128]{2,1,0:T(8,128)S(1)}, f32[24,8,128]{2,1,0:T(8,128)S(1)}, u32[]{:S(2)}, u32[]{:S(2)}) collective-permute-start(f32[24,8,128]{2,1,0:T(8,128)S(1)} %get-tuple-element.28), channel_id=1, source_target_pairs={{0,480},{32,64},{64,32},{96,128},{128,96},{160,192},{192,160},{224... | collective-permute-start | bytes 294920 | tf_op jit(solution)/shard_map/ppermute | solution.py:573
  37.1 1.9 %collective-permute-start.3 = (f32[24,8,128]{2,1,0:T(8,128)S(1)}, f32[24,8,128]{2,1,0:T(8,128)S(1)}, u32[]{:S(2)}, u32[]{:S(2)}) collective-permute-start(f32[24,8,128]{2,1,0:T(8,128)S(1)} %get-tuple-element.29), channel_id=1, source_target_pairs={{0,32},{32,0},{64,96},{96,64},{128,160},{160,128},{192,224},{224,1... | collective-permute-start | bytes 294920 | tf_op jit(solution)/shard_map/ppermute | solution.py:574
  39.0 4.6 %shard_map.107 = (f32[2,32,8,256]{3,2,1,0:T(8,128)S(1)}, f32[8,32,8,128]{3,2,1,0:T(8,128)S(1)}, f32[8,16,8,128]{3,2,1,0:T(8,128)S(1)}) custom-call(s32[5]{0:T(128)S(1)} %stack.27.flags, f32[8,32,8,256]{3,2,1,0:T(8,128)S(1)} %get-tuple-element.20.rows, f32[8,16,8,256]{3,2,1,0:T(8,128)S(1)} %get-tuple-element.24.ghost, ...), custom_call_target="tpu_custom_call" | custom-call | flops 50000000 | bytes 8000000 | tf_op jit(solution)/shard_map/pallas_call | solution.py:463
  43.6 0.0 collective-permute-done.2.odd_strip
  43.6 0.0 collective-permute-done.3.even_strip
  43.6 6.3 %shard_map.108 = (f32[512,128]{1,0:T(8,128)}, f32[512,128]{1,0:T(8,128)}) custom-call(s32[5]{0:T(128)S(1)} %stack.27.flags, f32[8,32,8,128]{3,2,1,0:T(8,128)S(1)} %get-tuple-element.19.base1, f32[8,32,8,128]{3,2,1,0:T(8,128)S(1)} %get-tuple-element.25.base2, f32[8,16,8,128]{3,2,1,0:T(8,128)S(1)} %get-tuple-element.26.beyond1, ...), custom_call_target="tpu_custom_call" | custom-call | flops 50000000 | bytes 8000000 | tf_op jit(solution)/shard_map/pallas_call | solution.py:463
Async XLA Ops:
  3.0 23.7 %collective-permute-start.1 = (f32[55,8,256]{2,1,0:T(8,128)S(1)}, f32[55,8,256]{2,1,0:T(8,128)S(1)}, u32[]{:S(2)}, u32[]{:S(2)}) collective-permute-start(f32[55,8,256]{2,1,0:T(8,128)S(1)} %get-tuple-element.21), channel_id=1, source_target_pairs={{0,1},{1,0},{2,3},{3,2},{4,5},{5,4},{6,7},{7,6},{8,9},{9,8},{10,11... | collective-permute-start | bytes 1351688 | tf_op jit(solution)/shard_map/ppermute | solution.py:570
  5.6 22.8 %collective-permute-start = (f32[55,8,256]{2,1,0:T(8,128)S(1)}, f32[55,8,256]{2,1,0:T(8,128)S(1)}, u32[]{:S(2)}, u32[]{:S(2)}) collective-permute-start(f32[55,8,256]{2,1,0:T(8,128)S(1)} %get-tuple-element.18.refs_9_), channel_id=1, source_target_pairs={{1,2},{2,1},{3,4},{4,3},{5,6},{6,5},{7,8},{8,7},{9,10},{10,9},{11,... | collective-permute-start | bytes 1351688 | tf_op jit(solution)/shard_map/ppermute | solution.py:569
  30.1 13.5 %collective-permute-start.2 = (f32[24,8,128]{2,1,0:T(8,128)S(1)}, f32[24,8,128]{2,1,0:T(8,128)S(1)}, u32[]{:S(2)}, u32[]{:S(2)}) collective-permute-start(f32[24,8,128]{2,1,0:T(8,128)S(1)} %get-tuple-element.28), channel_id=1, source_target_pairs={{0,480},{32,64},{64,32},{96,128},{128,96},{160,192},{192,160},{224... | collective-permute-start | bytes 294920 | tf_op jit(solution)/shard_map/ppermute | solution.py:573
  37.1 6.6 %collective-permute-start.3 = (f32[24,8,128]{2,1,0:T(8,128)S(1)}, f32[24,8,128]{2,1,0:T(8,128)S(1)}, u32[]{:S(2)}, u32[]{:S(2)}) collective-permute-start(f32[24,8,128]{2,1,0:T(8,128)S(1)} %get-tuple-element.29), channel_id=1, source_target_pairs={{0,32},{32,0},{64,96},{96,64},{128,160},{160,128},{192,224},{224,1... | collective-permute-start | bytes 294920 | tf_op jit(solution)/shard_map/ppermute | solution.py:574

commit v6 on v5

--- a/solution.py
+++ b/solution.py
@@ -12,6 +12,7 @@
 PAD = 4
 INNER_FIRST = 4
 OUTER_FIRST = 3
+WAITS_FROM = 6
 LEVELS = 8
 HEIGHT = 32
 WIDTH = 256
@@ -80,7 +81,8 @@
 
 
 def pack_kernel(flags, *refs):
-    args, (odd_msg, even_msg), held, sems = refs[:9], refs[9:11], refs[11:20], refs[20]
+    args, (odd_msg, even_msg, done), held, sems = refs[:9], refs[9:12], refs[12:21], refs[21]
+    done[...] = jnp.zeros((LEVELS, 128), F32)
     copies = []
     for n, (x, y) in enumerate(zip(args, held)):
         for part, start in enumerate((0, 2 * HEIGHT - 16)):
@@ -90,32 +92,36 @@
     for copy in copies:
         copy.wait()
 
-    def fill(part, msg):
-        for k in range(8):
+    odd = flags[0]
+
+    def row(i):
+        for msg, part in ((odd_msg, odd), (even_msg, 1 - odd)):
+            k = jnp.where(part == 1, i, 7 - i)
 
             def at(ref):
                 flat = ref.at[part].reshape(LEVELS * 16, 128)
                 return jnp.concatenate([flat[pl.ds(8 * c + k, LEVELS, stride=16), :] for c in range(2)], axis=1)
 
             for f, x in enumerate(fields(held, at)):
-                to = k - (8 - rows_of(f)) * part
-                if 0 <= to < rows_of(f):
-                    msg[slot(f, to)] = x
-
-    @pl.when(flags[0] == 1)
-    def _():
-        fill(1, odd_msg)
-        fill(0, even_msg)
-
-    @pl.when(flags[0] == 0)
-    def _():
-        fill(0, odd_msg)
-        fill(1, even_msg)
+                n = rows_of(f)
+                msg[slot(f, 0) + jnp.clip(k - (8 - n) * part, 0, n - 1)] = x
+
+    loop(8, row, 4)
+
+
+def add_sides(parts, x, half):
+    east, west = parts
+    for f in range(8):
+        to = 8 * f + 64 * half
+        east = jnp.where(within(to, to + 8), roll(x[f][:, 128:], to + 8), east)
+        to = 8 * f + 64 * (1 - half)
+        west = jnp.where(within(to, to + 8), roll(x[f][:, :128], to), west)
+    return east, west
 
 
 def rows_kernel(flags, *refs):
-    args, _, outs, held, sems = refs[:9], refs[9], refs[10:14], refs[14:23], refs[23]
-    rows, cuts, mid, base = outs
+    args, _, outs, held, sems = refs[:9], refs[9], refs[10:16], refs[16:25], refs[25]
+    rows, east_own, west_own, cuts, mid, base = outs
     copies = [pltpu.make_async_copy(x, y, sems.at[n]) for n, (x, y) in enumerate(zip(args, held))]
     for copy in copies:
         copy.start()
@@ -128,9 +134,19 @@
 
     loop(HEIGHT, one, 4)
 
+    def sides(r):
+        parts = [jnp.zeros((LEVELS, 128), F32)] * 2
+        for half in range(2):
+            idx = r + half * (EXT // 2)
+            j = jnp.clip(idx - HALO, 0, HEIGHT - 1)
+            parts = add_sides(parts, [rows[f, j] for f in range(8)], half)
+        east_own[r], west_own[r] = parts
+
+    loop(EXT // 2, sides, 4)
+
     @pl.when(flags[3] == 1)
     def _():
-        inner_part(rows, cuts, mid, base, *refs[24:])
+        inner_part(rows, cuts, mid, base, *refs[26:])
 
 
 def mirrored(x):
@@ -154,7 +170,7 @@
                 ghost[f, HALO + k - 1] = x
 
 
-def ghost_kernel(flags, rows, odd_msg, even_msg, cuts, mid, ghost, odd_strip, even_strip, result, base, *scratch):
+def ghost_kernel(flags, rows, odd_msg, even_msg, east_own, west_own, cuts, mid, ghost, odd_strip, even_strip, result, base, *scratch):
     is_odd = flags[0] == 1
     for f in range(8):
         n = rows_of(f)
@@ -172,22 +188,13 @@
 
     swap = flags[2] == 1
     for r in range(EXT // 2):
-        east, west = jnp.zeros((LEVELS, 128), F32), jnp.zeros((LEVELS, 128), F32)
-        for half in range(2):
-            idx = r + half * (EXT // 2)
-            for f in range(8):
-                if idx < HALO:
-                    x = ghost[f, idx]
-                elif idx <= TOP:
-                    x = rows[f, idx - HALO]
-                else:
-                    x = ghost[f, idx - HEIGHT]
-                to = 8 * f + 64 * half
-                east = jnp.where(within(to, to + 8), roll(x[:, 128:], to + 8), east)
-                to = 8 * f + 64 * (1 - half)
-                west = jnp.where(within(to, to + 8), roll(x[:, :128], to), west)
-        even_strip[r] = jnp.where(swap, west, east)
-        odd_strip[r] = jnp.where(swap, east, west)
+        parts = [east_own[r], west_own[r]]
+        if r < HALO:
+            parts = add_sides(parts, [ghost[f, r] for f in range(8)], 0)
+        if r >= 2 * HALO:
+            parts = add_sides(parts, [ghost[f, r - HALO] for f in range(8)], 1)
+        even_strip[r] = jnp.where(swap, parts[1], parts[0])
+        odd_strip[r] = jnp.where(swap, parts[0], parts[1])
 
     @pl.when(flags[4] == 1)
     def _():
@@ -300,6 +307,14 @@
     return jnp.where(within(16, 32), roll(x[:, :128], 16), roll(x[:, 128:], 72))
 
 
+def store_edges(base, k, x):
+    x = [edges_of(y) for y in x]
+    is_temp = within(8, 32) | within(56, 80)
+    base[0, k] = jnp.where(is_temp, x[0], roll(x[1], SALT))
+    for f in range(2, 8):
+        base[f - 1, k] = jnp.where(is_temp, x[f], roll(x[f], SALT))
+
+
 def inner_part(rows, cuts, mid, base, s0, s1, s2, s3, s4, cx, cy):
     def own(j):
         for n in TRACERS:
@@ -307,8 +322,7 @@
         x = [rows[f, j] for f in range(8)]
         store_x(cx, HALO + j, *(x[f] for f in XF))
         store_y(cy, HALO + j, *(x[f] for f in YF))
-        for f in range(8):
-            base[f, j] = edges_of(x[f])
+        store_edges(base, j, x)
 
     loop(HEIGHT, own, 4)
     for src, dst, first, count in ((s0, s1, 0, 4), (s1, s2, 4, 3), (s2, s3, 4, 3), (s3, s4, 8, 2)):
@@ -340,18 +354,17 @@
     loop(HALO, near, 4)
     store_y(cy, TOP - HALO, *(rows[f, HEIGHT - HALO - 1] for f in YF))
 
-    def beyond(k):
-        to = jnp.where(k < HALO, k, HEIGHT + k)
+    def beyond(k, north):
+        to = HEIGHT + k if north else k
         x = [ghost[f, k] for f in range(8)]
-        for f in range(8):
-            base[f, k] = edges_of(x[f])
+        store_edges(base, k, x)
         for n in TRACERS:
             qa[n, to] = x[n]
-        turn = top & (k >= HALO)
-        store_x(cx, to, *(jnp.where(turn, roll(x[f], -1), x[f]) for f in XF))
+        store_x(cx, to, *(jnp.where(top, roll(x[f], -1), x[f]) if north else x[f] for f in XF))
         store_y(cy, to, *(x[f] for f in YF))
 
-    loop(2 * HALO, beyond, 4)
+    loop(HALO, lambda k: beyond(k, False), 4)
+    loop(HALO, lambda k: beyond(HALO + k, True), 4)
 
     def one(src, dst, step):
         low = HALO + 2 * step
@@ -400,15 +413,13 @@
         outer_part(flags, rows, ghost, my_cuts, my_mid, result, beyond, *states[:2], cx, cy)
 
 
-def edge_kernel(flags, base1, base2, beyond1, beyond2, odd_strip, even_strip, result1, result2, temp, salt, qa, qb, cx, cy):
+def edge_kernel(flags, base1, base2, beyond1, beyond2, odd_strip, even_strip, result1, result2, temp, salt, qa, qb, cx, cy, temp_out, salt_out, sems):
     top, inner_first, outer_first = flags[1] == 1, flags[3] == 1, flags[4] == 1
     lane = lanes(128)
     from_odd = (lane < 64).astype(jnp.int32) != flags[2]
-    is_temp = within(8, 32) | within(56, 80)
-    beside = within(8, 16) | within(72, 80)
-
-    def both(y):
-        return jnp.where(is_temp, y, roll(y, SALT))
+    beside = within(8, 16) | within(72, 80) | within(32, 40) | within(96, 104)
+    for_temp = within(8, 16) | within(72, 80)
+    place = [within(8 * f, 8 * f + 8) | within(8 * f + 64, 8 * f + 72) for f in range(8)]
 
     def base(f, k):
         return jnp.where(inner_first, base1[f, k], base2[f, k])
@@ -419,14 +430,18 @@
     def assemble(either, k, r, half, turn=None):
         a, b = odd_strip[r], even_strip[r]
         halo = jnp.where(from_odd, a, b) if half == 0 else jnp.where(from_odd, b, a)
-        y = [jnp.where(beside, roll(halo, 8 - 8 * f - 64 * half), either(f, k)) for f in range(8)]
+        again = roll(halo, SALT)
         to = PAD + r + half * (EXT // 2)
-        qa[0, to] = jnp.where(is_temp, y[0], roll(y[1], SALT))
-        x = [both(y[f]) for f in XF]
+        y = jnp.where(for_temp, roll(halo, 8 - 64 * half), roll(halo, SALT - 64 * half))
+        qa[0, to] = jnp.where(beside, y, either(0, k))
+        x = []
+        for f in XF + YF:
+            y = roll(jnp.where(place[f], halo, again), 8 - 8 * f - 64 * half)
+            x.append(jnp.where(beside, y, either(f - 1, k)))
         if turn is not None:
-            x = [jnp.where(turn, roll(z, -1), z) for z in x]
-        store_x(cx, to, *x)
-        store_y(cy, to, *(both(y[f]) for f in YF))
+            x[:3] = [jnp.where(turn, roll(z, -1), z) for z in x[:3]]
+        store_x(cx, to, *x[:3])
+        store_y(cy, to, *x[3:])
 
     def ghosts(k):
         assemble(beyond, k, k, 0)
@@ -438,33 +453,42 @@
         assemble(base, k, HALO + k, 0)
         assemble(base, 2 * HALO + k, k, 1)
 
-    loop(2 * HALO, own, 4)
+    loop(2 * HALO, own, 8)
 
     def two(_):
         for src, dst in ((qa, qb), (qb, qa)):
-            rows_forward(src, dst, cx, cy, 2, EXT - 4, 1, 1, seam=True, pad=PAD)
+            loop(2, lambda i: rows_forward(src, dst, cx, cy, 2 + 22 * i, 22, 1, 1, seam=True, pad=PAD))
 
     loop(STEPS // 2, two)
 
     def patch(j):
         e = qa[0, PAD + HALO + j]
-        for n, out in enumerate((temp, salt)):
+        for n, out in enumerate((temp_out, salt_out)):
             x = jnp.where(outer_first, result1[n, j], result2[n, j])
             w = jnp.where(lane < 8, roll(e, -16 - SALT * n), x[:, :128])
             z = jnp.where(lane >= 120, roll(e, 56 - SALT * n), x[:, 128:])
             for at, y in zip(places(j), (w, z)):
                 out[at, :] = y
 
-    loop(HEIGHT, patch, 8)
-
-
-def call(kernel, outs, args, scratch=(), args_in=None, flags=None):
+    copies = []
+    for i in range(HEIGHT // 8):
+        loop(8, lambda j: patch(8 * i + j), 8)
+        for n, (x, y) in enumerate(((temp_out, temp), (salt_out, salt))):
+            x = x.reshape(LEVELS, 2 * HEIGHT, 128)
+            part = pl.ds(16 * i, 16)
+            copies.append(pltpu.make_async_copy(x.at[:, part, :], y.at[:, part, :], sems.at[n, i]))
+            copies[-1].start()
+    for copy in copies:
+        copy.wait()
+
+
+def call(kernel, outs, args, scratch=(), args_in=None, flags=None, outs_in=VMEM):
     first = [] if flags is None else [flags]
     return pl.pallas_call(
         kernel,
         out_shape=[jax.ShapeDtypeStruct(s, F32) for s in outs],
         in_specs=[SMEM] * len(first) + (args_in or [VMEM] * len(args)),
-        out_specs=[VMEM] * len(outs),
+        out_specs=[outs_in] * len(outs),
         scratch_shapes=[pltpu.VMEM(s, F32) if isinstance(s, tuple) else s for s in scratch],
         compiler_params=PARAMS,
         cost_estimate=COST,
@@ -481,7 +505,7 @@
 STATES = [STATE] * 5 + [(6, EXT, *ROW), (5, EXT, *ROW)]
 OUTER = [STATE] * 2 + [(6, EXT, *ROW), (5, EXT, *ROW)]
 RESULT = (2, HEIGHT, *ROW)
-CUTS, MID, BASE, BEYOND = (STEPS, 2, 8, *ROW), (2, 2 * HALO, *ROW), (8, HEIGHT, *TILE), (8, 2 * HALO, *TILE)
+CUTS, MID, BASE, BEYOND = (STEPS, 2, 8, *ROW), (2, 2 * HALO, *ROW), (7, HEIGHT, *TILE), (7, 2 * HALO, *TILE)
 GHOST = (8, 2 * HALO, *ROW)
 IN_HBM = pl.BlockSpec(memory_space=pltpu.HBM)
 
@@ -491,7 +515,7 @@
     args = [pltpu.with_memory_space_constraint(x.reshape(LEVELS, -1, 128), pltpu.HBM) for x in args]
     return call(
         pack_kernel,
-        [(MESSAGE, *ROW)] * 2,
+        [(MESSAGE, *ROW)] * 2 + [TILE],
         args,
         [*held, pltpu.SemaphoreType.DMA((9, 2))],
         [IN_HBM] * 9,
@@ -504,7 +528,7 @@
     args = [pltpu.with_memory_space_constraint(x, pltpu.HBM) for x in args]
     return call(
         rows_kernel,
-        [(8, HEIGHT, *ROW), CUTS, MID, BASE],
+        [(8, HEIGHT, *ROW), STRIP, STRIP, CUTS, MID, BASE],
         [*args, after],
         [*held, pltpu.SemaphoreType.DMA((9,)), *STATES],
         [IN_HBM] * 9 + [VMEM],
@@ -512,11 +536,11 @@
     )
 
 
-def fill_ghost(flags, rows, odd_in, even_in, cuts, mid):
+def fill_ghost(flags, *args):
     return call(
         ghost_kernel,
         [GHOST, STRIP, STRIP, RESULT, BEYOND],
-        [rows, odd_in, even_in, cuts, mid],
+        args,
         OUTER,
         flags=flags,
     )
@@ -535,10 +559,12 @@
 def edge(flags, *args):
     return call(
         edge_kernel,
-        [FLAT] * 2,
+        [(LEVELS, 2 * HEIGHT, 128)] * 2,
         args,
-        [(1, EDGE_DEPTH, *TILE)] * 2 + [(6, EDGE_DEPTH, *TILE), (5, EDGE_DEPTH, *TILE)],
+        [(1, EDGE_DEPTH, *TILE)] * 2
+        + [(6, EDGE_DEPTH, *TILE), (5, EDGE_DEPTH, *TILE), FLAT, FLAT, pltpu.SemaphoreType.DMA((2, HEIGHT // 8))],
         flags=flags,
+        outs_in=IN_HBM,
     )
 
 
@@ -546,8 +572,9 @@
     lon, lat = lax.axis_index("lon"), lax.axis_index("lat")
     top = (lat == lat_count - 1).astype(jnp.int32)
     place = lon % 8
-    inner_first = (place < INNER_FIRST).astype(jnp.int32)
-    outer_first = (place < OUTER_FIRST).astype(jnp.int32) * (1 - top)
+    waits = (lat == lat_count - 2) & (place >= WAITS_FROM)
+    inner_first = ((place < INNER_FIRST) | waits | (lat == lat_count - 1)).astype(jnp.int32)
+    outer_first = (((place < OUTER_FIRST) & (lat < lat_count - 2)) | waits).astype(jnp.int32)
     flags = jnp.stack([lat % 2, top, lon % 2, inner_first, outer_first])
     flat = [level_major(x) for x in args]
 
@@ -565,11 +592,13 @@
     lon_even = [(i, i ^ 1) for i in lons]
     lon_odd = [(i, (i + 1 if i % 2 else i - 1) % lon_count) for i in lons]
     both = ("lon", "lat")
-    odd_msg, even_msg = pack(flags, flat)
+    odd_msg, even_msg, packed = pack(flags, flat)
     odd_in = lax.ppermute(odd_msg, both, lat_odd)
     even_in = lax.ppermute(even_msg, both, lat_even)
-    rows, cuts, mid, base1 = transpose(flags, flat, odd_msg)
-    ghost, odd_strip, even_strip, result1, beyond1 = fill_ghost(flags, rows, odd_in, even_in, cuts, mid)
+    rows, east, west, cuts, mid, base1 = transpose(flags, flat, packed)
+    ghost, odd_strip, even_strip, result1, beyond1 = fill_ghost(
+        flags, rows, odd_in, even_in, east, west, cuts, mid
+    )
     odd_strip = lax.ppermute(odd_strip, "lon", lon_odd)
     even_strip = lax.ppermute(even_strip, "lon", lon_even)
     result2, base2, beyond2 = late(flags, rows, ghost, cuts, mid)

time: 50.2 us -> 48.4 us (0.964)
  the two profiles are of different devices: /device:TPU:59 before, /device:TPU:58 now
where the time goes in v6:
time: 48.4 us; the launch traced here: 48.1 us
  Pallas kernels  24 us (50%)
  starting transfers between devices  23.3 us (48%)
  between operations  0.77 us (2%)
    pallas_call x5, Pallas kernels, call(): pl.pallas_call(kernel, out_shape=[jax.ShapeDtypeStruct(s, F32) for s in o...  24 us
    ppermute x1, starting transfers between devices, on_device(): even_in = lax.ppermute(even_msg, both, lat_even)  11.3 us
    ppermute x1, starting transfers between devices, on_device(): odd_strip = lax.ppermute(odd_strip, 'lon', lon_odd)  7.36 us
    ppermute x1, starting transfers between devices, on_device(): odd_in = lax.ppermute(odd_msg, both, lat_odd)  2.7 us
    ppermute x1, starting transfers between devices, on_device(): even_strip = lax.ppermute(even_strip, 'lon', lon_even)  1.92 us
  transfers between devices with their start and end apart: 4, of which 0 were waited for; matrix products, arithmetic and copies ran while one was open for 0% of the time, Pallas kernels for 32%

profile of v6, /device:TPU:58, one launch (start us, length us, event | category | flops | bytes accessed | tf_op | source)
XLA Modules:
  0.0 48.1 jit_solution(5470949511483662708)
XLA Ops:
  0.7 0.1 stack.35.flags
  0.8 2.4 %shard_map.104 = (f32[55,8,256]{2,1,0:T(8,128)S(1)}, f32[55,8,256]{2,1,0:T(8,128)S(1)}, f32[8,128]{1,0:T(8,128)S(1)}) custom-call(s32[5]{0:T(128)S(1)} %stack.35.flags, f32[8,64,128]{2,1,0:T(8,128)} %bitcast.78, f32[8,64,128]{2,1,0:T(8,128)} %bitcast.80, f32[8,64,128]{2,1,0:T(8,128)} %bitcast.82, f32[8,64,128]{2,1,0:T(8,128)} %bitcast.84, ...), custom_call_target="tpu_custom_call" | custom-call | flops 50000000 | bytes 8000000 | tf_op jit(solution)/shard_map/pallas_call | solution.py:487
  3.2 2.7 %collective-permute-start = (f32[55,8,256]{2,1,0:T(8,128)S(1)}, f32[55,8,256]{2,1,0:T(8,128)S(1)}, u32[]{:S(2)}, u32[]{:S(2)}) collective-permute-start(f32[55,8,256]{2,1,0:T(8,128)S(1)} %get-tuple-element.24), channel_id=1, source_target_pairs={{1,2},{2,1},{3,4},{4,3},{5,6},{6,5},{7,8},{8,7},{9,10},{10,9},{11,... | collective-permute-start | bytes 1351688 | tf_op jit(solution)/shard_map/ppermute | solution.py:596
  5.9 11.3 %collective-permute-start.1 = (f32[55,8,256]{2,1,0:T(8,128)S(1)}, f32[55,8,256]{2,1,0:T(8,128)S(1)}, u32[]{:S(2)}, u32[]{:S(2)}) collective-permute-start(f32[55,8,256]{2,1,0:T(8,128)S(1)} %get-tuple-element.25), channel_id=1, source_target_pairs={{0,1},{1,0},{2,3},{3,2},{4,5},{5,4},{6,7},{7,6},{8,9},{9,8},{10,11... | collective-permute-start | bytes 1351688 | tf_op jit(solution)/shard_map/ppermute | solution.py:597
  17.2 10.6 %shard_map.105 = (f32[8,32,8,256]{3,2,1,0:T(8,128)S(1)}, f32[24,8,128]{2,1,0:T(8,128)S(1)}, f32[24,8,128]{2,1,0:T(8,128)S(1)}, f32[4,2,8,8,256]{4,3,2,1,0:T(8,12...) custom-call(s32[5]{0:T(128)S(1)} %stack.35.flags, f32[512,128]{1,0:T(8,128)} %bitcast.79, ...), custom_call_target="tpu_custom_call" | custom-call | flops 50000000 | bytes 8000000 | tf_op jit(solution)/shard_map/pallas_call | solution.py:487
  27.8 0.0 collective-permute-done.odd_msg
  27.8 0.0 collective-permute-done.1.even_msg
  27.8 0.9 %shard_map.106 = (f32[8,16,8,256]{3,2,1,0:T(8,128)S(1)}, f32[24,8,128]{2,1,0:T(8,128)S(1)}, f32[24,8,128]{2,1,0:T(8,128)S(1)}, f32[2,32,8,256]{3,2,1,0:T(8,128)S(1)}, f32[7,16,8,128]{3,2,1,0:T(8,128)S(1)}) custom-call(s32[5]{0:T(128)S(1)} %stack.35.flags, f32[8,32,8,256]{3,2,1,0:T(8,128)S(1)} %get-tuple-element.23.rows, ...), custom_call_target="tpu_custom_call" | custom-call | flops 50000000 | bytes 8000000 | tf_op jit(solution)/shard_map/pallas_call | solution.py:487
  28.8 7.4 %collective-permute-start.2 = (f32[24,8,128]{2,1,0:T(8,128)S(1)}, f32[24,8,128]{2,1,0:T(8,128)S(1)}, u32[]{:S(2)}, u32[]{:S(2)}) collective-permute-start(f32[24,8,128]{2,1,0:T(8,128)S(1)} %get-tuple-element.34), channel_id=1, source_target_pairs={{0,480},{32,64},{64,32},{96,128},{128,96},{160,192},{192,160},{224... | collective-permute-start | bytes 294920 | tf_op jit(solution)/shard_map/ppermute | solution.py:602
  36.1 1.9 %collective-permute-start.3 = (f32[24,8,128]{2,1,0:T(8,128)S(1)}, f32[24,8,128]{2,1,0:T(8,128)S(1)}, u32[]{:S(2)}, u32[]{:S(2)}) collective-permute-start(f32[24,8,128]{2,1,0:T(8,128)S(1)} %get-tuple-element.35), channel_id=1, source_target_pairs={{0,32},{32,0},{64,96},{96,64},{128,160},{160,128},{192,224},{224,1... | collective-permute-start | bytes 294920 | tf_op jit(solution)/shard_map/ppermute | solution.py:603
  38.1 4.8 %shard_map.107 = (f32[2,32,8,256]{3,2,1,0:T(8,128)S(1)}, f32[7,32,8,128]{3,2,1,0:T(8,128)S(1)}, f32[7,16,8,128]{3,2,1,0:T(8,128)S(1)}) custom-call(s32[5]{0:T(128)S(1)} %stack.35.flags, f32[8,32,8,256]{3,2,1,0:T(8,128)S(1)} %get-tuple-element.23.rows, f32[8,16,8,256]{3,2,1,0:T(8,128)S(1)} %get-tuple-element.30.ghost, ...), custom_call_target="tpu_custom_call" | custom-call | flops 50000000 | bytes 8000000 | tf_op jit(solution)/shard_map/pallas_call | solution.py:487
  42.9 0.0 collective-permute-done.2.odd_strip
  42.9 0.0 collective-permute-done.3.even_strip
  42.9 5.2 %shard_map.108 = (f32[8,64,128]{2,1,0:T(8,128)}, f32[8,64,128]{2,1,0:T(8,128)}) custom-call(s32[5]{0:T(128)S(1)} %stack.35.flags, f32[7,32,8,128]{3,2,1,0:T(8,128)S(1)} %get-tuple-element.22.base1, f32[7,32,8,128]{3,2,1,0:T(8,128)S(1)} %get-tuple-element.31.base2, f32[7,16,8,128]{3,2,1,0:T(8,128)S(1)} %get-tuple-element.32.beyond1, ...), custom_call_target="tpu_custom_call" | custom-call | flops 50000000 | bytes 8000000 | tf_op jit(solution)/shard_map/pallas_call | solution.py:487
Async XLA Ops:
  3.2 24.6 %collective-permute-start = (f32[55,8,256]{2,1,0:T(8,128)S(1)}, f32[55,8,256]{2,1,0:T(8,128)S(1)}, u32[]{:S(2)}, u32[]{:S(2)}) collective-permute-start(f32[55,8,256]{2,1,0:T(8,128)S(1)} %get-tuple-element.24), channel_id=1, source_target_pairs={{1,2},{2,1},{3,4},{4,3},{5,6},{6,5},{7,8},{8,7},{9,10},{10,9},{11,... | collective-permute-start | bytes 1351688 | tf_op jit(solution)/shard_map/ppermute | solution.py:596
  5.9 21.9 %collective-permute-start.1 = (f32[55,8,256]{2,1,0:T(8,128)S(1)}, f32[55,8,256]{2,1,0:T(8,128)S(1)}, u32[]{:S(2)}, u32[]{:S(2)}) collective-permute-start(f32[55,8,256]{2,1,0:T(8,128)S(1)} %get-tuple-element.25), channel_id=1, source_target_pairs={{0,1},{1,0},{2,3},{3,2},{4,5},{5,4},{6,7},{7,6},{8,9},{9,8},{10,11... | collective-permute-start | bytes 1351688 | tf_op jit(solution)/shard_map/ppermute | solution.py:597
  28.8 14.1 %collective-permute-start.2 = (f32[24,8,128]{2,1,0:T(8,128)S(1)}, f32[24,8,128]{2,1,0:T(8,128)S(1)}, u32[]{:S(2)}, u32[]{:S(2)}) collective-permute-start(f32[24,8,128]{2,1,0:T(8,128)S(1)} %get-tuple-element.34), channel_id=1, source_target_pairs={{0,480},{32,64},{64,32},{96,128},{128,96},{160,192},{192,160},{224... | collective-permute-start | bytes 294920 | tf_op jit(solution)/shard_map/ppermute | solution.py:602
  36.1 6.8 %collective-permute-start.3 = (f32[24,8,128]{2,1,0:T(8,128)S(1)}, f32[24,8,128]{2,1,0:T(8,128)S(1)}, u32[]{:S(2)}, u32[]{:S(2)}) collective-permute-start(f32[24,8,128]{2,1,0:T(8,128)S(1)} %get-tuple-element.35), channel_id=1, source_target_pairs={{0,32},{32,0},{64,96},{96,64},{128,160},{160,128},{192,224},{224,1... | collective-permute-start | bytes 294920 | tf_op jit(solution)/shard_map/ppermute | solution.py:603

commit v7 on v6

--- a/solution.py
+++ b/solution.py
@@ -12,7 +12,6 @@
 PAD = 4
 INNER_FIRST = 4
 OUTER_FIRST = 3
-WAITS_FROM = 6
 LEVELS = 8
 HEIGHT = 32
 WIDTH = 256
@@ -198,7 +197,11 @@
 
     @pl.when(flags[4] == 1)
     def _():
-        outer_part(flags, rows, ghost, cuts, mid, result, base, *scratch)
+        outer_part(flags, rows, ghost, cuts, mid, result, *scratch)
+
+    @pl.when(flags[5] == 1)
+    def _():
+        sides_beyond(ghost, base)
 
 
 def minmod(p, t):
@@ -340,7 +343,11 @@
         loop(2 * HALO, out, 4)
 
 
-def outer_part(flags, rows, ghost, cuts, mid, result, base, qa, qb, cx, cy):
+def sides_beyond(ghost, base):
+    loop(2 * HALO, lambda k: store_edges(base, k, [ghost[f, k] for f in range(8)]), 4)
+
+
+def outer_part(flags, rows, ghost, cuts, mid, result, qa, qb, cx, cy):
     top = flags[1] == 1
 
     def near(k):
@@ -357,7 +364,6 @@
     def beyond(k, north):
         to = HEIGHT + k if north else k
         x = [ghost[f, k] for f in range(8)]
-        store_edges(base, k, x)
         for n in TRACERS:
             qa[n, to] = x[n]
         store_x(cx, to, *(jnp.where(top, roll(x[f], -1), x[f]) if north else x[f] for f in XF))
@@ -410,11 +416,15 @@
 
             loop(8, copy, 4)
 
-        outer_part(flags, rows, ghost, my_cuts, my_mid, result, beyond, *states[:2], cx, cy)
+        outer_part(flags, rows, ghost, my_cuts, my_mid, result, *states[:2], cx, cy)
+
+    @pl.when(flags[5] == 0)
+    def _():
+        sides_beyond(ghost, beyond)
 
 
 def edge_kernel(flags, base1, base2, beyond1, beyond2, odd_strip, even_strip, result1, result2, temp, salt, qa, qb, cx, cy, temp_out, salt_out, sems):
-    top, inner_first, outer_first = flags[1] == 1, flags[3] == 1, flags[4] == 1
+    top, inner_first, outer_first, sides_first = (flags[n] == 1 for n in (1, 3, 4, 5))
     lane = lanes(128)
     from_odd = (lane < 64).astype(jnp.int32) != flags[2]
     beside = within(8, 16) | within(72, 80) | within(32, 40) | within(96, 104)
@@ -425,7 +435,7 @@
         return jnp.where(inner_first, base1[f, k], base2[f, k])
 
     def beyond(f, k):
-        return jnp.where(outer_first, beyond1[f, k], beyond2[f, k])
+        return jnp.where(sides_first, beyond1[f, k], beyond2[f, k])
 
     def assemble(either, k, r, half, turn=None):
         a, b = odd_strip[r], even_strip[r]
@@ -572,10 +582,10 @@
     lon, lat = lax.axis_index("lon"), lax.axis_index("lat")
     top = (lat == lat_count - 1).astype(jnp.int32)
     place = lon % 8
-    waits = (lat == lat_count - 2) & (place >= WAITS_FROM)
-    inner_first = ((place < INNER_FIRST) | waits | (lat == lat_count - 1)).astype(jnp.int32)
-    outer_first = (((place < OUTER_FIRST) & (lat < lat_count - 2)) | waits).astype(jnp.int32)
-    flags = jnp.stack([lat % 2, top, lon % 2, inner_first, outer_first])
+    inner_first = ((place < INNER_FIRST) | (lat >= lat_count - 2)).astype(jnp.int32)
+    outer_first = ((place < OUTER_FIRST) & (lat < lat_count - 2)).astype(jnp.int32)
+    sides_first = (place < INNER_FIRST).astype(jnp.int32)
+    flags = jnp.stack([lat % 2, top, lon % 2, inner_first, outer_first, sides_first])
     flat = [level_major(x) for x in args]
 
     def index(i, j):

time: 48.4 us -> 45.8 us (0.946)
  the two profiles are of different devices: /device:TPU:58 before, /device:TPU:59 now
where the time goes in v7:
time: 45.8 us; the launch traced here: 45.5 us
  Pallas kernels  24.4 us (53%)
  starting transfers between devices  20.3 us (44%)
  between operations  0.76 us (2%)
    pallas_call x5, Pallas kernels, call(): pl.pallas_call(kernel, out_shape=[jax.ShapeDtypeStruct(s, F32) for s in o...  24.4 us
    ppermute x1, starting transfers between devices, on_device(): odd_in = lax.ppermute(odd_msg, both, lat_odd)  12.2 us
    ppermute x1, starting transfers between devices, on_device(): odd_strip = lax.ppermute(odd_strip, 'lon', lon_odd)  4.2 us
    ppermute x1, starting transfers between devices, on_device(): even_in = lax.ppermute(even_msg, both, lat_even)  1.92 us
    ppermute x1, starting transfers between devices, on_device(): even_strip = lax.ppermute(even_strip, 'lon', lon_even)  1.92 us
  transfers between devices with their start and end apart: 4, of which 0 were waited for; matrix products, arithmetic and copies ran while one was open for 0% of the time, Pallas kernels for 33%

profile of v7, /device:TPU:59, one launch (start us, length us, event | category | flops | bytes accessed | tf_op | source)
XLA Modules:
  0.0 45.5 jit_solution(14206640873423246891)
XLA Ops:
  0.7 0.1 stack.43.flags
  0.8 2.4 %shard_map.104 = (f32[55,8,256]{2,1,0:T(8,128)S(1)}, f32[55,8,256]{2,1,0:T(8,128)S(1)}, f32[8,128]{1,0:T(8,128)S(1)}) custom-call(s32[6]{0:T(128)S(1)} %stack.43.flags, f32[8,64,128]{2,1,0:T(8,128)} %bitcast.79, f32[8,64,128]{2,1,0:T(8,128)} %bitcast.81, f32[8,64,128]{2,1,0:T(8,128)} %bitcast.83, f32[8,64,128]{2,1,0:T(8,128)} %bitcast.85, ...), custom_call_target="tpu_custom_call" | custom-call | flops 50000000 | bytes 8000000 | tf_op jit(solution)/shard_map/pallas_call | solution.py:497
  3.2 12.2 %collective-permute-start = (f32[55,8,256]{2,1,0:T(8,128)S(1)}, f32[55,8,256]{2,1,0:T(8,128)S(1)}, u32[]{:S(2)}, u32[]{:S(2)}) collective-permute-start(f32[55,8,256]{2,1,0:T(8,128)S(1)} %get-tuple-element.24), channel_id=1, source_target_pairs={{1,2},{2,1},{3,4},{4,3},{5,6},{6,5},{7,8},{8,7},{9,10},{10,9},{11,... | collective-permute-start | bytes 1351688 | tf_op jit(solution)/shard_map/ppermute | solution.py:606
  15.4 1.9 %collective-permute-start.1 = (f32[55,8,256]{2,1,0:T(8,128)S(1)}, f32[55,8,256]{2,1,0:T(8,128)S(1)}, u32[]{:S(2)}, u32[]{:S(2)}) collective-permute-start(f32[55,8,256]{2,1,0:T(8,128)S(1)} %get-tuple-element.25), channel_id=1, source_target_pairs={{0,1},{1,0},{2,3},{3,2},{4,5},{5,4},{6,7},{7,6},{8,9},{9,8},{10,11... | collective-permute-start | bytes 1351688 | tf_op jit(solution)/shard_map/ppermute | solution.py:607
  17.3 10.6 %shard_map.105 = (f32[8,32,8,256]{3,2,1,0:T(8,128)S(1)}, f32[24,8,128]{2,1,0:T(8,128)S(1)}, f32[24,8,128]{2,1,0:T(8,128)S(1)}, f32[4,2,8,8,256]{4,3,2,1,0:T(8,12...) custom-call(s32[6]{0:T(128)S(1)} %stack.43.flags, f32[512,128]{1,0:T(8,128)} %bitcast.80, ...), custom_call_target="tpu_custom_call" | custom-call | flops 50000000 | bytes 8000000 | tf_op jit(solution)/shard_map/pallas_call | solution.py:497
  28.0 0.0 collective-permute-done.odd_msg
  28.0 0.0 collective-permute-done.1.even_msg
  28.0 1.9 %shard_map.106 = (f32[8,16,8,256]{3,2,1,0:T(8,128)S(1)}, f32[24,8,128]{2,1,0:T(8,128)S(1)}, f32[24,8,128]{2,1,0:T(8,128)S(1)}, f32[2,32,8,256]{3,2,1,0:T(8,128)S(1)}, f32[7,16,8,128]{3,2,1,0:T(8,128)S(1)}) custom-call(s32[6]{0:T(128)S(1)} %stack.43.flags, f32[8,32,8,256]{3,2,1,0:T(8,128)S(1)} %get-tuple-element.23.rows, ...), custom_call_target="tpu_custom_call" | custom-call | flops 50000000 | bytes 8000000 | tf_op jit(solution)/shard_map/pallas_call | solution.py:497
  29.9 4.2 %collective-permute-start.2 = (f32[24,8,128]{2,1,0:T(8,128)S(1)}, f32[24,8,128]{2,1,0:T(8,128)S(1)}, u32[]{:S(2)}, u32[]{:S(2)}) collective-permute-start(f32[24,8,128]{2,1,0:T(8,128)S(1)} %get-tuple-element.34), channel_id=1, source_target_pairs={{0,480},{32,64},{64,32},{96,128},{128,96},{160,192},{192,160},{224... | collective-permute-start | bytes 294920 | tf_op jit(solution)/shard_map/ppermute | solution.py:612
  34.1 1.9 %collective-permute-start.3 = (f32[24,8,128]{2,1,0:T(8,128)S(1)}, f32[24,8,128]{2,1,0:T(8,128)S(1)}, u32[]{:S(2)}, u32[]{:S(2)}) collective-permute-start(f32[24,8,128]{2,1,0:T(8,128)S(1)} %get-tuple-element.35), channel_id=1, source_target_pairs={{0,32},{32,0},{64,96},{96,64},{128,160},{160,128},{192,224},{224,1... | collective-permute-start | bytes 294920 | tf_op jit(solution)/shard_map/ppermute | solution.py:613
  36.0 4.3 %shard_map.107 = (f32[2,32,8,256]{3,2,1,0:T(8,128)S(1)}, f32[7,32,8,128]{3,2,1,0:T(8,128)S(1)}, f32[7,16,8,128]{3,2,1,0:T(8,128)S(1)}) custom-call(s32[6]{0:T(128)S(1)} %stack.43.flags, f32[8,32,8,256]{3,2,1,0:T(8,128)S(1)} %get-tuple-element.23.rows, f32[8,16,8,256]{3,2,1,0:T(8,128)S(1)} %get-tuple-element.30.ghost, ...), custom_call_target="tpu_custom_call" | custom-call | flops 50000000 | bytes 8000000 | tf_op jit(solution)/shard_map/pallas_call | solution.py:497
  40.3 0.0 collective-permute-done.2.odd_strip
  40.3 0.0 collective-permute-done.3.even_strip
  40.3 5.2 %shard_map.108 = (f32[8,64,128]{2,1,0:T(8,128)}, f32[8,64,128]{2,1,0:T(8,128)}) custom-call(s32[6]{0:T(128)S(1)} %stack.43.flags, f32[7,32,8,128]{3,2,1,0:T(8,128)S(1)} %get-tuple-element.22.base1, f32[7,32,8,128]{3,2,1,0:T(8,128)S(1)} %get-tuple-element.31.base2, f32[7,16,8,128]{3,2,1,0:T(8,128)S(1)} %get-tuple-element.32.beyond1, ...), custom_call_target="tpu_custom_call" | custom-call | flops 50000000 | bytes 8000000 | tf_op jit(solution)/shard_map/pallas_call | solution.py:497
Async XLA Ops:
  3.2 24.8 %collective-permute-start = (f32[55,8,256]{2,1,0:T(8,128)S(1)}, f32[55,8,256]{2,1,0:T(8,128)S(1)}, u32[]{:S(2)}, u32[]{:S(2)}) collective-permute-start(f32[55,8,256]{2,1,0:T(8,128)S(1)} %get-tuple-element.24), channel_id=1, source_target_pairs={{1,2},{2,1},{3,4},{4,3},{5,6},{6,5},{7,8},{8,7},{9,10},{10,9},{11,... | collective-permute-start | bytes 1351688 | tf_op jit(solution)/shard_map/ppermute | solution.py:606
  15.4 12.6 %collective-permute-start.1 = (f32[55,8,256]{2,1,0:T(8,128)S(1)}, f32[55,8,256]{2,1,0:T(8,128)S(1)}, u32[]{:S(2)}, u32[]{:S(2)}) collective-permute-start(f32[55,8,256]{2,1,0:T(8,128)S(1)} %get-tuple-element.25), channel_id=1, source_target_pairs={{0,1},{1,0},{2,3},{3,2},{4,5},{5,4},{6,7},{7,6},{8,9},{9,8},{10,11... | collective-permute-start | bytes 1351688 | tf_op jit(solution)/shard_map/ppermute | solution.py:607
  29.9 10.4 %collective-permute-start.2 = (f32[24,8,128]{2,1,0:T(8,128)S(1)}, f32[24,8,128]{2,1,0:T(8,128)S(1)}, u32[]{:S(2)}, u32[]{:S(2)}) collective-permute-start(f32[24,8,128]{2,1,0:T(8,128)S(1)} %get-tuple-element.34), channel_id=1, source_target_pairs={{0,480},{32,64},{64,32},{96,128},{128,96},{160,192},{192,160},{224... | collective-permute-start | bytes 294920 | tf_op jit(solution)/shard_map/ppermute | solution.py:612
  34.1 6.2 %collective-permute-start.3 = (f32[24,8,128]{2,1,0:T(8,128)S(1)}, f32[24,8,128]{2,1,0:T(8,128)S(1)}, u32[]{:S(2)}, u32[]{:S(2)}) collective-permute-start(f32[24,8,128]{2,1,0:T(8,128)S(1)} %get-tuple-element.35), channel_id=1, source_target_pairs={{0,32},{32,0},{64,96},{96,64},{128,160},{160,128},{192,224},{224,1... | collective-permute-start | bytes 294920 | tf_op jit(solution)/shard_map/ppermute | solution.py:613

commit v8 on v7

--- a/solution.py
+++ b/solution.py
@@ -86,26 +86,39 @@
     for n, (x, y) in enumerate(zip(args, held)):
         for part, start in enumerate((0, 2 * HEIGHT - 16)):
             copies.append(pltpu.make_async_copy(x.at[:, pl.ds(start, 16), :], y.at[part], sems.at[n, part]))
-    for copy in copies:
-        copy.start()
-    for copy in copies:
-        copy.wait()
-
+    for n in (0, 1, 2, 4, 5, 7, 3, 6, 8):
+        copies[2 * n].start()
+        copies[2 * n + 1].start()
     odd = flags[0]
 
-    def row(i):
-        for msg, part in ((odd_msg, odd), (even_msg, 1 - odd)):
-            k = jnp.where(part == 1, i, 7 - i)
-
-            def at(ref):
-                flat = ref.at[part].reshape(LEVELS * 16, 128)
-                return jnp.concatenate([flat[pl.ds(8 * c + k, LEVELS, stride=16), :] for c in range(2)], axis=1)
-
-            for f, x in enumerate(fields(held, at)):
-                n = rows_of(f)
-                msg[slot(f, 0) + jnp.clip(k - (8 - n) * part, 0, n - 1)] = x
-
-    loop(8, row, 4)
+    def put(group, make):
+        def row(i):
+            for msg, part in ((odd_msg, odd), (even_msg, 1 - odd)):
+                k = jnp.where(part == 1, i, 7 - i)
+
+                def at(n):
+                    flat = held[n].at[part].reshape(LEVELS * 16, 128)
+                    return jnp.concatenate([flat[pl.ds(8 * c + k, LEVELS, stride=16), :] for c in range(2)], axis=1)
+
+                for f, x in zip(group, make(at)):
+                    n = rows_of(f)
+                    msg[slot(f, 0) + jnp.clip(k - (8 - n) * part, 0, n - 1)] = x
+
+        loop(8, row, 4)
+
+    def face(at, c, slope, mask):
+        wet = at(mask).astype(F32)
+        return at(c) * wet, at(4) * wet, at(slope)
+
+    for group, needs, make in (
+        (TRACERS, (0, 1), lambda at: (at(0), at(1))),
+        (XF, (2, 4, 5, 7), lambda at: face(at, 2, 5, 7)),
+        (YF, (3, 6, 8), lambda at: face(at, 3, 6, 8)),
+    ):
+        for n in needs:
+            copies[2 * n].wait()
+            copies[2 * n + 1].wait()
+        put(group, make)
 
 
 def add_sides(parts, x, half):
@@ -169,7 +182,7 @@
                 ghost[f, HALO + k - 1] = x
 
 
-def ghost_kernel(flags, rows, odd_msg, even_msg, east_own, west_own, cuts, mid, ghost, odd_strip, even_strip, result, base, *scratch):
+def ghost_kernel(flags, rows, odd_msg, even_msg, east_own, west_own, cuts, mid, ghost, odd_strip, even_strip, result, base, q, cx, cy, qa, qb):
     is_odd = flags[0] == 1
     for f in range(8):
         n = rows_of(f)
@@ -195,13 +208,24 @@
         even_strip[r] = jnp.where(swap, parts[1], parts[0])
         odd_strip[r] = jnp.where(swap, parts[0], parts[1])
 
-    @pl.when(flags[4] == 1)
-    def _():
-        outer_part(flags, rows, ghost, cuts, mid, result, *scratch)
-
     @pl.when(flags[5] == 1)
     def _():
         sides_beyond(ghost, base)
+        outer_prepare(flags, rows, ghost, q, cx, cy)
+
+    @pl.when(flags[4] == 1)
+    def _():
+        start_from(q, qa)
+        outer_steps(cuts, mid, result, qa, qb, cx, cy)
+
+
+def start_from(q, qa):
+    def copy(k):
+        for n in TRACERS:
+            qa[n, k] = q[n, k]
+            qa[n, EXT - 12 + k] = q[n, EXT - 12 + k]
+
+    loop(12, copy, 4)
 
 
 def minmod(p, t):
@@ -347,14 +371,14 @@
     loop(2 * HALO, lambda k: store_edges(base, k, [ghost[f, k] for f in range(8)]), 4)
 
 
-def outer_part(flags, rows, ghost, cuts, mid, result, qa, qb, cx, cy):
+def outer_prepare(flags, rows, ghost, q, cx, cy):
     top = flags[1] == 1
 
     def near(k):
         for start in (0, HEIGHT - HALO):
             j = start + k
             for n in TRACERS:
-                qa[n, HALO + j] = rows[n, j]
+                q[n, HALO + j] = rows[n, j]
             store_x(cx, HALO + j, *(rows[f, j] for f in XF))
             store_y(cy, HALO + j, *(rows[f, j] for f in YF))
 
@@ -365,13 +389,15 @@
         to = HEIGHT + k if north else k
         x = [ghost[f, k] for f in range(8)]
         for n in TRACERS:
-            qa[n, to] = x[n]
+            q[n, to] = x[n]
         store_x(cx, to, *(jnp.where(top, roll(x[f], -1), x[f]) if north else x[f] for f in XF))
         store_y(cy, to, *(x[f] for f in YF))
 
     loop(HALO, lambda k: beyond(k, False), 4)
     loop(HALO, lambda k: beyond(HALO + k, True), 4)
 
+
+def outer_steps(cuts, mid, result, qa, qb, cx, cy):
     def one(src, dst, step):
         low = HALO + 2 * step
         for n in TRACERS:
@@ -396,15 +422,23 @@
     loop(HALO, out, 2)
 
 
-def late_kernel(flags, rows, ghost, cuts, mid, result, base, beyond, my_cuts, my_mid, *scratch):
-    states, (cx, cy) = scratch[:5], scratch[5:]
+def late_kernel(flags, rows, ghost, cuts, mid, q, cx, cy, result, base, beyond, my_cuts, my_mid, *scratch):
+    states, (my_cx, my_cy) = scratch[:5], scratch[5:]
+    qa, qb = states[:2]
 
     @pl.when(flags[3] == 0)
     def _():
-        inner_part(rows, my_cuts, my_mid, base, *states, cx, cy)
-
-    @pl.when(flags[4] == 0)
+        inner_part(rows, my_cuts, my_mid, base, *states, my_cx, my_cy)
+
+    @pl.when((flags[5] == 1) & (flags[4] == 0))
     def _():
+        start_from(q, qa)
+        outer_steps(cuts, mid, result, qa, qb, cx, cy)
+
+    @pl.when(flags[5] == 0)
+    def _():
+        sides_beyond(ghost, beyond)
+
         @pl.when(flags[3] == 1)
         def _():
             def copy(k):
@@ -416,11 +450,8 @@
 
             loop(8, copy, 4)
 
-        outer_part(flags, rows, ghost, my_cuts, my_mid, result, *states[:2], cx, cy)
-
-    @pl.when(flags[5] == 0)
-    def _():
-        sides_beyond(ghost, beyond)
+        outer_prepare(flags, rows, ghost, qa, my_cx, my_cy)
+        outer_steps(my_cuts, my_mid, result, qa, qb, my_cx, my_cy)
 
 
 def edge_kernel(flags, base1, base2, beyond1, beyond2, odd_strip, even_strip, result1, result2, temp, salt, qa, qb, cx, cy, temp_out, salt_out, sems):
@@ -513,7 +544,7 @@
 
 
 STATES = [STATE] * 5 + [(6, EXT, *ROW), (5, EXT, *ROW)]
-OUTER = [STATE] * 2 + [(6, EXT, *ROW), (5, EXT, *ROW)]
+OUTER = [STATE, (6, EXT, *ROW), (5, EXT, *ROW)]
 RESULT = (2, HEIGHT, *ROW)
 CUTS, MID, BASE, BEYOND = (STEPS, 2, 8, *ROW), (2, 2 * HALO, *ROW), (7, HEIGHT, *TILE), (7, 2 * HALO, *TILE)
 GHOST = (8, 2 * HALO, *ROW)
@@ -549,18 +580,18 @@
 def fill_ghost(flags, *args):
     return call(
         ghost_kernel,
-        [GHOST, STRIP, STRIP, RESULT, BEYOND],
+        [GHOST, STRIP, STRIP, RESULT, BEYOND, *OUTER],
         args,
-        OUTER,
+        [STATE] * 2,
         flags=flags,
     )
 
 
-def late(flags, rows, ghost, cuts, mid):
+def late(flags, *args):
     return call(
         late_kernel,
         [RESULT, BASE, BEYOND],
-        [rows, ghost, cuts, mid],
+        args,
         [CUTS, MID, *STATES],
         flags=flags,
     )
@@ -584,7 +615,7 @@
     place = lon % 8
     inner_first = ((place < INNER_FIRST) | (lat >= lat_count - 2)).astype(jnp.int32)
     outer_first = ((place < OUTER_FIRST) & (lat < lat_count - 2)).astype(jnp.int32)
-    sides_first = (place < INNER_FIRST).astype(jnp.int32)
+    sides_first = ((place < INNER_FIRST) & (lat != lat_count - 2)).astype(jnp.int32)
     flags = jnp.stack([lat % 2, top, lon % 2, inner_first, outer_first, sides_first])
     flat = [level_major(x) for x in args]
 
@@ -606,12 +637,12 @@
     odd_in = lax.ppermute(odd_msg, both, lat_odd)
     even_in = lax.ppermute(even_msg, both, lat_even)
     rows, east, west, cuts, mid, base1 = transpose(flags, flat, packed)
-    ghost, odd_strip, even_strip, result1, beyond1 = fill_ghost(
+    ghost, odd_strip, even_strip, result1, beyond1, *prepared = fill_ghost(
         flags, rows, odd_in, even_in, east, west, cuts, mid
     )
     odd_strip = lax.ppermute(odd_strip, "lon", lon_odd)
     even_strip = lax.ppermute(even_strip, "lon", lon_even)
-    result2, base2, beyond2 = late(flags, rows, ghost, cuts, mid)
+    result2, base2, beyond2 = late(flags, rows, ghost, cuts, mid, *prepared)
     temp, salt = edge(flags, base1, base2, beyond1, beyond2, odd_strip, even_strip, result1, result2)
     return from_level_major(temp), from_level_major(salt)
 

time: 45.8 us -> 45.2 us (0.987)
  starting transfers between devices: 20.3 us -> 19.4 us
    ppermute x1, starting transfers between devices: 4.2 us -> 3.31 us  [on_device(): odd_strip = lax.ppermute(odd_strip, 'lon', lon_odd)]
  transfers between devices with their start and end apart: 4 -> 4, of which waited for: 0 -> 1; matrix products, arithmetic and copies ran while one was open for 0% -> 0% of each run, Pallas kernels for 33% -> 31%
where the time goes in v8:
time: 45.2 us; the launch traced here: 44.9 us
  Pallas kernels  24.4 us (54%)
  starting transfers between devices  19.4 us (43%)
  between operations  0.75 us (2%)
    pallas_call x5, Pallas kernels, call(): pl.pallas_call(kernel, out_shape=[jax.ShapeDtypeStruct(s, F32) for s in o...  24.4 us
    ppermute x1, starting transfers between devices, on_device(): odd_in = lax.ppermute(odd_msg, both, lat_odd)  12.2 us
    ppermute x1, starting transfers between devices, on_device(): odd_strip = lax.ppermute(odd_strip, 'lon', lon_odd)  3.31 us
    ppermute x1, starting transfers between devices, on_device(): even_strip = lax.ppermute(even_strip, 'lon', lon_even)  1.96 us
    ppermute x1, starting transfers between devices, on_device(): even_in = lax.ppermute(even_msg, both, lat_even)  1.92 us
  transfers between devices with their start and end apart: 4, of which 1 were waited for; matrix products, arithmetic and copies ran while one was open for 0% of the time, Pallas kernels for 31%

profile of v8, /device:TPU:59, one launch (start us, length us, event | category | flops | bytes accessed | tf_op | source)
XLA Modules:
  0.0 44.9 jit_solution(6916752150711260650)
XLA Ops:
  0.7 0.1 stack.43.flags
  0.8 2.2 %shard_map.104 = (f32[55,8,256]{2,1,0:T(8,128)S(1)}, f32[55,8,256]{2,1,0:T(8,128)S(1)}, f32[8,128]{1,0:T(8,128)S(1)}) custom-call(s32[6]{0:T(128)S(1)} %stack.43.flags, f32[8,64,128]{2,1,0:T(8,128)} %bitcast.79, f32[8,64,128]{2,1,0:T(8,128)} %bitcast.81, f32[8,64,128]{2,1,0:T(8,128)} %bitcast.83, f32[8,64,128]{2,1,0:T(8,128)} %bitcast.85, ...), custom_call_target="tpu_custom_call" | custom-call | flops 50000000 | bytes 8000000 | tf_op jit(solution)/shard_map/pallas_call | solution.py:528
  3.0 12.2 %collective-permute-start = (f32[55,8,256]{2,1,0:T(8,128)S(1)}, f32[55,8,256]{2,1,0:T(8,128)S(1)}, u32[]{:S(2)}, u32[]{:S(2)}) collective-permute-start(f32[55,8,256]{2,1,0:T(8,128)S(1)} %get-tuple-element.27), channel_id=1, source_target_pairs={{1,2},{2,1},{3,4},{4,3},{5,6},{6,5},{7,8},{8,7},{9,10},{10,9},{11,... | collective-permute-start | bytes 1351688 | tf_op jit(solution)/shard_map/ppermute | solution.py:637
  15.2 1.9 %collective-permute-start.1 = (f32[55,8,256]{2,1,0:T(8,128)S(1)}, f32[55,8,256]{2,1,0:T(8,128)S(1)}, u32[]{:S(2)}, u32[]{:S(2)}) collective-permute-start(f32[55,8,256]{2,1,0:T(8,128)S(1)} %get-tuple-element.28), channel_id=1, source_target_pairs={{0,1},{1,0},{2,3},{3,2},{4,5},{5,4},{6,7},{7,6},{8,9},{9,8},{10,11... | collective-permute-start | bytes 1351688 | tf_op jit(solution)/shard_map/ppermute | solution.py:638
  17.1 10.6 %shard_map.105 = (f32[8,32,8,256]{3,2,1,0:T(8,128)S(1)}, f32[24,8,128]{2,1,0:T(8,128)S(1)}, f32[24,8,128]{2,1,0:T(8,128)S(1)}, f32[4,2,8,8,256]{4,3,2,1,0:T(8,12...) custom-call(s32[6]{0:T(128)S(1)} %stack.43.flags, f32[512,128]{1,0:T(8,128)} %bitcast.80, ...), custom_call_target="tpu_custom_call" | custom-call | flops 50000000 | bytes 8000000 | tf_op jit(solution)/shard_map/pallas_call | solution.py:528
  27.8 0.0 collective-permute-done.odd_msg
  27.8 0.0 collective-permute-done.1.even_msg
  27.8 2.8 %shard_map.106 = (f32[8,16,8,256]{3,2,1,0:T(8,128)S(1)}, f32[24,8,128]{2,1,0:T(8,128)S(1)}, f32[24,8,128]{2,1,0:T(8,128)S(1)}, f32[2,32,8,256]{3,2,1,0:T(8,128)S...) custom-call(s32[6]{0:T(128)S(1)} %stack.43.flags, ...), custom_call_target="tpu_custom_call" | custom-call | flops 50000000 | bytes 8000000 | tf_op jit(solution)/shard_map/pallas_call | solution.py:528
  30.6 3.3 %collective-permute-start.2 = (f32[24,8,128]{2,1,0:T(8,128)S(1)}, f32[24,8,128]{2,1,0:T(8,128)S(1)}, u32[]{:S(2)}, u32[]{:S(2)}) collective-permute-start(f32[24,8,128]{2,1,0:T(8,128)S(1)} %get-tuple-element.40), channel_id=1, source_target_pairs={{0,480},{32,64},{64,32},{96,128},{128,96},{160,192},{192,160},{224... | collective-permute-start | bytes 294920 | tf_op jit(solution)/shard_map/ppermute | solution.py:643
  33.9 2.0 %collective-permute-start.3 = (f32[24,8,128]{2,1,0:T(8,128)S(1)}, f32[24,8,128]{2,1,0:T(8,128)S(1)}, u32[]{:S(2)}, u32[]{:S(2)}) collective-permute-start(f32[24,8,128]{2,1,0:T(8,128)S(1)} %get-tuple-element.41), channel_id=1, source_target_pairs={{0,32},{32,0},{64,96},{96,64},{128,160},{160,128},{192,224},{224,1... | collective-permute-start | bytes 294920 | tf_op jit(solution)/shard_map/ppermute | solution.py:644
  35.9 3.5 %shard_map.107 = (f32[2,32,8,256]{3,2,1,0:T(8,128)S(1)}, f32[7,32,8,128]{3,2,1,0:T(8,128)S(1)}, f32[7,16,8,128]{3,2,1,0:T(8,128)S(1)}) custom-call(s32[6]{0:T(128)S(1)} %stack.43.flags, f32[8,32,8,256]{3,2,1,0:T(8,128)S(1)} %get-tuple-element.26.rows, f32[8,16,8,256]{3,2,1,0:T(8,128)S(1)} %get-tuple-element.33.ghost, ...), custom_call_target="tpu_custom_call" | custom-call | flops 50000000 | bytes 8000000 | tf_op jit(solution)/shard_map/pallas_call | solution.py:528
  39.4 0.3 collective-permute-done.2.odd_strip
  39.7 0.0 collective-permute-done.3.even_strip
  39.7 5.2 %shard_map.108 = (f32[8,64,128]{2,1,0:T(8,128)}, f32[8,64,128]{2,1,0:T(8,128)}) custom-call(s32[6]{0:T(128)S(1)} %stack.43.flags, f32[7,32,8,128]{3,2,1,0:T(8,128)S(1)} %get-tuple-element.25.base1, f32[7,32,8,128]{3,2,1,0:T(8,128)S(1)} %get-tuple-element.37.base2, f32[7,16,8,128]{3,2,1,0:T(8,128)S(1)} %get-tuple-element.38.beyond1, ...), custom_call_target="tpu_custom_call" | custom-call | flops 50000000 | bytes 8000000 | tf_op jit(solution)/shard_map/pallas_call | solution.py:528
Async XLA Ops:
  3.0 24.8 %collective-permute-start = (f32[55,8,256]{2,1,0:T(8,128)S(1)}, f32[55,8,256]{2,1,0:T(8,128)S(1)}, u32[]{:S(2)}, u32[]{:S(2)}) collective-permute-start(f32[55,8,256]{2,1,0:T(8,128)S(1)} %get-tuple-element.27), channel_id=1, source_target_pairs={{1,2},{2,1},{3,4},{4,3},{5,6},{6,5},{7,8},{8,7},{9,10},{10,9},{11,... | collective-permute-start | bytes 1351688 | tf_op jit(solution)/shard_map/ppermute | solution.py:637
  15.2 12.6 %collective-permute-start.1 = (f32[55,8,256]{2,1,0:T(8,128)S(1)}, f32[55,8,256]{2,1,0:T(8,128)S(1)}, u32[]{:S(2)}, u32[]{:S(2)}) collective-permute-start(f32[55,8,256]{2,1,0:T(8,128)S(1)} %get-tuple-element.28), channel_id=1, source_target_pairs={{0,1},{1,0},{2,3},{3,2},{4,5},{5,4},{6,7},{7,6},{8,9},{9,8},{10,11... | collective-permute-start | bytes 1351688 | tf_op jit(solution)/shard_map/ppermute | solution.py:638
  30.6 9.1 %collective-permute-start.2 = (f32[24,8,128]{2,1,0:T(8,128)S(1)}, f32[24,8,128]{2,1,0:T(8,128)S(1)}, u32[]{:S(2)}, u32[]{:S(2)}) collective-permute-start(f32[24,8,128]{2,1,0:T(8,128)S(1)} %get-tuple-element.40), channel_id=1, source_target_pairs={{0,480},{32,64},{64,32},{96,128},{128,96},{160,192},{192,160},{224... | collective-permute-start | bytes 294920 | tf_op jit(solution)/shard_map/ppermute | solution.py:643
  33.9 5.8 %collective-permute-start.3 = (f32[24,8,128]{2,1,0:T(8,128)S(1)}, f32[24,8,128]{2,1,0:T(8,128)S(1)}, u32[]{:S(2)}, u32[]{:S(2)}) collective-permute-start(f32[24,8,128]{2,1,0:T(8,128)S(1)} %get-tuple-element.41), channel_id=1, source_target_pairs={{0,32},{32,0},{64,96},{96,64},{128,160},{160,128},{192,224},{224,1... | collective-permute-start | bytes 294920 | tf_op jit(solution)/shard_map/ppermute | solution.py:644

commit v9 on v8

--- a/solution.py
+++ b/solution.py
@@ -10,7 +10,8 @@
 STEPS = 4
 HALO = 2 * STEPS
 PAD = 4
-INNER_FIRST = 4
+INNER_FIRST = 7
+SIDES_FIRST = 4
 OUTER_FIRST = 3
 LEVELS = 8
 HEIGHT = 32
@@ -488,7 +489,7 @@
         assemble(beyond, k, k, 0)
         assemble(beyond, HALO + k, 2 * HALO + k, 1, top)
 
-    loop(HALO, ghosts, 4)
+    loop(HALO, ghosts, 8)
 
     def own(k):
         assemble(base, k, HALO + k, 0)
@@ -615,7 +616,7 @@
     place = lon % 8
     inner_first = ((place < INNER_FIRST) | (lat >= lat_count - 2)).astype(jnp.int32)
     outer_first = ((place < OUTER_FIRST) & (lat < lat_count - 2)).astype(jnp.int32)
-    sides_first = ((place < INNER_FIRST) & (lat != lat_count - 2)).astype(jnp.int32)
+    sides_first = ((place < SIDES_FIRST) & (lat != lat_count - 2)).astype(jnp.int32)
     flags = jnp.stack([lat % 2, top, lon % 2, inner_first, outer_first, sides_first])
     flat = [level_major(x) for x in args]
 

time: 45.2 us -> 45.1 us (level)
  transfers between devices with their start and end apart: 4 -> 4, of which waited for: 1 -> 1; matrix products, arithmetic and copies ran while one was open for 0% -> 0% of each run, Pallas kernels for 31% -> 32%
where the time goes in v9:
time: 45.1 us; the launch traced here: 44.8 us
  Pallas kernels  24.2 us (54%)
  starting transfers between devices  19.4 us (43%)
  between operations  0.75 us (2%)
    pallas_call x5, Pallas kernels, call(): pl.pallas_call(kernel, out_shape=[jax.ShapeDtypeStruct(s, F32) for s in o...  24.2 us
    ppermute x1, starting transfers between devices, on_device(): odd_in = lax.ppermute(odd_msg, both, lat_odd)  12.2 us
    ppermute x1, starting transfers between devices, on_device(): odd_strip = lax.ppermute(odd_strip, 'lon', lon_odd)  3.31 us
    ppermute x1, starting transfers between devices, on_device(): even_strip = lax.ppermute(even_strip, 'lon', lon_even)  1.96 us
    ppermute x1, starting transfers between devices, on_device(): even_in = lax.ppermute(even_msg, both, lat_even)  1.92 us
  transfers between devices with their start and end apart: 4, of which 1 were waited for; matrix products, arithmetic and copies ran while one was open for 0% of the time, Pallas kernels for 32%

profile of v9, /device:TPU:59, one launch (start us, length us, event | category | flops | bytes accessed | tf_op | source)
XLA Modules:
  0.0 44.8 jit_solution(14456886779709024935)
XLA Ops:
  0.7 0.1 stack.43.flags
  0.8 2.2 %shard_map.104 = (f32[55,8,256]{2,1,0:T(8,128)S(1)}, f32[55,8,256]{2,1,0:T(8,128)S(1)}, f32[8,128]{1,0:T(8,128)S(1)}) custom-call(s32[6]{0:T(128)S(1)} %stack.43.flags, f32[8,64,128]{2,1,0:T(8,128)} %bitcast.79, f32[8,64,128]{2,1,0:T(8,128)} %bitcast.81, f32[8,64,128]{2,1,0:T(8,128)} %bitcast.83, f32[8,64,128]{2,1,0:T(8,128)} %bitcast.85, ...), custom_call_target="tpu_custom_call" | custom-call | flops 50000000 | bytes 8000000 | tf_op jit(solution)/shard_map/pallas_call | solution.py:529
  3.0 12.2 %collective-permute-start = (f32[55,8,256]{2,1,0:T(8,128)S(1)}, f32[55,8,256]{2,1,0:T(8,128)S(1)}, u32[]{:S(2)}, u32[]{:S(2)}) collective-permute-start(f32[55,8,256]{2,1,0:T(8,128)S(1)} %get-tuple-element.27), channel_id=1, source_target_pairs={{1,2},{2,1},{3,4},{4,3},{5,6},{6,5},{7,8},{8,7},{9,10},{10,9},{11,... | collective-permute-start | bytes 1351688 | tf_op jit(solution)/shard_map/ppermute | solution.py:638
  15.2 1.9 %collective-permute-start.1 = (f32[55,8,256]{2,1,0:T(8,128)S(1)}, f32[55,8,256]{2,1,0:T(8,128)S(1)}, u32[]{:S(2)}, u32[]{:S(2)}) collective-permute-start(f32[55,8,256]{2,1,0:T(8,128)S(1)} %get-tuple-element.28), channel_id=1, source_target_pairs={{0,1},{1,0},{2,3},{3,2},{4,5},{5,4},{6,7},{7,6},{8,9},{9,8},{10,11... | collective-permute-start | bytes 1351688 | tf_op jit(solution)/shard_map/ppermute | solution.py:639
  17.1 10.6 %shard_map.105 = (f32[8,32,8,256]{3,2,1,0:T(8,128)S(1)}, f32[24,8,128]{2,1,0:T(8,128)S(1)}, f32[24,8,128]{2,1,0:T(8,128)S(1)}, f32[4,2,8,8,256]{4,3,2,1,0:T(8,12...) custom-call(s32[6]{0:T(128)S(1)} %stack.43.flags, f32[512,128]{1,0:T(8,128)} %bitcast.80, ...), custom_call_target="tpu_custom_call" | custom-call | flops 50000000 | bytes 8000000 | tf_op jit(solution)/shard_map/pallas_call | solution.py:529
  27.8 0.0 collective-permute-done.odd_msg
  27.8 0.0 collective-permute-done.1.even_msg
  27.8 2.8 %shard_map.106 = (f32[8,16,8,256]{3,2,1,0:T(8,128)S(1)}, f32[24,8,128]{2,1,0:T(8,128)S(1)}, f32[24,8,128]{2,1,0:T(8,128)S(1)}, f32[2,32,8,256]{3,2,1,0:T(8,128)S...) custom-call(s32[6]{0:T(128)S(1)} %stack.43.flags, ...), custom_call_target="tpu_custom_call" | custom-call | flops 50000000 | bytes 8000000 | tf_op jit(solution)/shard_map/pallas_call | solution.py:529
  30.6 3.3 %collective-permute-start.2 = (f32[24,8,128]{2,1,0:T(8,128)S(1)}, f32[24,8,128]{2,1,0:T(8,128)S(1)}, u32[]{:S(2)}, u32[]{:S(2)}) collective-permute-start(f32[24,8,128]{2,1,0:T(8,128)S(1)} %get-tuple-element.40), channel_id=1, source_target_pairs={{0,480},{32,64},{64,32},{96,128},{128,96},{160,192},{192,160},{224... | collective-permute-start | bytes 294920 | tf_op jit(solution)/shard_map/ppermute | solution.py:644
  33.9 2.0 %collective-permute-start.3 = (f32[24,8,128]{2,1,0:T(8,128)S(1)}, f32[24,8,128]{2,1,0:T(8,128)S(1)}, u32[]{:S(2)}, u32[]{:S(2)}) collective-permute-start(f32[24,8,128]{2,1,0:T(8,128)S(1)} %get-tuple-element.41), channel_id=1, source_target_pairs={{0,32},{32,0},{64,96},{96,64},{128,160},{160,128},{192,224},{224,1... | collective-permute-start | bytes 294920 | tf_op jit(solution)/shard_map/ppermute | solution.py:645
  35.9 3.5 %shard_map.107 = (f32[2,32,8,256]{3,2,1,0:T(8,128)S(1)}, f32[7,32,8,128]{3,2,1,0:T(8,128)S(1)}, f32[7,16,8,128]{3,2,1,0:T(8,128)S(1)}) custom-call(s32[6]{0:T(128)S(1)} %stack.43.flags, f32[8,32,8,256]{3,2,1,0:T(8,128)S(1)} %get-tuple-element.26.rows, f32[8,16,8,256]{3,2,1,0:T(8,128)S(1)} %get-tuple-element.33.ghost, ...), custom_call_target="tpu_custom_call" | custom-call | flops 50000000 | bytes 8000000 | tf_op jit(solution)/shard_map/pallas_call | solution.py:529
  39.4 0.3 collective-permute-done.2.odd_strip
  39.7 0.0 collective-permute-done.3.even_strip
  39.7 5.1 %shard_map.108 = (f32[8,64,128]{2,1,0:T(8,128)}, f32[8,64,128]{2,1,0:T(8,128)}) custom-call(s32[6]{0:T(128)S(1)} %stack.43.flags, f32[7,32,8,128]{3,2,1,0:T(8,128)S(1)} %get-tuple-element.25.base1, f32[7,32,8,128]{3,2,1,0:T(8,128)S(1)} %get-tuple-element.37.base2, f32[7,16,8,128]{3,2,1,0:T(8,128)S(1)} %get-tuple-element.38.beyond1, ...), custom_call_target="tpu_custom_call" | custom-call | flops 50000000 | bytes 8000000 | tf_op jit(solution)/shard_map/pallas_call | solution.py:529
Async XLA Ops:
  3.0 24.8 %collective-permute-start = (f32[55,8,256]{2,1,0:T(8,128)S(1)}, f32[55,8,256]{2,1,0:T(8,128)S(1)}, u32[]{:S(2)}, u32[]{:S(2)}) collective-permute-start(f32[55,8,256]{2,1,0:T(8,128)S(1)} %get-tuple-element.27), channel_id=1, source_target_pairs={{1,2},{2,1},{3,4},{4,3},{5,6},{6,5},{7,8},{8,7},{9,10},{10,9},{11,... | collective-permute-start | bytes 1351688 | tf_op jit(solution)/shard_map/ppermute | solution.py:638
  15.2 12.6 %collective-permute-start.1 = (f32[55,8,256]{2,1,0:T(8,128)S(1)}, f32[55,8,256]{2,1,0:T(8,128)S(1)}, u32[]{:S(2)}, u32[]{:S(2)}) collective-permute-start(f32[55,8,256]{2,1,0:T(8,128)S(1)} %get-tuple-element.28), channel_id=1, source_target_pairs={{0,1},{1,0},{2,3},{3,2},{4,5},{5,4},{6,7},{7,6},{8,9},{9,8},{10,11... | collective-permute-start | bytes 1351688 | tf_op jit(solution)/shard_map/ppermute | solution.py:639
  30.6 9.1 %collective-permute-start.2 = (f32[24,8,128]{2,1,0:T(8,128)S(1)}, f32[24,8,128]{2,1,0:T(8,128)S(1)}, u32[]{:S(2)}, u32[]{:S(2)}) collective-permute-start(f32[24,8,128]{2,1,0:T(8,128)S(1)} %get-tuple-element.40), channel_id=1, source_target_pairs={{0,480},{32,64},{64,32},{96,128},{128,96},{160,192},{192,160},{224... | collective-permute-start | bytes 294920 | tf_op jit(solution)/shard_map/ppermute | solution.py:644
  33.9 5.8 %collective-permute-start.3 = (f32[24,8,128]{2,1,0:T(8,128)S(1)}, f32[24,8,128]{2,1,0:T(8,128)S(1)}, u32[]{:S(2)}, u32[]{:S(2)}) collective-permute-start(f32[24,8,128]{2,1,0:T(8,128)S(1)} %get-tuple-element.41), channel_id=1, source_target_pairs={{0,32},{32,0},{64,96},{96,64},{128,160},{160,128},{192,224},{224,1... | collective-permute-start | bytes 294920 | tf_op jit(solution)/shard_map/ppermute | solution.py:645
